TPU v7x, 128 devices: a whole 4x4x4 slice. The times are simulated.
128 devices in a mesh: grp: 8 (over z, core), sub: 16 (over x, y).
Axes of the slice: x: 4, y: 4, z: 4, core: 2. Of those that a mesh axis runs over, the one named last changes fastest.
Arguments:
- amplitudes: bfloat16 [128, 896, 896], P(('grp', 'sub')), may hold values from -0.5 to 0.5
- exchange_ints: bfloat16 [128, 896, 896], P(('grp', 'sub')), may hold values from -6 to 6
- chol: bfloat16 [8, 4096, 4096], P('grp', 'sub'), may hold values from -1.5 to 1.5
- domain: int32 [128, 7], P(('grp', 'sub')), may hold values from 0 to 31, as said below
- virt_energy: float32 [4096], replicated, may hold values from 0.5 to 4
- pair_energy: float32 [128], P(('grp', 'sub')), may hold values from -3 to -1
Outputs:
- residual: bfloat16 [128, 896, 896], P(('grp', 'sub'))
Inputs may be any that keep to these rules, and one draw needn't show every extreme that they name: `domain`: each row holds 7 increasing tile numbers, no two with the same quotient by 2; rows p and p + 64 are equal.
All inputs are finite; a program needn't handle non-finite values.
Results may differ from a plain program's by a relative error of at most 0.0045.
Values may be sent and summed in bfloat16 or wider, within the bound.
No kernel may reach another device: no remote copies, remote signals or barrier semaphores. Data moves between devices by JAX's collectives and lax.ppermute only.
A program may use at most 192 MiB of HBM per device.

v0:
```python
import jax
import jax.numpy as jnp
from jax import lax
from jax.sharding import PartitionSpec as P

TILE = 128
NVT = 32
DT = 7


def partner(value, axis, distance):
    return lax.ppermute(value, axis, [(i, i ^ 1 << distance) for i in range(lax.axis_size(axis))])


def local(amplitudes, exchange_ints, chol, domain, virt_energy, pair_energy):
    pair_dev = amplitudes.shape[0]
    groups = lax.axis_size("grp")
    owners = lax.axis_size("sub")
    devices = groups * owners
    vec_local = chol.shape[0]
    per_owner = chol.shape[1] // TILE
    my_sub = lax.axis_index("sub")
    all_domains = lax.all_gather(domain, ("grp", "sub"), axis=0, tiled=True)
    row_owner_all = all_domains // per_owner
    within = all_domains % per_owner
    mine = row_owner_all == my_sub
    tile_view = chol.reshape(vec_local, per_owner, TILE, NVT, TILE).transpose(1, 3, 0, 2, 4)
    outgoing = jnp.zeros((all_domains.shape[0], DT, vec_local, TILE, TILE), jnp.bfloat16)
    for slot_index in range(per_owner):
        holds_row = jnp.any(mine & (within == slot_index), axis=1)
        picked = jnp.take(tile_view[slot_index], all_domains, axis=0)
        outgoing = jnp.where(holds_row[:, None, None, None, None], picked, outgoing)
    cycle_terms = jnp.einsum(
        "kad,kdb->kab", amplitudes, exchange_ints, preferred_element_type=jnp.float32
    ).astype(jnp.bfloat16)
    partner_bit = groups.bit_length() - 2
    arrived = lax.all_to_all(
        outgoing.reshape(devices, pair_dev, DT, vec_local, TILE, TILE),
        ("grp", "sub"),
        split_axis=0,
        concat_axis=0,
        tiled=True,
    )
    arrived = arrived.reshape(groups, owners, pair_dev, DT, vec_local, TILE, TILE)
    pair_slot = 0
    slot_owner = domain[pair_slot] // per_owner
    picked_list = [jnp.take(arrived[:, :, pair_slot], slot_owner, axis=1)]
    gathered = jnp.stack(picked_list, axis=1)
    partner_cycle = partner(cycle_terms, "grp", partner_bit)
    dom_width = DT * TILE
    energy_tiles = virt_energy.reshape(NVT, TILE)
    pair_slot = 0
    domain_block = (
        gathered[:, pair_slot]
        .transpose(0, 3, 1, 4, 2, 5)
        .reshape(groups * vec_local, dom_width, dom_width)
    )
    pair_amps = amplitudes[pair_slot]
    half_ladder = jnp.einsum(
        "ad,qbd->qab", pair_amps, domain_block, preferred_element_type=jnp.float32
    ).astype(jnp.bfloat16)
    ladder = jnp.einsum(
        "qac,qcb->ab", domain_block, half_ladder, preferred_element_type=jnp.float32
    )
    energies = jnp.take(energy_tiles, domain[pair_slot], axis=0).reshape(dom_width)
    denominator = energies[:, None] + energies[None, :] - pair_energy[pair_slot]
    result = (
        exchange_ints[pair_slot].astype(jnp.float32)
        + denominator * pair_amps.astype(jnp.float32)
        + ladder
    )
    result = (
        result
        + cycle_terms[pair_slot].astype(jnp.float32)
        + partner_cycle[pair_slot].astype(jnp.float32).T
    )
    results = [result.astype(jnp.bfloat16)]
    return jnp.stack(results, axis=0)


def solution(mesh):
    placed = (
        P(("grp", "sub"), None, None),
        P(("grp", "sub"), None, None),
        P("grp", "sub", None),
        P(("grp", "sub"), None),
        P(),
        P(("grp", "sub")),
    )
    return jax.shard_map(
        local, mesh=mesh, in_specs=placed, out_specs=P(("grp", "sub"), None, None), check_vma=False
    )
```

profile of v0, /device:TPU:82, one launch (start us, length us, event | category | flops | bytes accessed | tf_op | source)
XLA Modules:
  0.0 743.9 jit_solution(5638652594811849324)
XLA Ops:
  0.0 0.0 copy-start
  0.0 46.0 %all-gather = s32[128,1,7]{2,1,0:T(1,128)S(1)} all-gather(s32[1,1,7]{2,1,0:T(1,128)} %bitcast.165), channel_id=1, replica_groups=mesh['grp'=8,'sub'=16] {'grp','sub'}, dimensions={0}, use_global_device_ids=true | all-gather | bytes 3612 | tf_op jit(solution)/shard_map/all_gather | solution.py:23
  46.0 0.1 copy.23
  46.1 0.1 copy.26
  46.2 0.2 reshape.236
  46.4 2.1 copy.36
  48.5 0.8 copy.38
  49.3 0.1 slice_bitcast_fusion.1
  49.5 21.9 %gather_fusion.2 = bf16[896,128,128]{2,1,0:T(8,128)(2,1)} fusion(bf16[32,128,128]{2,1,0:T(8,128)(2,1)S(1)} %get-tuple-element.8, s32[1024]{0:T(1024)S(1)} %pad_clamp_fusion.1), kind=kCustom, calls=%fused_computation.clone | custom fusion | bytes 58723840 | tf_op jit(solution)/shard_map/jit(_take)/gather | solution.py:31
  71.4 21.8 %gather_fusion.3 = bf16[896,128,128]{2,1,0:T(8,128)(2,1)} fusion(bf16[32,128,128]{2,1,0:T(8,128)(2,1)S(1)} %get-tuple-element.9, s32[1024]{0:T(1024)S(1)} %pad_clamp_fusion.1), kind=kCustom, calls=%fused_computation.1.clone | custom fusion | bytes 58723840 | tf_op jit(solution)/shard_map/jit(_take)/gather | solution.py:31
  93.2 0.1 copy.24
  93.4 29.1 %fusion.1 = bf16[128,1,7,1,128,128]{5,4,2,3,1,0:T(8,128)(2,1)} fusion(bf16[128,7,1,128,128]{4,3,1,0,2:T(8,128)(2,1)} %bitcast.161, bf16[128,7,1,128,128]{4,3,1,0,2:T(8,128)(2,1)} %bitcast.160, pred[128]{0:T(512)(128)(4,1)S(1)} %get-tuple-element.7, pred[128]{0:T(512)(128)(4,1)S(1)} %get-tuple-element.6, pred[128,7]{1,0:T(8,128)(4,1)S(1)} %copy.24), kind=kLoop, calls=%fused_computation.6 | loop fusion | flops 58720256 | bytes 88081536 | tf_op jit(solution)/shard_map/reshape | solution.py:38
  122.4 0.0 copy-start.4
  122.5 11.6 %all-to-all-start = ((bf16[128,1,7,1,128,128]{5,4,2,3,1,0:T(8,128)(2,1)}), bf16[128,1,7,1,128,128]{5,4,2,3,1,0:T(8,128)(2,1)}, u32[]{:S(2)}, u32[]{:S(2)}) async-start(bf16[128,1,7,1,128,128]{5,4,2,3,1,0:T(8,128)(2,1)} %fusion.1), calls=%async_computation | async-start | bytes 58720256 | tf_op jit(solution)/shard_map/all_to_all | solution.py:37
  134.1 0.0 copy-done.3
  134.1 0.0 copy-done.4
  134.1 0.0 copy-start.2
  134.1 3.2 convolution_convert_fusion
  137.3 0.0 collective-permute-start
  137.4 2.8 copy.33
  140.9 0.0 copy-done.2
  140.9 0.0 copy-done
  140.9 0.6 gather_fusion
  141.5 0.1 select_bitcast_fusion
  141.6 499.8 %all-to-all-done = bf16[128,1,7,1,128,128]{5,4,2,3,1,0:T(8,128)(2,1)} async-done(((bf16[128,1,7,1,128,128]{5,4,2,3,1,0:T(8,128)(2,1)}), bf16[128,1,7,1,128,128]{5,4,2,3,1,0:T(8,128)(2,1)}, u32[]{:S(2)}, u32[]{:S(2)}) %all-to-all-start) | async-done | bytes 29360160 | tf_op jit(solution)/shard_map/all_to_all | solution.py:37
  641.4 16.0 %gather_fusion.1 = bf16[7,8,7,128,128]{4,3,2,1,0:T(8,128)(2,1)} fusion(bf16[8,16,7,128,128]{4,3,2,1,0:T(8,128)(2,1)} %bitcast.19, s32[1024]{0:T(1024)S(1)} %pad_clamp_fusion), kind=kCustom, calls=%fused_computation.3 | custom fusion | bytes 25690140 | tf_op jit(solution)/shard_map/jit(_take)/gather | solution.py:47
  657.4 7.2 fusion.2
  664.6 11.0 %copy.30 = bf16[8,1,7,128,7,128]{5,4,3,2,0,1:T(8,128)(2,1)} copy(bf16[8,1,7,128,7,128]{5,3,4,0,2,1:T(8,128)(2,1)S(1)} %fusion.2) | data formatting | bytes 25690112 | tf_op jit(solution)/shard_map/transpose | solution.py:55
  675.6 25.3 %reshape.186 = bf16[8,896,896]{2,1,0:T(8,128)(2,1)} reshape(bf16[8,1,7,128,7,128]{5,4,3,2,0,1:T(8,128)(2,1)} %copy.30) | data formatting | bytes 25690112 | tf_op jit(solution)/shard_map/reshape | solution.py:56
  700.9 21.1 %fusion.37 = bf16[8,896,896]{1,2,0:T(8,128)(2,1)} fusion(bf16[8,896,896]{2,1,0:T(8,128)(2,1)} %reshape.186, bf16[1,896,896]{2,1,0:T(8,128)(2,1)} %param.8), kind=kOutput, calls=%fused_computation.10.clone.clone.clone.1 | convolution fusion | flops 11515592704 | bytes 27295744 | tf_op jit(solution)/shard_map/ad,qbd->qab/dot_general | solution.py:59
  722.0 0.0 collective-permute-done
  722.0 21.9 %fusion.11 = bf16[1,896,896]{2,1,0:T(8,128)(2,1)} fusion(f32[896,896]{1,0:T(8,128)S(1)} %copy.33, bf16[1,896,896]{1,2,0:T(8,128)(2,1)} %collective-permute-done, bf16[1,896,896]{2,1,0:T(8,128)(2,1)} %param.8, bf16[1,896,896]{2,1,0:T(8,128)(2,1)} %param.9, f32[]{:T(128)} %bitcast.158, f32[896]{0:T(1024)S(1)} %select_bitcast_fusion, ...), kind=kOutput, calls=%fused_computation.20 | convolution fusion | flops 11518001152 | bytes 35327492 | tf_op jit(solution)/shard_map/qac,qcb->ab/dot_general | solution.py:62
  (10 shorter events, 0.1 us)
Async XLA Ops:
  0.0 140.9 %copy-start = (f32[4096]{0:T(1024)S(1)}, f32[4096]{0:T(1024)}, u32[]{:S(2)}) copy-start(f32[4096]{0:T(1024)} %param.12) | copy-start | bytes 49156
  122.4 11.7 %copy-start.3 = (bf16[1,896,896]{2,1,0:T(8,128)(2,1)S(1)}, bf16[1,896,896]{2,1,0:T(8,128)(2,1)}, u32[]{:S(2)}) copy-start(bf16[1,896,896]{2,1,0:T(8,128)(2,1)} %param.8) | copy-start | bytes 4816900
  122.4 11.7 %copy-start.4 = (bf16[1,896,896]{2,1,0:T(8,128)(2,1)S(1)}, bf16[1,896,896]{2,1,0:T(8,128)(2,1)}, u32[]{:S(2)}) copy-start(bf16[1,896,896]{2,1,0:T(8,128)(2,1)} %param.9) | copy-start | bytes 4816900
  122.5 518.9 %all-to-all-start = ((bf16[128,1,7,1,128,128]{5,4,2,3,1,0:T(8,128)(2,1)}), bf16[128,1,7,1,128,128]{5,4,2,3,1,0:T(8,128)(2,1)}, u32[]{:S(2)}, u32[]{:S(2)}) async-start(bf16[128,1,7,1,128,128]{5,4,2,3,1,0:T(8,128)(2,1)} %fusion.1), calls=%async_computation | async-start | bytes 58720256 | tf_op jit(solution)/shard_map/all_to_all | solution.py:37
  134.1 6.7 copy-start.2
  137.3 584.6 %collective-permute-start = (bf16[1,896,896]{1,2,0:T(8,128)(2,1)}, bf16[1,896,896]{1,2,0:T(8,128)(2,1)}, u32[]{:S(2)}, u32[]{:S(2)}) collective-permute-start(bf16[1,896,896]{1,2,0:T(8,128)(2,1)} %bitcast.27), channel_id=1, source_target_pairs={{0,64},{16,80},{32,96},{48,112},{64,0},{80,16},{96,32},{112,48},{1... | collective-permute-start | bytes 4816904 | tf_op jit(solution)/shard_map/ppermute | solution.py:12
  722.0 21.9 %copy-start.1 = (f32[4096]{0:T(1024)S(1)}, f32[4096]{0:T(1024)}, u32[]{:S(2)}) copy-start(f32[4096]{0:T(1024)} %param.12) | copy-start | bytes 49156
where the time goes:
time: 745 us; the launch traced here: 744 us
  waiting for transfers between devices  500 us (67%)
  local copies, waits for them, and re-layouts  103 us (14%)
  matrix products  46.2 us (6%)
  blocking collectives  46 us (6%)
  other arithmetic  36.4 us (5%)
  starting transfers between devices  11.7 us (2%)
    all_to_all x1, waiting for transfers between devices, local(): lax.all_to_all(outgoing.reshape(devices, pair_dev, DT, vec_local, TILE, T...  500 us
    all_gather x1, blocking collectives, local(): all_domains = lax.all_gather(domain, ('grp', 'sub'), axis=0, tiled=True)  46 us
    gather x2, local copies, waits for them, and re-layouts, local(): picked = jnp.take(tile_view[slot_index], all_domains, axis=0)  43.7 us
    reshape x1, other arithmetic, local(): outgoing.reshape(devices, pair_dev, DT, vec_local, TILE, TILE)  29.1 us
    reshape x1, local copies, waits for them, and re-layouts, local(): domain_block = gathered[:, pair_slot].transpose(0, 3, 1, 4, 2, 5).reshape...  25.3 us
    dot_general x1, matrix products, local(): jnp.einsum('qac,qcb->ab', domain_block, half_ladder, preferred_element_ty...  21.9 us
    dot_general x1, matrix products, local(): jnp.einsum('ad,qbd->qab', pair_amps, domain_block, preferred_element_type...  21.1 us
    gather x1, local copies, waits for them, and re-layouts, local(): picked_list = [jnp.take(arrived[:, :, pair_slot], slot_owner, axis=1)]  16 us
  transfers between devices with their start and end apart: 2, of which 1 were waited for; matrix products, arithmetic and copies ran while one was open for 12% of the time, Pallas kernels for 0%

commit v1 on v0

v1 whole, which is shorter than its diff:
```python
import functools

import jax
import jax.numpy as jnp
from jax import lax
from jax.experimental import pallas as pl
from jax.experimental.pallas import tpu as pltpu
from jax.sharding import Mesh
from jax.sharding import PartitionSpec as P

TILE = 128
NVT = 32
DT = 7
DV = DT * TILE
NZ, NC, NX, NY = 4, 2, 4, 4
OWNERS = NX * NY
SLICE = TILE // OWNERS
CHIPS = NZ * OWNERS
CHUNKS = ((0, 7),)
PACK = 4


def partner_perm(to_other_core):
    pairs = []
    for z in range(NZ):
        core = 1 - z // 2
        target = 1 - core if to_other_core else core
        pairs.append((z * NC + core, (z ^ 2) * NC + target))
    return pairs


def core_swap(value):
    return lax.ppermute(value, "core", [(0, 1), (1, 0)])


def gather_small(value, axis, size):
    parts = [value]
    for step in range(1, size):
        parts.append(lax.ppermute(value, axis, [((i + step) % size, i) for i in range(size)]))
    stacked = jnp.stack(parts)
    return jnp.roll(stacked, lax.axis_index(axis), axis=0)


def pack_kernel(first, count, tiles_ref, rows_ref, out_ref):
    step = pl.program_id(0)
    for slot in range(PACK):
        dest = step * PACK + slot
        tiles = [tiles_ref[dest * DT + t] for t in range(DT)]
        columns = [pl.multiple_of(tile * TILE, TILE) for tile in tiles]
        for i in range(count):
            for j in range(DT):
                out_ref[slot, i, :, j * TILE : (j + 1) * TILE] = rows_ref[
                    tiles[first + i], :, pl.ds(columns[j], TILE)
                ]


def pack(tiles, rows, first, count):
    return pl.pallas_call(
        functools.partial(pack_kernel, first, count),
        out_shape=jax.ShapeDtypeStruct((CHIPS, count, SLICE, DV), jnp.bfloat16),
        grid_spec=pltpu.PrefetchScalarGridSpec(
            num_scalar_prefetch=1,
            grid=(CHIPS // PACK,),
            in_specs=[pl.BlockSpec((NVT, SLICE, NVT * TILE), lambda s, t: (0, 0, 0))],
            out_specs=pl.BlockSpec((PACK, count, SLICE, DV), lambda s, t: (s, 0, 0, 0)),
        ),
        compiler_params=pltpu.CompilerParams(vmem_limit_bytes=16 * 1024 * 1024),
        cost_estimate=pl.CostEstimate(
            flops=0, bytes_accessed=2 * CHIPS * count * SLICE * DV * 2, transcendentals=0
        ),
    )(tiles, rows)


def local(amplitudes, exchange_ints, chol, domain, virt_energy, pair_energy):
    z = lax.axis_index("z")
    core = lax.axis_index("core")
    home = core == z // 2
    amps, exch = amplitudes[0], exchange_ints[0]

    spread = chol.reshape(2, OWNERS, SLICE, NVT * TILE).transpose(1, 0, 2, 3)
    spread = lax.all_to_all(spread, ("x", "y"), 0, 0, tiled=True)
    rows = spread.reshape(NVT, SLICE, NVT * TILE)

    zones = lax.ppermute(domain[0], "z", [(i, i ^ 1) for i in range(NZ)])
    column = jnp.stack([jnp.where(z % 2 == 0, domain[0], zones), jnp.where(z % 2 == 0, zones, domain[0])])
    other = core_swap(column)
    column = jnp.concatenate([jnp.where(core == 0, column, other), jnp.where(core == 0, other, column)])
    everyone = gather_small(gather_small(column, "y", NY), "x", NX)
    everyone = everyone.transpose(2, 0, 1, 3).reshape(CHIPS * DT)

    moved = lax.ppermute(amps, ("z", "core"), partner_perm(True))
    mine = jnp.where(home, amps, moved)
    both = jnp.stack([mine, core_swap(mine)])

    cycle = jnp.dot(amps, exch, preferred_element_type=jnp.float32).astype(jnp.bfloat16)
    partner_cycle = lax.ppermute(cycle, ("z", "core"), partner_perm(False))

    blocks = []
    for first, count in CHUNKS:
        outgoing = pack(everyone, rows, first, count)
        arrived = lax.all_to_all(outgoing, ("z", "x", "y"), 0, 0, tiled=True)
        blocks.append(
            arrived.reshape(NZ, OWNERS, count, SLICE, DV)
            .transpose(0, 2, 1, 3, 4)
            .reshape(NZ, count * TILE, DV)
        )
    block = jnp.concatenate(blocks, axis=1) if len(blocks) > 1 else blocks[0]
    half_ladder = jnp.einsum(
        "pad,qbd->pqab", both, block, preferred_element_type=jnp.float32
    ).astype(jnp.bfloat16)
    ladder = jnp.einsum(
        "qac,pqcb->pab", block, half_ladder, preferred_element_type=jnp.float32
    )
    to_other = ladder[1] + jnp.where(home, cycle.T.astype(jnp.float32), 0.0)
    from_other = core_swap(to_other.astype(jnp.bfloat16))
    finished = ladder[0] + from_other.astype(jnp.float32)
    returned = lax.ppermute(finished.astype(jnp.bfloat16), ("z", "core"), partner_perm(True))
    added = jnp.where(
        home, finished + partner_cycle.T.astype(jnp.float32), returned.astype(jnp.float32)
    )
    energies = jnp.take(virt_energy.reshape(NVT, TILE), domain[0], axis=0).reshape(DV)
    denominator = energies[:, None] + energies[None, :] - pair_energy[0]
    result = (
        exch.astype(jnp.float32)
        + denominator * amps.astype(jnp.float32)
        + cycle.astype(jnp.float32)
        + added
    )
    return result.astype(jnp.bfloat16)[None]


def solution(mesh):
    finer = Mesh(mesh.devices.reshape(NZ, NC, NX, NY), ("z", "core", "x", "y"))
    group, everywhere = ("z", "core"), ("z", "core", "x", "y")
    placed = (
        P(everywhere, None, None),
        P(everywhere, None, None),
        P(group, ("x", "y"), None),
        P(everywhere, None),
        P(),
        P(everywhere),
    )
    return jax.shard_map(
        local, mesh=finer, in_specs=placed, out_specs=P(everywhere, None, None), check_vma=False
    )
```

time: 745 us -> 260 us (0.35)
  the two profiles are of different devices: /device:TPU:82 before, /device:TPU:1 now
where the time goes in v1:
time: 260 us; the launch traced here: 259 us
  waiting for transfers between devices  118 us (45%)
  starting transfers between devices  51.5 us (20%)
  matrix products  38.5 us (15%)
  local copies, waits for them, and re-layouts  32.8 us (13%)
  other arithmetic  13.1 us (5%)
  Pallas kernels  3.94 us (2%)
    ppermute x1, waiting for transfers between devices, local(): moved = lax.ppermute(amps, ('z', 'core'), partner_perm(True))  80.9 us
    dot_general x1, matrix products, local(): jnp.einsum('qac,pqcb->pab', block, half_ladder, preferred_element_type=jn...  35.3 us
    ppermute x6, starting transfers between devices, gather_small(): lax.ppermute(value, axis, [((i + step) % size, i) for i in range(size)])  14.1 us
    ppermute x6, waiting for transfers between devices, gather_small(): lax.ppermute(value, axis, [((i + step) % size, i) for i in range(size)])  13.7 us
    ppermute x1, waiting for transfers between devices, local(): partner_cycle = lax.ppermute(cycle, ('z', 'core'), partner_perm(False))  11.5 us
    ppermute x1, starting transfers between devices, local(): moved = lax.ppermute(amps, ('z', 'core'), partner_perm(True))  10.3 us
    all_to_all x1, starting transfers between devices, local(): arrived = lax.all_to_all(outgoing, ('z', 'x', 'y'), 0, 0, tiled=True)  8.92 us
    unnamed x28, local copies, waits for them, and re-layouts  7.95 us
  transfers between devices with their start and end apart: 15, of which 11 were waited for; matrix products, arithmetic and copies ran while one was open for 12% of the time, Pallas kernels for 0%

profile of v1, /device:TPU:1, one launch (start us, length us, event | category | flops | bytes accessed | tf_op | source)
XLA Modules:
  0.0 258.6 jit_solution(4932281019425716404)
XLA Ops:
  0.0 2.5 collective-permute-start
  2.5 3.2 %copy.30 = bf16[2,16,8,4096]{3,2,0,1:T(8,128)(2,1)} copy(bf16[2,16,8,4096]{3,2,1,0:T(8,128)(2,1)} %bitcast.119) | data formatting | bytes 4194304 | tf_op jit(solution)/shard_map/reshape | solution.py:80
  5.6 6.8 %all-to-all-start = ((bf16[16,2,8,4096]{3,2,1,0:T(8,128)(2,1)}), bf16[16,2,8,4096]{3,2,1,0:T(8,128)(2,1)S(1)}, u32[]{:S(2)}, u32[]{:S(2)}) async-start(bf16[16,2,8,4096]{3,2,1,0:T(8,128)(2,1)} %bitcast.117), calls=%async_computation | async-start | bytes 4194304 | tf_op jit(solution)/shard_map/all_to_all | solution.py:81
  12.5 1.3 collective-permute-start.1
  14.6 2.9 %collective-permute-start.2 = (s32[4,7]{1,0:T(4,128)S(1)}, s32[4,7]{1,0:T(4,128)S(1)}, u32[]{:S(2)}, u32[]{:S(2)}) collective-permute-start(s32[4,7]{1,0:T(4,128)S(1)} %pad_add_fusion), channel_id=1, source_target_pairs={{1,0},{2,1},{3,2},{0,3},{5,4},{6,5},{7,6},{4,7},{9,8},{10,9},{11,1... | collective-permute-start | bytes 344 | tf_op jit(solution)/shard_map/ppermute | solution.py:39
  19.8 6.9 %collective-permute-done.3 = s32[4,7]{1,0:T(4,128)S(1)} collective-permute-done((s32[4,7]{1,0:T(4,128)S(1)}, s32[4,7]{1,0:T(4,128)S(1)}, u32[]{:S(2)}, u32[]{:S(2)}) %collective-permute-start.3) | collective-permute-done | bytes 144 | tf_op jit(solution)/shard_map/ppermute | solution.py:39
  26.8 2.0 collective-permute-done.4
  28.8 9.4 %collective-permute-start.5 = (s32[4,4,7]{2,1,0:T(4,128)S(1)}, s32[4,4,7]{2,1,0:T(4,128)S(1)}, u32[]{:S(2)}, u32[]{:S(2)}) collective-permute-start(s32[4,4,7]{2,1,0:T(4,128)S(1)} %get-tuple-element.8), channel_id=1, source_target_pairs={{4,0},{8,4},{12,8},{0,12},{5,1},{9,5},{13,9},{1,13},{6,2},{10,6},{... | collective-permute-start | bytes 1352 | tf_op jit(solution)/shard_map/ppermute | solution.py:39
  39.0 3.2 %collective-permute-done.6 = s32[4,4,7]{2,1,0:T(4,128)S(1)} collective-permute-done((s32[4,4,7]{2,1,0:T(4,128)S(1)}, s32[4,4,7]{2,1,0:T(4,128)S(1)}, u32[]{:S(2)}, u32[]{:S(2)}) %collective-permute-start.6) | collective-permute-done | bytes 480 | tf_op jit(solution)/shard_map/ppermute | solution.py:39
  42.8 3.9 %shard_map.64 = bf16[64,7,8,896]{3,2,1,0:T(8,128)(2,1)S(1)} custom-call(s32[448]{0:T(512)S(1)} %reshape.77.tiles_ref, bf16[32,8,4096]{2,1,0:T(8,128)(2,1)S(1)} %bitcast.115), custom_call_target="tpu_custom_call" | custom-call | bytes 12845056 | tf_op jit(solution)/shard_map/pallas_call | solution.py:58
  46.8 2.7 %copy-done.1 = bf16[64,7,8,896]{3,2,1,0:T(8,128)(2,1)} copy-done((bf16[64,7,8,896]{3,2,1,0:T(8,128)(2,1)}, bf16[64,7,8,896]{3,2,1,0:T(8,128)(2,1)S(1)}, u32[]{:S(2)}) %copy-start.1) | copy-done | bytes 6422552
  49.5 8.9 %all-to-all-start.1 = ((bf16[64,7,8,896]{3,2,1,0:T(8,128)(2,1)}), bf16[64,7,8,896]{3,2,1,0:T(8,128)(2,1)}, u32[]{:S(2)}, u32[]{:S(2)}) async-start(bf16[64,7,8,896]{3,2,1,0:T(8,128)(2,1)} %copy-done.1), calls=%async_computation.1 | async-start | bytes 12845056 | tf_op jit(solution)/shard_map/all_to_all | solution.py:101
  58.4 1.6 copy.17
  60.0 10.3 %collective-permute-start.8 = (bf16[896,896]{0,1:T(8,128)(2,1)S(1)}, bf16[896,896]{0,1:T(8,128)(2,1)S(1)}, u32[]{:S(2)}, u32[]{:S(2)}) collective-permute-start(bf16[896,896]{0,1:T(8,128)(2,1)S(1)} %bitcast.116), channel_id=1, source_target_pairs={{16,64},{48,96},{64,16},{96,48},{17,65},{49,97},{65,17},{97,49},{1... | collective-permute-start | bytes 4816904 | tf_op jit(solution)/shard_map/ppermute | solution.py:91
  70.3 80.9 %collective-permute-done.8 = bf16[896,896]{0,1:T(8,128)(2,1)S(1)} collective-permute-done((bf16[896,896]{0,1:T(8,128)(2,1)S(1)}, bf16[896,896]{0,1:T(8,128)(2,1)S(1)}, u32[]{:S(2)}, u32[]{:S(2)}) %collective-permute-start.8) | collective-permute-done | bytes 1605664 | tf_op jit(solution)/shard_map/ppermute | solution.py:91
  151.3 1.4 broadcast_select_fusion
  152.6 3.1 %convolution_convert_fusion = bf16[896,896]{1,0:T(8,128)(2,1)} fusion(bf16[1,896,896]{2,1,0:T(8,128)(2,1)S(1)} %copy-done.5, bf16[1,896,896]{2,1,0:T(8,128)(2,1)S(1)} %copy-done.4), kind=kOutput, calls=%fused_computation.22 | convolution fusion | flops 1439449088 | bytes 4816896 | tf_op jit(solution)/shard_map/dot_general | solution.py:95
  155.8 2.9 %copy.18 = bf16[896,896]{0,1:T(8,128)(2,1)S(1)} copy(bf16[896,896]{1,0:T(8,128)(2,1)} %convolution_convert_fusion) | data formatting | bytes 3211264 | tf_op jit(solution)/shard_map/convert_element_type | solution.py:95
  158.7 6.5 %copy.21 = bf16[4,7,16,8,896]{4,3,2,1,0:T(8,128)(2,1)} copy(bf16[4,7,16,8,896]{4,3,1,2,0:T(8,128)(2,1)} %bitcast.23) | data formatting | bytes 12845056 | tf_op jit(solution)/shard_map/transpose | solution.py:104
  165.2 35.3 %fusion.13 = f32[2,896,896]{2,1,0:T(8,128)} fusion(bf16[4,896,896,1]{2,1,0,3:T(8,128)(2,1)} %bitcast.118, bf16[1,896,896]{1,2,0:T(8,128)(2,1)} %bitcast.27, bf16[1,896,896]{1,2,0:T(8,128)(2,1)} %bitcast.26), kind=kOutput, calls=%fused_computation.20 | convolution fusion | flops 23031185408 | bytes 16056320 | tf_op jit(solution)/shard_map/qac,pqcb->pab/dot_general | solution.py:111
  200.5 2.4 fusion.7
  203.8 3.1 %collective-permute-done.10 = bf16[896,896]{1,0:T(8,128)(2,1)S(1)} collective-permute-done((bf16[896,896]{1,0:T(8,128)(2,1)S(1)}, bf16[896,896]{1,0:T(8,128)(2,1)S(1)}, u32[]{:S(2)}, u32[]{:S(2)}) %collective-permute-start.10) | collective-permute-done | bytes 1605664 | tf_op jit(solution)/shard_map/ppermute | solution.py:33
  206.9 2.6 %fusion.24 = (bf16[896,896]{1,0:T(8,128)(2,1)}, f32[896,896]{1,0:T(8,128)}) fusion(bf16[896,896]{1,0:T(8,128)(2,1)S(1)} %collective-permute-done.10, f32[2,896,896]{2,1,0:T(8,128)S(1)} %copy-done.2), kind=kLoop, calls=%fused_computation.60 | loop fusion | flops 2408448 | bytes 9633792 | tf_op jit(solution)/shard_map/convert_element_type | solution.py:117
  209.5 3.8 %collective-permute-start.12 = (bf16[896,896]{1,0:T(8,128)(2,1)}, bf16[896,896]{1,0:T(8,128)(2,1)}, u32[]{:S(2)}, u32[]{:S(2)}) collective-permute-start(bf16[896,896]{1,0:T(8,128)(2,1)} %get-tuple-element.5), channel_id=1, source_target_pairs={{16,64},{48,96},{64,16},{96,48},{17,65},{49,97},{65,17},{97,49},{1... | collective-permute-start | bytes 4816904 | tf_op jit(solution)/shard_map/ppermute | solution.py:117
  213.3 3.0 %collective-permute-start.11 = (bf16[896,896]{1,0:T(8,128)(2,1)}, bf16[896,896]{1,0:T(8,128)(2,1)}, u32[]{:S(2)}, u32[]{:S(2)}) collective-permute-start(bf16[896,896]{1,0:T(8,128)(2,1)} %convolution_convert_fusion), channel_id=1, source_target_pairs={{16,80},{48,112},{64,0},{96,32},{17,81},{49,113},{65,1},{97,33},{1... | collective-permute-start | bytes 4816904 | tf_op jit(solution)/shard_map/ppermute | solution.py:96
  216.4 3.6 %copy.16 = bf16[1,896,896]{1,2,0:T(8,128)(2,1)} copy(bf16[1,896,896]{2,1,0:T(8,128)(2,1)} %param.7) | data formatting | bytes 3211264 | tf_op args[1]
  221.3 4.3 %copy.23 = f32[896,896]{0,1:T(8,128)} copy(f32[896,896]{1,0:T(8,128)} %get-tuple-element.6) | data formatting | bytes 6422528 | tf_op jit(solution)/shard_map/add | solution.py:116
  225.6 7.8 %collective-permute-done.12 = bf16[896,896]{1,0:T(8,128)(2,1)} collective-permute-done((bf16[896,896]{1,0:T(8,128)(2,1)}, bf16[896,896]{1,0:T(8,128)(2,1)}, u32[]{:S(2)}, u32[]{:S(2)}) %collective-permute-start.12) | collective-permute-done | bytes 1605664 | tf_op jit(solution)/shard_map/ppermute | solution.py:117
  233.4 3.6 %copy.24 = f32[896,896]{0,1:T(8,128)} copy(bf16[896,896]{1,0:T(8,128)(2,1)} %collective-permute-done.12) | data formatting | bytes 4816896 | tf_op jit(solution)/shard_map/convert_element_type | solution.py:119
  237.0 11.5 %collective-permute-done.11 = bf16[896,896]{1,0:T(8,128)(2,1)} collective-permute-done((bf16[896,896]{1,0:T(8,128)(2,1)}, bf16[896,896]{1,0:T(8,128)(2,1)}, u32[]{:S(2)}, u32[]{:S(2)}) %collective-permute-start.11) | collective-permute-done | bytes 1605664 | tf_op jit(solution)/shard_map/ppermute | solution.py:96
  248.5 6.5 %fusion.16 = bf16[1,896,896]{1,2,0:T(8,128)(2,1)} fusion(f32[896,896]{0,1:T(8,128)} %copy.24, f32[896,896]{0,1:T(8,128)} %copy.23, bf16[896,896]{1,0:T(8,128)(2,1)} %collective-permute-done.11, bf16[896,896]{0,1:T(8,128)(2,1)S(1)} %copy.18, bf16[1,896,896]{1,2,0:T(8,128)(2,1)} %copy.16, f32[]{:T(128)} %bitcast.113, f32[896]{0:T(1024)S(1)} %select_bitcast_fusion, ...), kind=kLoop, calls=%fused_computation.23 | loop fusion | flops 10436608 | bytes 14454277 | tf_op jit(solution)/shard_map/broadcast_in_dim | solution.py:129
  255.1 3.6 %copy.25 = bf16[1,896,896]{2,1,0:T(8,128)(2,1)} copy(bf16[1,896,896]{1,2,0:T(8,128)(2,1)} %fusion.16) | data formatting | bytes 3211264 | tf_op jit(solution)/shard_map/broadcast_in_dim | solution.py:129
  (55 shorter events, 6.1 us)
Async XLA Ops:
  0.0 220.6 %copy-start = (f32[4096]{0:T(1024)S(1)}, f32[4096]{0:T(1024)}, u32[]{:S(2)}) copy-start(f32[4096]{0:T(1024)} %param.10) | copy-start | bytes 49156
  0.0 12.4 %collective-permute-start = (s32[7]{0:T(128)}, s32[7]{0:T(128)S(1)}, u32[]{:S(2)}, u32[]{:S(2)}) collective-permute-start(s32[7]{0:T(128)} %bitcast.120), channel_id=1, source_target_pairs={{0,32},{32,0},{64,96},{96,64},{1,33},{33,1},{65,97},{97,65},{2,34}... | collective-permute-start | bytes 92 | tf_op jit(solution)/shard_map/ppermute | solution.py:84
  2.5 10.0 %copy-start.6 = (s32[1,7]{1,0:T(1,128)S(1)}, s32[1,7]{1,0:T(1,128)}, u32[]{:S(2)}) copy-start(s32[1,7]{1,0:T(1,128)} %param.9) | copy-start | bytes 88
  5.6 37.2 %all-to-all-start = ((bf16[16,2,8,4096]{3,2,1,0:T(8,128)(2,1)}), bf16[16,2,8,4096]{3,2,1,0:T(8,128)(2,1)S(1)}, u32[]{:S(2)}, u32[]{:S(2)}) async-start(bf16[16,2,8,4096]{3,2,1,0:T(8,128)(2,1)} %bitcast.117), calls=%async_computation | async-start | bytes 4194304 | tf_op jit(solution)/shard_map/all_to_all | solution.py:81
  12.5 2.1 collective-permute-start.1
  14.6 5.2 %collective-permute-start.2 = (s32[4,7]{1,0:T(4,128)S(1)}, s32[4,7]{1,0:T(4,128)S(1)}, u32[]{:S(2)}, u32[]{:S(2)}) collective-permute-start(s32[4,7]{1,0:T(4,128)S(1)} %pad_add_fusion), channel_id=1, source_target_pairs={{1,0},{2,1},{3,2},{0,3},{5,4},{6,5},{7,6},{4,7},{9,8},{10,9},{11,1... | collective-permute-start | bytes 344 | tf_op jit(solution)/shard_map/ppermute | solution.py:39
  17.5 9.2 %collective-permute-start.3 = (s32[4,7]{1,0:T(4,128)S(1)}, s32[4,7]{1,0:T(4,128)S(1)}, u32[]{:S(2)}, u32[]{:S(2)}) collective-permute-start(s32[4,7]{1,0:T(4,128)S(1)} %pad_add_fusion), channel_id=1, source_target_pairs={{2,0},{3,1},{0,2},{1,3},{6,4},{7,5},{4,6},{5,7},{10,8},{11,9},{8,1... | collective-permute-start | bytes 344 | tf_op jit(solution)/shard_map/ppermute | solution.py:39
  18.1 10.6 %collective-permute-start.4 = (s32[4,7]{1,0:T(4,128)S(1)}, s32[4,7]{1,0:T(4,128)S(1)}, u32[]{:S(2)}, u32[]{:S(2)}) collective-permute-start(s32[4,7]{1,0:T(4,128)S(1)} %pad_add_fusion), channel_id=1, source_target_pairs={{3,0},{0,1},{1,2},{2,3},{7,4},{4,5},{5,6},{6,7},{11,8},{8,9},{9,10... | collective-permute-start | bytes 344 | tf_op jit(solution)/shard_map/ppermute | solution.py:39
  28.8 10.2 %collective-permute-start.5 = (s32[4,4,7]{2,1,0:T(4,128)S(1)}, s32[4,4,7]{2,1,0:T(4,128)S(1)}, u32[]{:S(2)}, u32[]{:S(2)}) collective-permute-start(s32[4,4,7]{2,1,0:T(4,128)S(1)} %get-tuple-element.8), channel_id=1, source_target_pairs={{4,0},{8,4},{12,8},{0,12},{5,1},{9,5},{13,9},{1,13},{6,2},{10,6},{... | collective-permute-start | bytes 1352 | tf_op jit(solution)/shard_map/ppermute | solution.py:39
  38.2 4.0 %collective-permute-start.6 = (s32[4,4,7]{2,1,0:T(4,128)S(1)}, s32[4,4,7]{2,1,0:T(4,128)S(1)}, u32[]{:S(2)}, u32[]{:S(2)}) collective-permute-start(s32[4,4,7]{2,1,0:T(4,128)S(1)} %get-tuple-element.8), channel_id=1, source_target_pairs={{8,0},{12,4},{0,8},{4,12},{9,1},{13,5},{1,9},{5,13},{10,2},{14,6},... | collective-permute-start | bytes 1352 | tf_op jit(solution)/shard_map/ppermute | solution.py:39
  38.9 3.7 %collective-permute-start.7 = (s32[4,4,7]{2,1,0:T(4,128)S(1)}, s32[4,4,7]{2,1,0:T(4,128)S(1)}, u32[]{:S(2)}, u32[]{:S(2)}) collective-permute-start(s32[4,4,7]{2,1,0:T(4,128)S(1)} %get-tuple-element.8), channel_id=1, source_target_pairs={{12,0},{0,4},{4,8},{8,12},{13,1},{1,5},{5,9},{9,13},{14,2},{2,6},{... | collective-permute-start | bytes 1352 | tf_op jit(solution)/shard_map/ppermute | solution.py:39
  46.8 2.7 %copy-start.1 = (bf16[64,7,8,896]{3,2,1,0:T(8,128)(2,1)}, bf16[64,7,8,896]{3,2,1,0:T(8,128)(2,1)S(1)}, u32[]{:S(2)}) copy-start(bf16[64,7,8,896]{3,2,1,0:T(8,128)(2,1)S(1)} %shard_map.64) | copy-start | bytes 19267588
  49.5 8.9 %copy-start.3 = (bf16[1,896,896]{2,1,0:T(8,128)(2,1)S(1)}, bf16[1,896,896]{2,1,0:T(8,128)(2,1)}, u32[]{:S(2)}) copy-start(bf16[1,896,896]{2,1,0:T(8,128)(2,1)} %param.6) | copy-start | bytes 4816900
  49.5 109.2 %all-to-all-start.1 = ((bf16[64,7,8,896]{3,2,1,0:T(8,128)(2,1)}), bf16[64,7,8,896]{3,2,1,0:T(8,128)(2,1)}, u32[]{:S(2)}, u32[]{:S(2)}) async-start(bf16[64,7,8,896]{3,2,1,0:T(8,128)(2,1)} %copy-done.1), calls=%async_computation.1 | async-start | bytes 12845056 | tf_op jit(solution)/shard_map/all_to_all | solution.py:101
  60.0 91.3 %collective-permute-start.8 = (bf16[896,896]{0,1:T(8,128)(2,1)S(1)}, bf16[896,896]{0,1:T(8,128)(2,1)S(1)}, u32[]{:S(2)}, u32[]{:S(2)}) collective-permute-start(bf16[896,896]{0,1:T(8,128)(2,1)S(1)} %bitcast.116), channel_id=1, source_target_pairs={{16,64},{48,96},{64,16},{96,48},{17,65},{49,97},{65,17},{97,49},{1... | collective-permute-start | bytes 4816904 | tf_op jit(solution)/shard_map/ppermute | solution.py:91
  70.3 82.3 %copy-start.4 = (bf16[1,896,896]{2,1,0:T(8,128)(2,1)S(1)}, bf16[1,896,896]{2,1,0:T(8,128)(2,1)}, u32[]{:S(2)}) copy-start(bf16[1,896,896]{2,1,0:T(8,128)(2,1)} %param.6) | copy-start | bytes 4816900
  70.3 82.3 %copy-start.5 = (bf16[1,896,896]{2,1,0:T(8,128)(2,1)S(1)}, bf16[1,896,896]{2,1,0:T(8,128)(2,1)}, u32[]{:S(2)}) copy-start(bf16[1,896,896]{2,1,0:T(8,128)(2,1)} %param.7) | copy-start | bytes 4816900
  152.6 12.6 %collective-permute-start.9 = (bf16[896,896]{0,1:T(8,128)(2,1)}, bf16[896,896]{0,1:T(8,128)(2,1)}, u32[]{:S(2)}, u32[]{:S(2)}) collective-permute-start(bf16[896,896]{0,1:T(8,128)(2,1)} %broadcast_select_fusion), channel_id=1, source_target_pairs={{0,16},{16,0},{1,17},{17,1},{2,18},{18,2},{3,19},{19,3},{4,20},{20... | collective-permute-start | bytes 4816904 | tf_op jit(solution)/shard_map/ppermute | solution.py:33
  200.5 6.3 %copy-start.2 = (f32[2,896,896]{2,1,0:T(8,128)S(1)}, f32[2,896,896]{2,1,0:T(8,128)}, u32[]{:S(2)}) copy-start(f32[2,896,896]{2,1,0:T(8,128)} %fusion.13) | copy-start | bytes 19267588
  203.0 3.9 %collective-permute-start.10 = (bf16[896,896]{1,0:T(8,128)(2,1)S(1)}, bf16[896,896]{1,0:T(8,128)(2,1)S(1)}, u32[]{:S(2)}, u32[]{:S(2)}) collective-permute-start(bf16[896,896]{1,0:T(8,128)(2,1)S(1)} %fusion.7), channel_id=1, source_target_pairs={{0,16},{16,0},{1,17},{17,1},{2,18},{18,2},{3,19},{19,3},{4,20},{20... | collective-permute-start | bytes 4816904 | tf_op jit(solution)/shard_map/ppermute | solution.py:33
  209.5 23.9 %collective-permute-start.12 = (bf16[896,896]{1,0:T(8,128)(2,1)}, bf16[896,896]{1,0:T(8,128)(2,1)}, u32[]{:S(2)}, u32[]{:S(2)}) collective-permute-start(bf16[896,896]{1,0:T(8,128)(2,1)} %get-tuple-element.5), channel_id=1, source_target_pairs={{16,64},{48,96},{64,16},{96,48},{17,65},{49,97},{65,17},{97,49},{1... | collective-permute-start | bytes 4816904 | tf_op jit(solution)/shard_map/ppermute | solution.py:117
  213.3 35.2 %collective-permute-start.11 = (bf16[896,896]{1,0:T(8,128)(2,1)}, bf16[896,896]{1,0:T(8,128)(2,1)}, u32[]{:S(2)}, u32[]{:S(2)}) collective-permute-start(bf16[896,896]{1,0:T(8,128)(2,1)} %convolution_convert_fusion), channel_id=1, source_target_pairs={{16,80},{48,112},{64,0},{96,32},{17,81},{49,113},{65,1},{97,33},{1... | collective-permute-start | bytes 4816904 | tf_op jit(solution)/shard_map/ppermute | solution.py:96

commit v2 on v1

v2 whole, which is shorter than its diff:
```python
import functools

import jax
import jax.numpy as jnp
from jax import lax
from jax.experimental import pallas as pl
from jax.experimental.pallas import tpu as pltpu
from jax.sharding import Mesh
from jax.sharding import PartitionSpec as P

TILE = 128
NVT = 32
DT = 7
DV = DT * TILE
NZ, NC, NX, NY = 4, 2, 4, 4
OWNERS = NX * NY
SLICE = TILE // OWNERS
CHIPS = NZ * OWNERS
PACK = 4
PIECES = ((0, 2), (2, 2), (4, 3))
MIB = 1024 * 1024


def partner_perm(to_other_core):
    pairs = []
    for z in range(NZ):
        core = 1 - z // 2
        target = 1 - core if to_other_core else core
        pairs.append((z * NC + core, (z ^ 2) * NC + target))
    return pairs


def home_perm(from_home):
    pairs = [(z * NC + z // 2, z * NC + 1 - z // 2) for z in range(NZ)]
    return pairs if from_home else [(b, a) for a, b in pairs]


def core_swap(value):
    return lax.ppermute(value, "core", [(0, 1), (1, 0)])


def gather_small(value, axis, size):
    parts = [value]
    for step in range(1, size):
        parts.append(lax.ppermute(value, axis, [((i + step) % size, i) for i in range(size)]))
    stacked = jnp.stack(parts)
    return jnp.roll(stacked, lax.axis_index(axis), axis=0)


def pack_kernel(tiles_ref, rows_ref, out_ref):
    step = pl.program_id(0)
    for slot in range(PACK):
        dest = step * PACK + slot
        tiles = [tiles_ref[dest * DT + t] for t in range(DT)]
        columns = [pl.multiple_of(tile * TILE, TILE) for tile in tiles]
        for i in range(DT):
            for j in range(DT):
                out_ref[slot, i, :, j * TILE : (j + 1) * TILE] = rows_ref[
                    tiles[i], :, pl.ds(columns[j], TILE)
                ]


def pack(tiles, rows):
    return pl.pallas_call(
        pack_kernel,
        out_shape=jax.ShapeDtypeStruct((CHIPS, DT, SLICE, DV), jnp.bfloat16),
        grid_spec=pltpu.PrefetchScalarGridSpec(
            num_scalar_prefetch=1,
            grid=(CHIPS // PACK,),
            in_specs=[pl.BlockSpec((NVT, SLICE, NVT * TILE), lambda s, t: (0, 0, 0))],
            out_specs=pl.BlockSpec((PACK, DT, SLICE, DV), lambda s, t: (s, 0, 0, 0)),
        ),
        compiler_params=pltpu.CompilerParams(vmem_limit_bytes=56 * MIB),
        cost_estimate=pl.CostEstimate(
            flops=0, bytes_accessed=2 * CHIPS * DT * SLICE * DV * 2, transcendentals=0
        ),
    )(tiles, rows)


def cycle_kernel(amps_ref, exch_all_ref, exch_ref, row_ref, col_ref, base_ref, turned_ref):
    cycle = jnp.dot(amps_ref[...], exch_all_ref[...], preferred_element_type=jnp.float32)
    cycle = cycle.astype(jnp.bfloat16).astype(jnp.float32)
    denominator = col_ref[...] + row_ref[...]
    base_ref[...] = (
        exch_ref[...].astype(jnp.float32)
        + denominator * amps_ref[...].astype(jnp.float32)
        + cycle
    )
    turned_ref[...] = cycle.T.astype(jnp.bfloat16)


def cycle_and_base(amps, exch, row, col):
    return pl.pallas_call(
        cycle_kernel,
        out_shape=(
            jax.ShapeDtypeStruct((DV, DV), jnp.float32),
            jax.ShapeDtypeStruct((DV, DV), jnp.bfloat16),
        ),
        grid=(DT,),
        in_specs=[
            pl.BlockSpec((TILE, DV), lambda i: (i, 0)),
            pl.BlockSpec((DV, DV), lambda i: (0, 0)),
            pl.BlockSpec((TILE, DV), lambda i: (i, 0)),
            pl.BlockSpec((1, DV), lambda i: (0, 0)),
            pl.BlockSpec((TILE, 1), lambda i: (i, 0)),
        ],
        out_specs=(
            pl.BlockSpec((TILE, DV), lambda i: (i, 0)),
            pl.BlockSpec((DV, TILE), lambda i: (0, i)),
        ),
        compiler_params=pltpu.CompilerParams(vmem_limit_bytes=32 * MIB),
        cost_estimate=pl.CostEstimate(
            flops=2 * DV**3, bytes_accessed=14 * DV * DV, transcendentals=0
        ),
    )(amps, exch, exch, row, col)


def ladder_step(amps, block, first, count):
    half = lax.dot_general(
        amps,
        block[first * TILE : (first + count) * TILE, :],
        (((1,), (1,)), ((), ())),
        preferred_element_type=jnp.float32,
    ).astype(jnp.bfloat16)
    return jnp.dot(block, half, preferred_element_type=jnp.float32)


def first_kernel(first, count, amps_ref, arrived_ref, extra_ref, kept_ref, sent_ref, block_ref):
    step = pl.program_id(0)
    for i in range(DT):
        tile = arrived_ref[0, :, i].astype(jnp.float32).reshape(TILE, DV)
        block_ref[i * TILE : (i + 1) * TILE, :] = tile.astype(jnp.bfloat16)
    part = ladder_step(amps_ref[...], block_ref[...], first, count)

    @pl.when(step == 0)
    def _():
        kept_ref[...] = part

    @pl.when(step > 0)
    def _():
        kept_ref[...] += part

    @pl.when(step == NZ - 1)
    def _():
        sent_ref[...] = (kept_ref[...] + extra_ref[...].astype(jnp.float32)).astype(jnp.bfloat16)


def next_kernel(first, count, amps_ref, block_ref, extra_ref, kept_ref, sent_ref):
    step = pl.program_id(0)
    part = ladder_step(amps_ref[...], block_ref[...], first, count)

    @pl.when(step == 0)
    def _():
        kept_ref[...] = part

    @pl.when(step > 0)
    def _():
        kept_ref[...] += part

    @pl.when(step == NZ - 1)
    def _():
        sent_ref[...] = (kept_ref[...] + extra_ref[...].astype(jnp.float32)).astype(jnp.bfloat16)


def home_kernel(amps_ref, block_ref, base_ref, home_ref, kept_ref, sent_ref, total):
    step = pl.program_id(0)
    for first, count in PIECES:
        columns = slice(first * TILE, (first + count) * TILE)
        part = ladder_step(amps_ref[...], block_ref[...], first, count)

        @pl.when(step == 0)
        def _(part=part, columns=columns):
            total[:, columns] = part

        @pl.when(step > 0)
        def _(part=part, columns=columns):
            total[:, columns] += part

    @pl.when(step == NZ - 1)
    def _():
        sent_ref[...] = total[...].astype(jnp.bfloat16)
        keep = (home_ref[0] > 0).astype(jnp.float32)
        kept_ref[...] = base_ref[...] + keep * total[...]


def whole(shape):
    return pl.BlockSpec(shape, lambda q: (0,) * len(shape))


def cost(columns):
    return pl.CostEstimate(
        flops=4 * NZ * DV * DV * columns,
        bytes_accessed=2 * NZ * DV * DV + 8 * DV * columns,
        transcendentals=0,
    )


def first_piece(amps, arrived, extra, first, count):
    width = count * TILE
    return pl.pallas_call(
        functools.partial(first_kernel, first, count),
        out_shape=(
            jax.ShapeDtypeStruct((DV, width), jnp.float32),
            jax.ShapeDtypeStruct((DV, width), jnp.bfloat16),
            jax.ShapeDtypeStruct((DV, NZ * DV), jnp.bfloat16),
        ),
        grid=(NZ,),
        in_specs=[
            whole((DV, DV)),
            pl.BlockSpec((1, OWNERS, DT, SLICE, DV), lambda q: (q, 0, 0, 0, 0)),
            whole((DV, width)),
        ],
        out_specs=(
            whole((DV, width)),
            whole((DV, width)),
            pl.BlockSpec((DV, DV), lambda q: (0, q)),
        ),
        compiler_params=pltpu.CompilerParams(vmem_limit_bytes=40 * MIB),
        cost_estimate=cost(width),
    )(amps, arrived, extra)


def next_piece(amps, blocks, extra, first, count):
    width = count * TILE
    return pl.pallas_call(
        functools.partial(next_kernel, first, count),
        out_shape=(
            jax.ShapeDtypeStruct((DV, width), jnp.float32),
            jax.ShapeDtypeStruct((DV, width), jnp.bfloat16),
        ),
        grid=(NZ,),
        in_specs=[
            whole((DV, DV)),
            pl.BlockSpec((DV, DV), lambda q: (0, q)),
            whole((DV, width)),
        ],
        out_specs=(whole((DV, width)), whole((DV, width))),
        compiler_params=pltpu.CompilerParams(vmem_limit_bytes=40 * MIB),
        cost_estimate=cost(width),
    )(amps, blocks, extra)


def home_piece(amps, blocks, base, home):
    return pl.pallas_call(
        home_kernel,
        out_shape=(
            jax.ShapeDtypeStruct((DV, DV), jnp.float32),
            jax.ShapeDtypeStruct((DV, DV), jnp.bfloat16),
        ),
        grid=(NZ,),
        in_specs=[
            whole((DV, DV)),
            pl.BlockSpec((DV, DV), lambda q: (0, q)),
            whole((DV, DV)),
            pl.BlockSpec(memory_space=pltpu.SMEM),
        ],
        out_specs=(whole((DV, DV)), whole((DV, DV))),
        scratch_shapes=[pltpu.VMEM((DV, DV), jnp.float32)],
        compiler_params=pltpu.CompilerParams(vmem_limit_bytes=48 * MIB),
        cost_estimate=cost(DV),
    )(amps, blocks, base, home)


def local(amplitudes, exchange_ints, chol, domain, virt_energy, pair_energy):
    z = lax.axis_index("z")
    core = lax.axis_index("core")
    home = core == z // 2
    amps, exch = amplitudes[0], exchange_ints[0]
    column_group = ("z", "core")

    moved = lax.ppermute(amps, column_group, partner_perm(True))
    mine = jnp.where(home, amps, moved)
    other = core_swap(mine)
    home_amps = jnp.where(home, mine, other)
    remote_amps = jnp.where(home, other, mine)

    spread = chol.reshape(2, OWNERS, SLICE, NVT * TILE).transpose(1, 0, 2, 3)
    spread = lax.all_to_all(spread, ("x", "y"), 0, 0, tiled=True)
    rows = spread.reshape(NVT, SLICE, NVT * TILE)

    zones = lax.ppermute(domain[0], "z", [(i, i ^ 1) for i in range(NZ)])
    column = jnp.stack([jnp.where(z % 2 == 0, domain[0], zones), jnp.where(z % 2 == 0, zones, domain[0])])
    swapped = core_swap(column)
    column = jnp.concatenate([jnp.where(core == 0, column, swapped), jnp.where(core == 0, swapped, column)])
    everyone = gather_small(gather_small(column, "y", NY), "x", NX)
    everyone = everyone.transpose(2, 0, 1, 3).reshape(CHIPS * DT)

    energies = jnp.take(virt_energy.reshape(NVT, TILE), domain[0], axis=0).reshape(DV)
    base, turned = cycle_and_base(
        amps, exch, energies[None, :], (energies - pair_energy[0])[:, None]
    )
    partner_turned = lax.ppermute(turned, column_group, partner_perm(False))

    rows, home_amps, remote_amps, partner_turned = lax.optimization_barrier(
        (rows, home_amps, remote_amps, partner_turned)
    )
    base = base + partner_turned.astype(jnp.float32)

    arrived = lax.all_to_all(pack(everyone, rows), ("z", "x", "y"), 0, 0, tiled=True)
    arrived = arrived.reshape(NZ, OWNERS, DT, SLICE, DV)

    returned = []
    blocks = None
    for first, count in PIECES:
        extra = turned[:, first * TILE : (first + count) * TILE]
        if blocks is None:
            kept, sent, blocks = first_piece(remote_amps, arrived, extra, first, count)
        else:
            kept, sent = next_piece(remote_amps, blocks, extra, first, count)
        received = lax.ppermute(sent, column_group, home_perm(True))
        finished = (kept + received.astype(jnp.float32)).astype(jnp.bfloat16)
        returned.append(lax.ppermute(finished, column_group, partner_perm(True)))
    kept, sent = home_piece(home_amps, blocks, base, home.astype(jnp.int32)[None])
    received = lax.ppermute(sent, column_group, home_perm(False))
    result = (
        kept
        + received.astype(jnp.float32)
        + jnp.concatenate(returned, axis=1).astype(jnp.float32)
    )
    return result.astype(jnp.bfloat16)[None]


def solution(mesh):
    finer = Mesh(mesh.devices.reshape(NZ, NC, NX, NY), ("z", "core", "x", "y"))
    group, everywhere = ("z", "core"), ("z", "core", "x", "y")
    placed = (
        P(everywhere, None, None),
        P(everywhere, None, None),
        P(group, ("x", "y"), None),
        P(everywhere, None),
        P(),
        P(everywhere),
    )
    return jax.shard_map(
        local, mesh=finer, in_specs=placed, out_specs=P(everywhere, None, None), check_vma=False
    )
```

time: 260 us -> 267 us (1.027)
  Pallas kernels: 3.94 us -> 74.4 us
  matrix products: 38.5 us -> 0 us
  local copies, waits for them, and re-layouts: 32.8 us -> 16.1 us
  waiting for transfers between devices: 118 us -> 113 us
  starting transfers between devices: 51.5 us -> 48.5 us
    all_to_all x1, waiting for transfers between devices: 0.01 us -> 86.8 us  [local(): lax.all_to_all(pack(everyone, rows), ('z', 'x', 'y'), 0, 0, tiled=True)]
    ppermute x3 -> x9, waiting for transfers between devices: 100 us -> 14.1 us  [the longest x3 14 us: local(): returned.append(lax.ppermute(finished, column_group, partner_perm(True)))]
    pallas_call x1 -> x6, Pallas kernels: 3.94 us -> 74.4 us  [the longest x1 30.2 us: home_piece(): pl.pallas_call(home_kernel, out_shape=(jax.ShapeDtypeStruct((DV, DV), jnp...]
    dot_general x2 -> x0, matrix products: 38.5 us -> none  [the longest x1 35.3 us: local(): jnp.einsum('qac,pqcb->pab', block, half_ladder, preferred_element_type=jn...]
    ppermute x3 -> x9, starting transfers between devices: 17.2 us -> 25 us  [the longest x3 9.25 us: local(): returned.append(lax.ppermute(finished, column_group, partner_perm(True)))]
    ppermute x6, starting transfers between devices: 14.1 us -> 7.09 us  [gather_small(): lax.ppermute(value, axis, [((i + step) % size, i) for i in range(size)])]
    convert_element_type x2 -> x0, local copies, waits for them, and re-layouts: 6.53 us -> none  [the longest x1 3.62 us: local(): returned.astype(jnp.float32)]
    transpose x1 -> x0, local copies, waits for them, and re-layouts: 6.5 us -> none  [local(): blocks.append(arrived.reshape(NZ, OWNERS, count, SLICE, DV).transpose(0,...]
  transfers between devices with their start and end apart: 15 -> 20, of which waited for: 11 -> 7; matrix products, arithmetic and copies ran while one was open for 12% -> 8% of each run, Pallas kernels for 0% -> 20%
where the time goes in v2:
time: 267 us; the launch traced here: 266 us
  waiting for transfers between devices  113 us (42%)
  Pallas kernels  74.4 us (28%)
  starting transfers between devices  48.5 us (18%)
  local copies, waits for them, and re-layouts  16.1 us (6%)
  other arithmetic  12.7 us (5%)
    all_to_all x1, waiting for transfers between devices, local(): lax.all_to_all(pack(everyone, rows), ('z', 'x', 'y'), 0, 0, tiled=True)  86.8 us
    pallas_call x1, Pallas kernels, home_piece(): pl.pallas_call(home_kernel, out_shape=(jax.ShapeDtypeStruct((DV, DV), jnp...  30.2 us
    pallas_call x2, Pallas kernels, next_piece(): pl.pallas_call(functools.partial(next_kernel, first, count), out_shape=(j...  18.4 us
    ppermute x3, waiting for transfers between devices, local(): returned.append(lax.ppermute(finished, column_group, partner_perm(True)))  14 us
    pallas_call x1, Pallas kernels, first_piece(): pl.pallas_call(functools.partial(first_kernel, first, count), out_shape=(...  10.6 us
    pallas_call x1, Pallas kernels, pack(): pl.pallas_call(pack_kernel, out_shape=jax.ShapeDtypeStruct((CHIPS, DT, SL...  10.1 us
    ppermute x3, starting transfers between devices, local(): returned.append(lax.ppermute(finished, column_group, partner_perm(True)))  9.25 us
    ppermute x6, waiting for transfers between devices, gather_small(): lax.ppermute(value, axis, [((i + step) % size, i) for i in range(size)])  8.54 us
  transfers between devices with their start and end apart: 20, of which 7 were waited for; matrix products, arithmetic and copies ran while one was open for 8% of the time, Pallas kernels for 20%

profile of v2, /device:TPU:1, one launch (start us, length us, event | category | flops | bytes accessed | tf_op | source)
XLA Modules:
  0.0 265.8 jit_solution(7166664473935860533)
XLA Ops:
  0.0 2.5 collective-permute-start.3
  2.5 6.0 %collective-permute-start = (bf16[896,896]{1,0:T(8,128)(2,1)}, bf16[896,896]{1,0:T(8,128)(2,1)}, u32[]{:S(2)}, u32[]{:S(2)}) collective-permute-start(bf16[896,896]{1,0:T(8,128)(2,1)} %bitcast.65), channel_id=1, source_target_pairs={{16,64},{48,96},{64,16},{96,48},{17,65},{49,97},{65,17},{97,49},{1... | collective-permute-start | bytes 4816904 | tf_op jit(solution)/shard_map/ppermute | solution.py:271
  8.5 3.2 %copy.17 = bf16[2,16,8,4096]{3,2,0,1:T(8,128)(2,1)} copy(bf16[2,16,8,4096]{3,2,1,0:T(8,128)(2,1)} %bitcast.70) | data formatting | bytes 4194304 | tf_op jit(solution)/shard_map/reshape | solution.py:277
  11.7 6.9 %all-to-all-start = ((bf16[16,2,8,4096]{3,2,1,0:T(8,128)(2,1)}), bf16[16,2,8,4096]{3,2,1,0:T(8,128)(2,1)}, u32[]{:S(2)}, u32[]{:S(2)}) async-start(bf16[16,2,8,4096]{3,2,1,0:T(8,128)(2,1)} %bitcast.62), calls=%async_computation | async-start | bytes 4194304 | tf_op jit(solution)/shard_map/all_to_all | solution.py:278
  21.0 1.4 copy-done.1
  24.8 5.1 %shard_map.64 = (f32[896,896]{1,0:T(8,128)S(1)}, bf16[896,896]{1,0:T(8,128)(2,1)}) custom-call(bf16[896,896]{1,0:T(8,128)(2,1)S(1)} %bitcast.66, bf16[896,896]{1,0:T(8,128)(2,1)S(1)} %bitcast.68, bf16[896,896]{1,0:T(8,128)(2,1)S(1)} %bitcast.69, f32[1,896]{1,0:T(1,128)S(1)} %get-tuple-element.48.row_ref, f32[896,1]{1,0:T(8,128)S(1)} %bitcast.67), custom_call_target="tpu_custom_call" | custom-call | flops 1438646272 | bytes 11239424 | tf_op jit(solution)/shard_map/pallas_call | solution.py:93
  29.9 2.5 collective-permute-start.2
  33.6 2.9 %collective-permute-start.6 = (s32[4,7]{1,0:T(4,128)S(1)}, s32[4,7]{1,0:T(4,128)S(1)}, u32[]{:S(2)}, u32[]{:S(2)}) collective-permute-start(s32[4,7]{1,0:T(4,128)S(1)} %pad_add_fusion), channel_id=1, source_target_pairs={{2,0},{3,1},{0,2},{1,3},{6,4},{7,5},{4,6},{5,7},{10,8},{11,9},{8,1... | collective-permute-start | bytes 344 | tf_op jit(solution)/shard_map/ppermute | solution.py:45
  38.0 1.7 collective-permute-done.5
  39.6 6.9 %collective-permute-done.6 = s32[4,7]{1,0:T(4,128)S(1)} collective-permute-done((s32[4,7]{1,0:T(4,128)S(1)}, s32[4,7]{1,0:T(4,128)S(1)}, u32[]{:S(2)}, u32[]{:S(2)}) %collective-permute-start.6) | collective-permute-done | bytes 144 | tf_op jit(solution)/shard_map/ppermute | solution.py:45
  46.7 1.9 collective-permute-start.9
  49.3 3.2 %broadcast_select_fusion.2 = bf16[896,896]{1,0:T(8,128)(2,1)} fusion(bf16[896,896]{1,0:T(8,128)(2,1)} %collective-permute-done, pred[]{:T(512)S(6)} %eq.19, bf16[1,896,896]{2,1,0:T(8,128)(2,1)} %param.6), kind=kLoop, calls=%fused_computation.7 | loop fusion | flops 802816 | bytes 4816897 | tf_op jit(solution)/shard_map/jit(_where)/select_n | solution.py:272
  54.7 2.6 collective-permute-done.1
  57.3 3.9 %broadcast_select_fusion = (bf16[896,896]{1,0:T(8,128)(2,1)}, bf16[896,896]{1,0:T(8,128)(2,1)}) fusion(bf16[896,896]{1,0:T(8,128)(2,1)} %collective-permute-done.1, bf16[896,896]{1,0:T(8,128)(2,1)} %broadcast_select_fusion.2, pred[]{:T(512)S(6)} %eq.19), kind=kLoop, calls=%fused_computation.5 | loop fusion | flops 1605632 | bytes 6422529 | tf_op jit(solution)/shard_map/jit(_where)/select_n | solution.py:275
  61.2 10.1 %shard_map.65 = bf16[64,7,8,896]{3,2,1,0:T(8,128)(2,1)} custom-call(s32[448]{0:T(512)} %reshape.100.tiles_ref, bf16[32,8,4096]{2,1,0:T(8,128)(2,1)} %bitcast.2.rows_ref), custom_call_target="tpu_custom_call" | custom-call | bytes 12845056 | tf_op jit(solution)/shard_map/pallas_call | solution.py:64
  71.2 5.7 %all-to-all-start.1 = ((bf16[64,7,8,896]{3,2,1,0:T(8,128)(2,1)}), bf16[64,7,8,896]{3,2,1,0:T(8,128)(2,1)}, u32[]{:S(2)}, u32[]{:S(2)}) async-start(bf16[64,7,8,896]{3,2,1,0:T(8,128)(2,1)} %shard_map.65), calls=%async_computation.1 | async-start | bytes 12845056 | tf_op jit(solution)/shard_map/all_to_all | solution.py:299
  76.9 2.0 slice.11.extra_ref
  79.0 2.2 fusion.4
  81.1 3.3 %convert_add_fusion.base_ref = f32[896,896]{1,0:T(8,128)} fusion(f32[896,896]{1,0:T(8,128)S(1)} %get-tuple-element.25, bf16[896,896]{1,0:T(8,128)(2,1)} %collective-permute-done.2), kind=kLoop, calls=%fused_computation.2 | loop fusion | flops 1605632 | bytes 8028160 | tf_op jit(solution)/shard_map/add | solution.py:297
  84.5 86.8 %all-to-all-done.1 = bf16[64,7,8,896]{3,2,1,0:T(8,128)(2,1)} async-done(((bf16[64,7,8,896]{3,2,1,0:T(8,128)(2,1)}), bf16[64,7,8,896]{3,2,1,0:T(8,128)(2,1)}, u32[]{:S(2)}, u32[]{:S(2)}) %all-to-all-start.1) | async-done | bytes 6422560 | tf_op jit(solution)/shard_map/all_to_all | solution.py:299
  173.7 10.6 %shard_map.66 = (f32[896,256]{1,0:T(8,128)S(1)}, bf16[896,256]{1,0:T(8,128)(2,1)S(1)}, bf16[896,3584]{1,0:T(8,128)(2,1)S(1)}) custom-call(bf16[896,896]{1,0:T(8,128)(2,1)S(1)} %copy-done.2, bf16[4,16,7,8,896]{4,3,2,1,0:T(8,128)(2,1)} %bitcast.21.arrived_ref, bf16[896,256]{1,0:T(8,128)(2,1)S(1)} %copy-done.7), custom_call_target="tpu_custom_call" | custom-call | flops 3288334336 | bytes 8257536 | tf_op jit(solution)/shard_map/pallas_call | solution.py:200
  185.6 9.4 %shard_map.69 = (f32[896,384]{1,0:T(8,128)S(1)}, bf16[896,384]{1,0:T(8,128)(2,1)S(1)}) custom-call(bf16[896,896]{1,0:T(8,128)(2,1)S(1)} %copy-done.2, bf16[896,3584]{1,0:T(8,128)(2,1)S(1)} %get-tuple-element.24.block_ref, bf16[896,384]{1,0:T(8,128)(2,1)S(1)} %copy-done.5), custom_call_target="tpu_custom_call" | custom-call | flops 4932501504 | bytes 9175040 | tf_op jit(solution)/shard_map/pallas_call | solution.py:225
  195.0 1.5 collective-permute-start.16
  196.5 30.2 %shard_map.67 = (f32[896,896]{1,0:T(8,128)}, bf16[896,896]{1,0:T(8,128)(2,1)S(1)}) custom-call(bf16[896,896]{1,0:T(8,128)(2,1)S(1)} %copy-done.4, bf16[896,3584]{1,0:T(8,128)(2,1)} %copy-done.10, f32[896,896]{1,0:T(8,128)} %convert_add_fusion.base_ref, s32[1]{0:T(128)} %bitcast.22.home_ref), custom_call_target="tpu_custom_call" | custom-call | flops 11509170176 | bytes 12845056 | tf_op jit(solution)/shard_map/pallas_call | solution.py:244
  226.7 3.2 %collective-permute-start.11 = (bf16[896,896]{1,0:T(8,128)(2,1)S(1)}, bf16[896,896]{1,0:T(8,128)(2,1)S(1)}, u32[]{:S(2)}, u32[]{:S(2)}) collective-permute-start(bf16[896,896]{1,0:T(8,128)(2,1)S(1)} %get-tuple-element.28), channel_id=1, source_target_pairs={{16,0},{48,32},{64,80},{96,112},{17,1},{49,33},{65,81},{97,113},{1... | collective-permute-start | bytes 4816904 | tf_op jit(solution)/shard_map/ppermute | solution.py:314
  230.0 9.1 %shard_map.68 = (f32[896,256]{1,0:T(8,128)S(1)}, bf16[896,256]{1,0:T(8,128)(2,1)S(1)}) custom-call(bf16[896,896]{1,0:T(8,128)(2,1)S(1)} %copy-done.3, bf16[896,3584]{1,0:T(8,128)(2,1)S(1)} %copy-done.11, bf16[896,256]{1,0:T(8,128)(2,1)S(1)} %copy-done.6), custom_call_target="tpu_custom_call" | custom-call | flops 3288334336 | bytes 8257536 | tf_op jit(solution)/shard_map/pallas_call | solution.py:225
  240.5 1.9 collective-permute-start.13
  242.5 5.4 %collective-permute-start.17 = (bf16[896,384]{1,0:T(8,128)(2,1)S(1)}, bf16[896,384]{1,0:T(8,128)(2,1)S(1)}, u32[]{:S(2)}, u32[]{:S(2)}) collective-permute-start(bf16[896,384]{1,0:T(8,128)(2,1)S(1)} %add_convert_fusion.1), channel_id=1, source_target_pairs={{16,64},{48,96},{64,16},{96,48},{17,65},{49,97},{65,17},{97,49},{1... | collective-permute-start | bytes 2064392 | tf_op jit(solution)/shard_map/ppermute | solution.py:312
  248.1 1.9 collective-permute-start.15
  250.0 1.7 collective-permute-done.13
  251.8 12.3 %collective-permute-done.15 = bf16[896,256]{1,0:T(8,128)(2,1)S(1)} collective-permute-done((bf16[896,256]{1,0:T(8,128)(2,1)S(1)}, bf16[896,256]{1,0:T(8,128)(2,1)S(1)}, u32[]{:S(2)}, u32[]{:S(2)}) %collective-permute-start.15) | collective-permute-done | bytes 458784 | tf_op jit(solution)/shard_map/ppermute | solution.py:312
  264.1 1.8 fusion
  (82 shorter events, 15.2 us)
Async XLA Ops:
  0.0 19.3 %copy-start = (f32[4096]{0:T(1024)S(1)}, f32[4096]{0:T(1024)}, u32[]{:S(2)}) copy-start(f32[4096]{0:T(1024)} %param.10) | copy-start | bytes 49156
  0.0 32.3 %collective-permute-start.3 = (s32[7]{0:T(128)}, s32[7]{0:T(128)S(1)}, u32[]{:S(2)}, u32[]{:S(2)}) collective-permute-start(s32[7]{0:T(128)} %bitcast.71), channel_id=1, source_target_pairs={{0,32},{32,0},{64,96},{96,64},{1,33},{33,1},{65,97},{97,65},{2,34}... | collective-permute-start | bytes 92 | tf_op jit(solution)/shard_map/ppermute | solution.py:281
  2.5 46.9 %collective-permute-start = (bf16[896,896]{1,0:T(8,128)(2,1)}, bf16[896,896]{1,0:T(8,128)(2,1)}, u32[]{:S(2)}, u32[]{:S(2)}) collective-permute-start(bf16[896,896]{1,0:T(8,128)(2,1)} %bitcast.65), channel_id=1, source_target_pairs={{16,64},{48,96},{64,16},{96,48},{17,65},{49,97},{65,17},{97,49},{1... | collective-permute-start | bytes 4816904 | tf_op jit(solution)/shard_map/ppermute | solution.py:271
  11.7 6.9 %copy-start.13 = (s32[1,7]{1,0:T(1,128)S(1)}, s32[1,7]{1,0:T(1,128)}, u32[]{:S(2)}) copy-start(s32[1,7]{1,0:T(1,128)} %param.9) | copy-start | bytes 88
  11.7 49.5 %all-to-all-start = ((bf16[16,2,8,4096]{3,2,1,0:T(8,128)(2,1)}), bf16[16,2,8,4096]{3,2,1,0:T(8,128)(2,1)}, u32[]{:S(2)}, u32[]{:S(2)}) async-start(bf16[16,2,8,4096]{3,2,1,0:T(8,128)(2,1)} %bitcast.62), calls=%async_computation | async-start | bytes 4194304 | tf_op jit(solution)/shard_map/all_to_all | solution.py:278
  21.0 1.4 copy-start.1
  23.4 1.4 copy-start.9
  29.9 31.3 %collective-permute-start.2 = (bf16[896,896]{1,0:T(8,128)(2,1)}, bf16[896,896]{1,0:T(8,128)(2,1)}, u32[]{:S(2)}, u32[]{:S(2)}) collective-permute-start(bf16[896,896]{1,0:T(8,128)(2,1)} %get-tuple-element.20), channel_id=1, source_target_pairs={{16,80},{48,112},{64,0},{96,32},{17,81},{49,113},{65,1},{97,33},{1... | collective-permute-start | bytes 4816904 | tf_op jit(solution)/shard_map/ppermute | solution.py:292
  32.3 1.2 collective-permute-start.4
  33.6 12.9 %collective-permute-start.6 = (s32[4,7]{1,0:T(4,128)S(1)}, s32[4,7]{1,0:T(4,128)S(1)}, u32[]{:S(2)}, u32[]{:S(2)}) collective-permute-start(s32[4,7]{1,0:T(4,128)S(1)} %pad_add_fusion), channel_id=1, source_target_pairs={{2,0},{3,1},{0,2},{1,3},{6,4},{7,5},{4,6},{5,7},{10,8},{11,9},{8,1... | collective-permute-start | bytes 344 | tf_op jit(solution)/shard_map/ppermute | solution.py:45
  36.5 3.1 %collective-permute-start.5 = (s32[4,7]{1,0:T(4,128)S(1)}, s32[4,7]{1,0:T(4,128)S(1)}, u32[]{:S(2)}, u32[]{:S(2)}) collective-permute-start(s32[4,7]{1,0:T(4,128)S(1)} %pad_add_fusion), channel_id=1, source_target_pairs={{1,0},{2,1},{3,2},{0,3},{5,4},{6,5},{7,6},{4,7},{9,8},{10,9},{11,1... | collective-permute-start | bytes 344 | tf_op jit(solution)/shard_map/ppermute | solution.py:45
  37.4 9.1 %collective-permute-start.7 = (s32[4,7]{1,0:T(4,128)S(1)}, s32[4,7]{1,0:T(4,128)S(1)}, u32[]{:S(2)}, u32[]{:S(2)}) collective-permute-start(s32[4,7]{1,0:T(4,128)S(1)} %pad_add_fusion), channel_id=1, source_target_pairs={{3,0},{0,1},{1,2},{2,3},{7,4},{4,5},{5,6},{6,7},{11,8},{8,9},{9,10... | collective-permute-start | bytes 344 | tf_op jit(solution)/shard_map/ppermute | solution.py:45
  46.6 7.3 %collective-permute-start.10 = (s32[4,4,7]{2,1,0:T(4,128)S(1)}, s32[4,4,7]{2,1,0:T(4,128)S(1)}, u32[]{:S(2)}, u32[]{:S(2)}) collective-permute-start(s32[4,4,7]{2,1,0:T(4,128)S(1)} %get-tuple-element.36), channel_id=1, source_target_pairs={{12,0},{0,4},{4,8},{8,12},{13,1},{1,5},{5,9},{9,13},{14,2},{2,6},{... | collective-permute-start | bytes 1352 | tf_op jit(solution)/shard_map/ppermute | solution.py:45
  46.7 7.2 %collective-permute-start.9 = (s32[4,4,7]{2,1,0:T(4,128)S(1)}, s32[4,4,7]{2,1,0:T(4,128)S(1)}, u32[]{:S(2)}, u32[]{:S(2)}) collective-permute-start(s32[4,4,7]{2,1,0:T(4,128)S(1)} %get-tuple-element.36), channel_id=1, source_target_pairs={{8,0},{12,4},{0,8},{4,12},{9,1},{13,5},{1,9},{5,13},{10,2},{14,6},... | collective-permute-start | bytes 1352 | tf_op jit(solution)/shard_map/ppermute | solution.py:45
  48.6 5.2 %collective-permute-start.8 = (s32[4,4,7]{2,1,0:T(4,128)S(1)}, s32[4,4,7]{2,1,0:T(4,128)S(1)}, u32[]{:S(2)}, u32[]{:S(2)}) collective-permute-start(s32[4,4,7]{2,1,0:T(4,128)S(1)} %get-tuple-element.36), channel_id=1, source_target_pairs={{4,0},{8,4},{12,8},{0,12},{5,1},{9,5},{13,9},{1,13},{6,2},{10,6},{... | collective-permute-start | bytes 1352 | tf_op jit(solution)/shard_map/ppermute | solution.py:45
  52.6 4.7 %collective-permute-start.1 = (bf16[896,896]{1,0:T(8,128)(2,1)}, bf16[896,896]{1,0:T(8,128)(2,1)}, u32[]{:S(2)}, u32[]{:S(2)}) collective-permute-start(bf16[896,896]{1,0:T(8,128)(2,1)} %broadcast_select_fusion.2), channel_id=1, source_target_pairs={{0,16},{16,0},{1,17},{17,1},{2,18},{18,2},{3,19},{19,3},{4,20},{20... | collective-permute-start | bytes 4816904 | tf_op jit(solution)/shard_map/ppermute | solution.py:39
  71.2 100.0 %all-to-all-start.1 = ((bf16[64,7,8,896]{3,2,1,0:T(8,128)(2,1)}), bf16[64,7,8,896]{3,2,1,0:T(8,128)(2,1)}, u32[]{:S(2)}, u32[]{:S(2)}) async-start(bf16[64,7,8,896]{3,2,1,0:T(8,128)(2,1)} %shard_map.65), calls=%async_computation.1 | async-start | bytes 12845056 | tf_op jit(solution)/shard_map/all_to_all | solution.py:299
  171.3 1.4 copy-start.2
  173.7 11.9 %copy-start.5 = (bf16[896,384]{1,0:T(8,128)(2,1)S(1)}, bf16[896,384]{1,0:T(8,128)(2,1)}, u32[]{:S(2)}) copy-start(bf16[896,384]{1,0:T(8,128)(2,1)} %slice.11.extra_ref) | copy-start | bytes 2064388
  184.3 10.7 %copy-start.10 = (bf16[896,3584]{1,0:T(8,128)(2,1)}, bf16[896,3584]{1,0:T(8,128)(2,1)S(1)}, u32[]{:S(2)}) copy-start(bf16[896,3584]{1,0:T(8,128)(2,1)S(1)} %get-tuple-element.24.block_ref) | copy-start | bytes 19267588
  184.3 56.1 %collective-permute-start.12 = (bf16[896,256]{1,0:T(8,128)(2,1)S(1)}, bf16[896,256]{1,0:T(8,128)(2,1)S(1)}, u32[]{:S(2)}, u32[]{:S(2)}) collective-permute-start(bf16[896,256]{1,0:T(8,128)(2,1)S(1)} %get-tuple-element.30), channel_id=1, source_target_pairs={{0,16},{32,48},{80,64},{112,96},{1,17},{33,49},{81,65},{113,97},{2... | collective-permute-start | bytes 1376264 | tf_op jit(solution)/shard_map/ppermute | solution.py:310
  185.6 10.9 %copy-start.4 = (bf16[896,896]{1,0:T(8,128)(2,1)S(1)}, bf16[896,896]{1,0:T(8,128)(2,1)}, u32[]{:S(2)}) copy-start(bf16[896,896]{1,0:T(8,128)(2,1)} %get-tuple-element.21.amps_ref) | copy-start | bytes 4816900
  195.0 47.4 %collective-permute-start.16 = (bf16[896,384]{1,0:T(8,128)(2,1)S(1)}, bf16[896,384]{1,0:T(8,128)(2,1)S(1)}, u32[]{:S(2)}, u32[]{:S(2)}) collective-permute-start(bf16[896,384]{1,0:T(8,128)(2,1)S(1)} %get-tuple-element.34), channel_id=1, source_target_pairs={{0,16},{32,48},{80,64},{112,96},{1,17},{33,49},{81,65},{113,97},{2... | collective-permute-start | bytes 2064392 | tf_op jit(solution)/shard_map/ppermute | solution.py:310
  196.5 33.4 %copy-start.3 = (bf16[896,896]{1,0:T(8,128)(2,1)S(1)}, bf16[896,896]{1,0:T(8,128)(2,1)}, u32[]{:S(2)}) copy-start(bf16[896,896]{1,0:T(8,128)(2,1)} %get-tuple-element.22.amps_ref) | copy-start | bytes 4816900
  196.5 33.4 %copy-start.6 = (bf16[896,256]{1,0:T(8,128)(2,1)S(1)}, bf16[896,256]{1,0:T(8,128)(2,1)}, u32[]{:S(2)}) copy-start(bf16[896,256]{1,0:T(8,128)(2,1)} %get-tuple-element.39.extra_ref) | copy-start | bytes 1376260
  196.5 33.4 %copy-start.11 = (bf16[896,3584]{1,0:T(8,128)(2,1)S(1)}, bf16[896,3584]{1,0:T(8,128)(2,1)}, u32[]{:S(2)}) copy-start(bf16[896,3584]{1,0:T(8,128)(2,1)} %copy-done.10) | copy-start | bytes 19267588
  226.7 37.3 %collective-permute-start.11 = (bf16[896,896]{1,0:T(8,128)(2,1)S(1)}, bf16[896,896]{1,0:T(8,128)(2,1)S(1)}, u32[]{:S(2)}, u32[]{:S(2)}) collective-permute-start(bf16[896,896]{1,0:T(8,128)(2,1)S(1)} %get-tuple-element.28), channel_id=1, source_target_pairs={{16,0},{48,32},{64,80},{96,112},{17,1},{49,33},{65,81},{97,113},{1... | collective-permute-start | bytes 4816904 | tf_op jit(solution)/shard_map/ppermute | solution.py:314
  239.0 8.9 %collective-permute-start.14 = (bf16[896,256]{1,0:T(8,128)(2,1)S(1)}, bf16[896,256]{1,0:T(8,128)(2,1)S(1)}, u32[]{:S(2)}, u32[]{:S(2)}) collective-permute-start(bf16[896,256]{1,0:T(8,128)(2,1)S(1)} %get-tuple-element.32), channel_id=1, source_target_pairs={{0,16},{32,48},{80,64},{112,96},{1,17},{33,49},{81,65},{113,97},{2... | collective-permute-start | bytes 1376264 | tf_op jit(solution)/shard_map/ppermute | solution.py:310
  240.5 11.3 %collective-permute-start.13 = (bf16[896,256]{1,0:T(8,128)(2,1)S(1)}, bf16[896,256]{1,0:T(8,128)(2,1)S(1)}, u32[]{:S(2)}, u32[]{:S(2)}) collective-permute-start(bf16[896,256]{1,0:T(8,128)(2,1)S(1)} %add_convert_fusion.3), channel_id=1, source_target_pairs={{16,64},{48,96},{64,16},{96,48},{17,65},{49,97},{65,17},{97,49},{1... | collective-permute-start | bytes 1376264 | tf_op jit(solution)/shard_map/ppermute | solution.py:312
  242.4 21.7 %copy-start.12 = (f32[896,896]{1,0:T(8,128)S(1)}, f32[896,896]{1,0:T(8,128)}, u32[]{:S(2)}) copy-start(f32[896,896]{1,0:T(8,128)} %get-tuple-element.27) | copy-start | bytes 9633796
  242.5 21.5 %collective-permute-start.17 = (bf16[896,384]{1,0:T(8,128)(2,1)S(1)}, bf16[896,384]{1,0:T(8,128)(2,1)S(1)}, u32[]{:S(2)}, u32[]{:S(2)}) collective-permute-start(bf16[896,384]{1,0:T(8,128)(2,1)S(1)} %add_convert_fusion.1), channel_id=1, source_target_pairs={{16,64},{48,96},{64,16},{96,48},{17,65},{49,97},{65,17},{97,49},{1... | collective-permute-start | bytes 2064392 | tf_op jit(solution)/shard_map/ppermute | solution.py:312
  248.1 16.0 %collective-permute-start.15 = (bf16[896,256]{1,0:T(8,128)(2,1)S(1)}, bf16[896,256]{1,0:T(8,128)(2,1)S(1)}, u32[]{:S(2)}, u32[]{:S(2)}) collective-permute-start(bf16[896,256]{1,0:T(8,128)(2,1)S(1)} %add_convert_fusion.2), channel_id=1, source_target_pairs={{16,64},{48,96},{64,16},{96,48},{17,65},{49,97},{65,17},{97,49},{1... | collective-permute-start | bytes 1376264 | tf_op jit(solution)/shard_map/ppermute | solution.py:312
  (2 other events, 2.0 us)

commit v3 on v1

v3 whole, which is shorter than its diff:
```python
import functools

import jax
import jax.numpy as jnp
from jax import lax
from jax.experimental import pallas as pl
from jax.experimental.pallas import tpu as pltpu
from jax.sharding import Mesh
from jax.sharding import PartitionSpec as P

TILE = 128
NVT = 32
DT = 7
DV = DT * TILE
NZ, NC, NX, NY = 4, 2, 4, 4
OWNERS = NX * NY
SLICE = TILE // OWNERS
CHIPS = NZ * OWNERS
REMOTE_PIECES = ((0, 2), (2, 2), (4, 3))
HOME_PIECES = ((0, 3), (3, 4))
MIB = 1024 * 1024


def partner_perm(to_other_core):
    pairs = []
    for z in range(NZ):
        core = 1 - z // 2
        target = 1 - core if to_other_core else core
        pairs.append((z * NC + core, (z ^ 2) * NC + target))
    return pairs


def home_perm(from_home):
    pairs = [(z * NC + z // 2, z * NC + 1 - z // 2) for z in range(NZ)]
    return pairs if from_home else [(b, a) for a, b in pairs]


def core_swap(value):
    return lax.ppermute(value, "core", [(0, 1), (1, 0)])


def gather_small(value, axis, size):
    parts = [value]
    for step in range(1, size):
        parts.append(lax.ppermute(value, axis, [((i + step) % size, i) for i in range(size)]))
    stacked = jnp.stack(parts)
    return jnp.roll(stacked, lax.axis_index(axis), axis=0)


def pack_kernel(tiles_ref, given_ref, out_ref, rows_ref, packed, row_sems, sems):
    fetches = []
    for k in range(NVT // 4):
        part = pl.ds(k * 4, 4)
        fetches.append(pltpu.make_async_copy(given_ref.at[part], rows_ref.at[part], row_sems.at[k]))
    for fetch in fetches:
        fetch.start()
    for fetch in fetches:
        fetch.wait()

    def one(dest, carry):
        tiles = [tiles_ref[dest * DT + t] for t in range(DT)]
        columns = [pl.multiple_of(tile * TILE, TILE) for tile in tiles]
        for i in range(DT):
            for j in range(DT):
                packed[dest, i, :, j * TILE : (j + 1) * TILE] = rows_ref[
                    tiles[i], :, pl.ds(columns[j], TILE)
                ]
        pltpu.make_async_copy(packed.at[dest], out_ref.at[dest], sems.at[dest]).start()
        return carry

    def finish(dest, carry):
        pltpu.make_async_copy(packed.at[dest], out_ref.at[dest], sems.at[dest]).wait()
        return carry

    lax.fori_loop(0, CHIPS, one, 0)
    lax.fori_loop(0, CHIPS, finish, 0)


def pack(tiles, rows):
    shape = (CHIPS, DT, SLICE, DV)
    return pl.pallas_call(
        pack_kernel,
        out_shape=jax.ShapeDtypeStruct(shape, jnp.bfloat16),
        in_specs=[
            pl.BlockSpec(memory_space=pltpu.SMEM),
            pl.BlockSpec(memory_space=pl.ANY),
        ],
        out_specs=pl.BlockSpec(memory_space=pl.ANY),
        scratch_shapes=[
            pltpu.VMEM(rows.shape, jnp.bfloat16),
            pltpu.VMEM(shape, jnp.bfloat16),
            pltpu.SemaphoreType.DMA((NVT // 4,)),
            pltpu.SemaphoreType.DMA((CHIPS,)),
        ],
        compiler_params=pltpu.CompilerParams(vmem_limit_bytes=56 * MIB),
        cost_estimate=pl.CostEstimate(
            flops=0, bytes_accessed=2 * CHIPS * DT * SLICE * DV * 2, transcendentals=0
        ),
    )(tiles, rows)


def cycle_kernel(
    amps_ref, exch_all_ref, exch_ref, row_ref, col_ref, after_ref, base_ref, turned_ref
):
    del after_ref
    cycle = jnp.dot(amps_ref[...], exch_all_ref[...], preferred_element_type=jnp.float32)
    cycle = cycle.astype(jnp.bfloat16).astype(jnp.float32)
    denominator = col_ref[...] + row_ref[...]
    base_ref[...] = (
        exch_ref[...].astype(jnp.float32)
        + denominator * amps_ref[...].astype(jnp.float32)
        + cycle
    )
    turned_ref[...] = cycle.T.astype(jnp.bfloat16)


def cycle_and_base(amps, exch, row, col, after):
    return pl.pallas_call(
        cycle_kernel,
        out_shape=(
            jax.ShapeDtypeStruct((DV, DV), jnp.float32),
            jax.ShapeDtypeStruct((DV, DV), jnp.bfloat16),
        ),
        grid=(DT,),
        in_specs=[
            pl.BlockSpec((TILE, DV), lambda i: (i, 0)),
            pl.BlockSpec((DV, DV), lambda i: (0, 0)),
            pl.BlockSpec((TILE, DV), lambda i: (i, 0)),
            pl.BlockSpec((1, DV), lambda i: (0, 0)),
            pl.BlockSpec((TILE, 1), lambda i: (i, 0)),
            pl.BlockSpec(memory_space=pl.ANY),
        ],
        out_specs=(
            pl.BlockSpec((TILE, DV), lambda i: (i, 0)),
            pl.BlockSpec((DV, TILE), lambda i: (0, i)),
        ),
        compiler_params=pltpu.CompilerParams(vmem_limit_bytes=32 * MIB),
        cost_estimate=pl.CostEstimate(
            flops=2 * DV**3, bytes_accessed=14 * DV * DV, transcendentals=0
        ),
    )(amps, exch, exch, row, col, after)


def whole(shape):
    return pl.BlockSpec(shape, lambda q: (0,) * len(shape))


def ladder_kernel(first, count, raw, home, *refs):
    refs = list(refs)
    amps = [refs.pop(0) for _ in range(DT)]
    given = [refs.pop(0) for _ in range(DT)]
    if home:
        base_ref, home_ref = refs.pop(0), refs.pop(0)
    else:
        extra_ref = refs.pop(0)
    refs.pop(0)
    kept_ref, sent_ref = refs.pop(0), refs.pop(0)
    block_ref = refs.pop(0) if raw else None
    half, total = refs.pop(0), refs.pop(0)
    step = pl.program_id(0)
    if home:
        base, base_sem = refs.pop(0), refs.pop(0)
        columns = pl.ds(first * TILE, count * TILE)
        fetch = pltpu.make_async_copy(base_ref.at[:, columns], base, base_sem)

        @pl.when(step == 0)
        def _():
            fetch.start()

    if raw:
        for i in range(DT):
            tile = given[i][0, :, 0].astype(jnp.float32).reshape(TILE, DV)
            block_ref[i * TILE : (i + 1) * TILE, :] = tile.astype(jnp.bfloat16)
        rows = [block_ref.at[i * TILE : (i + 1) * TILE, :] for i in range(DT)]
    else:
        rows = given
    for start in range(first, first + count, 2):
        some = range(start, min(start + 2, first + count))
        right = jnp.concatenate([rows[t][...] for t in some], axis=0)
        place = slice((start - first) * TILE, (some[-1] + 1 - first) * TILE)
        for c in range(DT):
            half[c * TILE : (c + 1) * TILE, place] = lax.dot_general(
                amps[c][...], right, (((1,), (1,)), ((), ())), preferred_element_type=jnp.float32
            ).astype(jnp.bfloat16)

    @pl.when(step == 0)
    def _():
        for i in range(DT):
            total[i * TILE : (i + 1) * TILE, :] = jnp.dot(
                rows[i][...], half[...], preferred_element_type=jnp.float32
            )

    @pl.when(step > 0)
    def _():
        for i in range(DT):
            total[i * TILE : (i + 1) * TILE, :] += jnp.dot(
                rows[i][...], half[...], preferred_element_type=jnp.float32
            )

    @pl.when(step == NZ - 1)
    def _():
        if home:
            fetch.wait()
            keep = (home_ref[0] > 0).astype(jnp.float32)
            sent_ref[...] = total[...].astype(jnp.bfloat16)
            kept_ref[...] = base[...] + keep * total[...]
        else:
            kept_ref[...] = total[...]
            sent_ref[...] = (total[...] + extra_ref[...].astype(jnp.float32)).astype(jnp.bfloat16)


def ladder_piece(amps, blocks, added, first, count, after, home=None):
    raw = blocks.ndim == 5
    width = count * TILE
    if raw:
        given = [
            pl.BlockSpec((1, OWNERS, 1, SLICE, DV), lambda q, i=i: (q, 0, i, 0, 0)) for i in range(DT)
        ]
    else:
        given = [pl.BlockSpec((TILE, DV), lambda q, i=i: (i, q)) for i in range(DT)]
    anywhere = pl.BlockSpec(memory_space=pl.ANY)
    scratch = [pltpu.VMEM((DV, width), jnp.bfloat16), pltpu.VMEM((DV, width), jnp.float32)]
    out_shape = [
        jax.ShapeDtypeStruct((DV, width), jnp.float32),
        jax.ShapeDtypeStruct((DV, width), jnp.bfloat16),
    ]
    out_specs = [whole((DV, width)), whole((DV, width))]
    if raw:
        out_shape.append(jax.ShapeDtypeStruct((DV, NZ * DV), jnp.bfloat16))
        out_specs.append(pl.BlockSpec((DV, DV), lambda q: (0, q)))
    if home is None:
        more, more_specs = [added], [whole((DV, width))]
    else:
        more, more_specs = [added, home], [anywhere, pl.BlockSpec(memory_space=pltpu.SMEM)]
        scratch += [pltpu.VMEM((DV, width), jnp.float32), pltpu.SemaphoreType.DMA]
    return pl.pallas_call(
        functools.partial(ladder_kernel, first, count, raw, home is not None),
        out_shape=out_shape,
        grid=(NZ,),
        in_specs=[pl.BlockSpec((TILE, DV), lambda q, i=i: (i, 0)) for i in range(DT)]
        + given
        + more_specs
        + [anywhere],
        out_specs=out_specs,
        scratch_shapes=scratch,
        compiler_params=pltpu.CompilerParams(vmem_limit_bytes=36 * MIB),
        cost_estimate=pl.CostEstimate(
            flops=4 * NZ * DV * DV * width,
            bytes_accessed=2 * NZ * DV * DV + 8 * DV * width,
            transcendentals=0,
        ),
    )(*[amps] * DT, *[blocks] * DT, *more, after)


def local(amplitudes, exchange_ints, chol, domain, virt_energy, pair_energy):
    z = lax.axis_index("z")
    core = lax.axis_index("core")
    home = core == z // 2
    amps, exch = amplitudes[0], exchange_ints[0]
    column_group = ("z", "core")

    moved = lax.ppermute(amps, column_group, partner_perm(True))
    mine = jnp.where(home, amps, moved)
    other = core_swap(mine)
    home_amps = jnp.where(home, mine, other)
    remote_amps = jnp.where(home, other, mine)

    spread = chol.reshape(2, OWNERS, SLICE, NVT * TILE).transpose(1, 0, 2, 3)
    spread = lax.all_to_all(spread, ("x", "y"), 0, 0, tiled=True)
    rows = spread.reshape(NVT, SLICE, NVT * TILE)

    zones = lax.ppermute(domain[0], "z", [(i, i ^ 1) for i in range(NZ)])
    column = jnp.stack([jnp.where(z % 2 == 0, domain[0], zones), jnp.where(z % 2 == 0, zones, domain[0])])
    swapped = core_swap(column)
    column = jnp.concatenate([jnp.where(core == 0, column, swapped), jnp.where(core == 0, swapped, column)])
    row_of_chips = gather_small(column, "y", NY)
    everyone = gather_small(row_of_chips, "x", NX)
    everyone = everyone.transpose(2, 0, 1, 3).reshape(CHIPS * DT)

    energies = jnp.take(virt_energy.reshape(NVT, TILE), domain[0], axis=0).reshape(DV)
    base, turned = cycle_and_base(
        amps, exch, energies[None, :], (energies - pair_energy[0])[:, None], row_of_chips
    )
    partner_turned = lax.ppermute(turned, column_group, partner_perm(False))
    base = base + partner_turned.astype(jnp.float32)

    arrived = lax.all_to_all(pack(everyone, rows), ("z", "x", "y"), 0, 0, tiled=True)
    blocks = arrived.reshape(NZ, OWNERS, DT, SLICE, DV)

    finished = []
    for k, (first, count) in enumerate(REMOTE_PIECES):
        extra = turned[:, first * TILE : (first + count) * TILE]
        after = finished[k - 2] if k >= 2 else domain
        parts = ladder_piece(remote_amps, blocks, extra, first, count, after)
        if k == 0:
            blocks = parts[2]
        received = lax.ppermute(parts[1], column_group, home_perm(True))
        finished.append((parts[0] + received.astype(jnp.float32)).astype(jnp.bfloat16))
    returned = [lax.ppermute(piece, column_group, partner_perm(True)) for piece in finished]

    results = []
    for k, (first, count) in enumerate(HOME_PIECES):
        after = finished[len(REMOTE_PIECES) - 2 + k]
        kept, sent = ladder_piece(
            home_amps, blocks, base, first, count, after, home.astype(jnp.int32)[None]
        )
        received = lax.ppermute(sent, column_group, home_perm(False))
        results.append(kept + received.astype(jnp.float32))
    result = jnp.concatenate(results, axis=1) + jnp.concatenate(returned, axis=1).astype(jnp.float32)
    return result.astype(jnp.bfloat16)[None]


def solution(mesh):
    finer = Mesh(mesh.devices.reshape(NZ, NC, NX, NY), ("z", "core", "x", "y"))
    group, everywhere = ("z", "core"), ("z", "core", "x", "y")
    placed = (
        P(everywhere, None, None),
        P(everywhere, None, None),
        P(group, ("x", "y"), None),
        P(everywhere, None),
        P(),
        P(everywhere),
    )
    return jax.shard_map(
        local, mesh=finer, in_specs=placed, out_specs=P(everywhere, None, None), check_vma=False
    )
```

time: 260 us -> 271 us (1.042)
  Pallas kernels: 3.94 us -> 67.3 us
  matrix products: 38.5 us -> 0 us
  local copies, waits for them, and re-layouts: 32.8 us -> 14.4 us
  starting transfers between devices: 51.5 us -> 68.4 us
  waiting for transfers between devices: 118 us -> 109 us
  other arithmetic: 13.1 us -> 9.45 us
    pallas_call x1 -> x7, Pallas kernels: 3.94 us -> 67.3 us  [the longest x5 55.2 us: ladder_piece(): pl.pallas_call(functools.partial(ladder_kernel, first, count, raw, home i...]
    dot_general x2 -> x0, matrix products: 38.5 us -> none  [the longest x1 35.3 us: local(): jnp.einsum('qac,pqcb->pab', block, half_ladder, preferred_element_type=jn...]
    ppermute x3 -> x10, starting transfers between devices: 17.2 us -> 34.7 us  [the longest x1 10.3 us: local(): moved = lax.ppermute(amps, column_group, partner_perm(True))]
    convert_element_type x2 -> x0, local copies, waits for them, and re-layouts: 6.53 us -> none  [the longest x1 3.62 us: local(): returned.astype(jnp.float32)]
    broadcast_in_dim x1 -> x0, other arithmetic: 6.52 us -> none  [local(): return result.astype(jnp.bfloat16)[None]]
    transpose x1 -> x0, local copies, waits for them, and re-layouts: 6.5 us -> none  [local(): blocks.append(arrived.reshape(NZ, OWNERS, count, SLICE, DV).transpose(0,...]
    ppermute x3 -> x10, waiting for transfers between devices: 100 us -> 94.9 us  [the longest x1 82 us: local(): moved = lax.ppermute(amps, column_group, partner_perm(True))]
    add x1 -> x0, local copies, waits for them, and re-layouts: 4.34 us -> none  [local(): finished = ladder[0] + from_other.astype(jnp.float32)]
  transfers between devices with their start and end apart: 15 -> 21, of which waited for: 11 -> 10; matrix products, arithmetic and copies ran while one was open for 12% -> 6% of each run, Pallas kernels for 0% -> 22%
where the time goes in v3:
time: 271 us; the launch traced here: 270 us
  waiting for transfers between devices  109 us (40%)
  starting transfers between devices  68.4 us (25%)
  Pallas kernels  67.3 us (25%)
  local copies, waits for them, and re-layouts  14.4 us (5%)
  other arithmetic  9.45 us (3%)
    ppermute x1, waiting for transfers between devices, local(): moved = lax.ppermute(amps, column_group, partner_perm(True))  82 us
    pallas_call x5, Pallas kernels, ladder_piece(): pl.pallas_call(functools.partial(ladder_kernel, first, count, raw, home i...  55.2 us
    ppermute x6, starting transfers between devices, gather_small(): lax.ppermute(value, axis, [((i + step) % size, i) for i in range(size)])  14.1 us
    ppermute x6, waiting for transfers between devices, gather_small(): lax.ppermute(value, axis, [((i + step) % size, i) for i in range(size)])  13.7 us
    ppermute x3, waiting for transfers between devices, local(): lax.ppermute(piece, column_group, partner_perm(True))  12.9 us
    ppermute x1, starting transfers between devices, local(): moved = lax.ppermute(amps, column_group, partner_perm(True))  10.3 us
    ppermute x3, starting transfers between devices, local(): lax.ppermute(piece, column_group, partner_perm(True))  10.2 us
    all_to_all x1, starting transfers between devices, local(): lax.all_to_all(pack(everyone, rows), ('z', 'x', 'y'), 0, 0, tiled=True)  8.93 us
  transfers between devices with their start and end apart: 21, of which 10 were waited for; matrix products, arithmetic and copies ran while one was open for 6% of the time, Pallas kernels for 22%

profile of v3, /device:TPU:1, one launch (start us, length us, event | category | flops | bytes accessed | tf_op | source)
XLA Modules:
  0.0 270.1 jit_solution(10872462904479266044)
XLA Ops:
  0.0 2.5 collective-permute-start.2
  2.5 3.2 %copy.17 = bf16[2,16,8,4096]{3,2,0,1:T(8,128)(2,1)} copy(bf16[2,16,8,4096]{3,2,1,0:T(8,128)(2,1)} %bitcast.78) | data formatting | bytes 4194304 | tf_op jit(solution)/shard_map/reshape | solution.py:268
  5.6 6.9 %all-to-all-start = ((bf16[16,2,8,4096]{3,2,1,0:T(8,128)(2,1)}), bf16[16,2,8,4096]{3,2,1,0:T(8,128)(2,1)S(1)}, u32[]{:S(2)}, u32[]{:S(2)}) async-start(bf16[16,2,8,4096]{3,2,1,0:T(8,128)(2,1)} %bitcast.77), calls=%async_computation | async-start | bytes 4194304 | tf_op jit(solution)/shard_map/all_to_all | solution.py:269
  14.8 2.9 %collective-permute-start.4 = (s32[4,7]{1,0:T(4,128)S(1)}, s32[4,7]{1,0:T(4,128)S(1)}, u32[]{:S(2)}, u32[]{:S(2)}) collective-permute-start(s32[4,7]{1,0:T(4,128)S(1)} %pad_add_fusion), channel_id=1, source_target_pairs={{1,0},{2,1},{3,2},{0,3},{5,4},{6,5},{7,6},{4,7},{9,8},{10,9},{11,1... | collective-permute-start | bytes 344 | tf_op jit(solution)/shard_map/ppermute | solution.py:45
  20.0 6.9 %collective-permute-done.5 = s32[4,7]{1,0:T(4,128)S(1)} collective-permute-done((s32[4,7]{1,0:T(4,128)S(1)}, s32[4,7]{1,0:T(4,128)S(1)}, u32[]{:S(2)}, u32[]{:S(2)}) %collective-permute-start.5) | collective-permute-done | bytes 144 | tf_op jit(solution)/shard_map/ppermute | solution.py:45
  26.9 2.0 collective-permute-done.6
  29.0 9.4 %collective-permute-start.7 = (s32[4,4,7]{2,1,0:T(4,128)S(1)}, s32[4,4,7]{2,1,0:T(4,128)S(1)}, u32[]{:S(2)}, u32[]{:S(2)}) collective-permute-start(s32[4,4,7]{2,1,0:T(4,128)S(1)} %get-tuple-element.32.after_ref), channel_id=1, source_target_pairs={{4,0},{8,4},{12,8},{0,12},{5,1},{9,5},{13,9},{1,13},{6,2},{10,6},{... | collective-permute-start | bytes 1352 | tf_op jit(solution)/shard_map/ppermute | solution.py:45
  39.1 3.2 %collective-permute-done.8 = s32[4,4,7]{2,1,0:T(4,128)S(1)} collective-permute-done((s32[4,4,7]{2,1,0:T(4,128)S(1)}, s32[4,4,7]{2,1,0:T(4,128)S(1)}, u32[]{:S(2)}, u32[]{:S(2)}) %collective-permute-start.8) | collective-permute-done | bytes 480 | tf_op jit(solution)/shard_map/ppermute | solution.py:45
  44.9 7.0 %shard_map.64 = bf16[64,7,8,896]{3,2,1,0:T(8,128)(2,1)} custom-call(s32[448]{0:T(512)} %reshape.171.tiles_ref, bf16[32,8,4096]{2,1,0:T(8,128)(2,1)} %bitcast.76), custom_call_target="tpu_custom_call" | custom-call | bytes 12845056 | tf_op jit(solution)/shard_map/pallas_call | solution.py:81
  51.9 8.9 %all-to-all-start.1 = ((bf16[64,7,8,896]{3,2,1,0:T(8,128)(2,1)}), bf16[64,7,8,896]{3,2,1,0:T(8,128)(2,1)}, u32[]{:S(2)}, u32[]{:S(2)}) async-start(bf16[64,7,8,896]{3,2,1,0:T(8,128)(2,1)} %shard_map.64), calls=%async_computation.1 | async-start | bytes 12845056 | tf_op jit(solution)/shard_map/all_to_all | solution.py:287
  60.8 10.3 %collective-permute-start = (bf16[896,896]{1,0:T(8,128)(2,1)S(1)}, bf16[896,896]{1,0:T(8,128)(2,1)}, u32[]{:S(2)}, u32[]{:S(2)}) collective-permute-start(bf16[896,896]{1,0:T(8,128)(2,1)S(1)} %bitcast.70), channel_id=1, source_target_pairs={{16,64},{48,96},{64,16},{96,48},{17,65},{49,97},{65,17},{97,49},{1... | collective-permute-start | bytes 4816904 | tf_op jit(solution)/shard_map/ppermute | solution.py:262
  71.8 82.0 %collective-permute-done = bf16[896,896]{1,0:T(8,128)(2,1)} collective-permute-done((bf16[896,896]{1,0:T(8,128)(2,1)S(1)}, bf16[896,896]{1,0:T(8,128)(2,1)}, u32[]{:S(2)}, u32[]{:S(2)}) %collective-permute-start) | collective-permute-done | bytes 1605664 | tf_op jit(solution)/shard_map/ppermute | solution.py:262
  153.8 2.8 %broadcast_select_fusion.2 = bf16[896,896]{1,0:T(8,128)(2,1)} fusion(bf16[896,896]{1,0:T(8,128)(2,1)} %collective-permute-done, pred[]{:T(512)S(6)} %eq.19, bf16[1,896,896]{2,1,0:T(8,128)(2,1)S(1)} %copy-done.7), kind=kLoop, calls=%fused_computation.8 | loop fusion | flops 802816 | bytes 4816897 | tf_op jit(solution)/shard_map/jit(_where)/select_n | solution.py:263
  158.9 5.0 %shard_map.65 = (f32[896,896]{1,0:T(8,128)S(1)}, bf16[896,896]{1,0:T(8,128)(2,1)}) custom-call(bf16[896,896]{1,0:T(8,128)(2,1)S(1)} %bitcast.71, bf16[896,896]{1,0:T(8,128)(2,1)S(1)} %bitcast.74, bf16[896,896]{1,0:T(8,128)(2,1)S(1)} %bitcast.75, f32[1,896]{1,0:T(1,128)S(1)} %get-tuple-element.44.row_ref, f32[896,1]{1,0:T(8,128)S(1)} %bitcast.72, ...), custom_call_target="tpu_custom_call" | custom-call | flops 1438646272 | bytes 11239424 | tf_op jit(solution)/shard_map/pallas_call | solution.py:118
  164.0 1.6 copy-done.2
  165.6 5.1 %collective-permute-start.10 = (bf16[896,896]{1,0:T(8,128)(2,1)}, bf16[896,896]{1,0:T(8,128)(2,1)}, u32[]{:S(2)}, u32[]{:S(2)}) collective-permute-start(bf16[896,896]{1,0:T(8,128)(2,1)} %get-tuple-element.18), channel_id=1, source_target_pairs={{16,80},{48,112},{64,0},{96,32},{17,81},{49,113},{65,1},{97,33},{1... | collective-permute-start | bytes 4816904 | tf_op jit(solution)/shard_map/ppermute | solution.py:284
  170.8 2.0 slice.11.refs_14_
  172.8 2.2 fusion.4
  175.0 2.2 broadcast_select_fusion
  178.2 9.5 %shard_map.66 = (f32[896,256]{1,0:T(8,128)S(1)}, bf16[896,256]{1,0:T(8,128)(2,1)S(1)}, bf16[896,3584]{1,0:T(8,128)(2,1)S(1)}) custom-call(bf16[896,896]{1,0:T(8,128)(2,1)S(1)} %get-tuple-element.33.refs_0_.refs_1_.refs_2_.refs_3_.refs_4_.refs_5_.refs_6_, bf16[896,896]{1,0:T(8,128)(2,1)S(1)} %get-tuple-element.33.refs_0_.refs_1_.refs_2_.refs_3_.refs_4_.refs_5_.refs_6_, ...), custom_call_target="tpu_custom_call" | custom-call | flops 3288334336 | bytes 8257536 | tf_op jit(solution)/shard_map/pallas_call | solution.py:236
  189.1 1.8 convert_add_fusion.refs_14_
  190.9 7.5 %shard_map.67 = (f32[896,256]{1,0:T(8,128)S(1)}, bf16[896,256]{1,0:T(8,128)(2,1)S(1)}) custom-call(bf16[896,896]{1,0:T(8,128)(2,1)S(1)} %get-tuple-element.33.refs_0_.refs_1_.refs_2_.refs_3_.refs_4_.refs_5_.refs_6_, bf16[896,896]{1,0:T(8,128)(2,1)S(1)} %get-tuple-element.33.refs_0_.refs_1_.refs_2_.refs_3_.refs_4_.refs_5_.refs_6_, ...), custom_call_target="tpu_custom_call" | custom-call | flops 3288334336 | bytes 8257536 | tf_op jit(solution)/shard_map/pallas_call | solution.py:236
  200.1 11.9 %shard_map.69 = (f32[896,384]{1,0:T(8,128)S(1)}, bf16[896,384]{1,0:T(8,128)(2,1)S(1)}) custom-call(bf16[896,896]{1,0:T(8,128)(2,1)S(1)} %get-tuple-element.33.refs_0_.refs_1_.refs_2_.refs_3_.refs_4_.refs_5_.refs_6_, bf16[896,896]{1,0:T(8,128)(2,1)S(1)} %get-tuple-element.33.refs_0_.refs_1_.refs_2_.refs_3_.refs_4_.refs_5_.refs_6_, ...), custom_call_target="tpu_custom_call" | custom-call | flops 4932501504 | bytes 9175040 | tf_op jit(solution)/shard_map/pallas_call | solution.py:236
  213.5 12.0 %shard_map.68 = (f32[896,384]{1,0:T(8,128)S(1)}, bf16[896,384]{1,0:T(8,128)(2,1)S(1)}) custom-call(bf16[896,896]{1,0:T(8,128)(2,1)S(1)} %get-tuple-element.34.refs_0_.refs_1_.refs_2_.refs_3_.refs_4_.refs_5_.refs_6_, bf16[896,896]{1,0:T(8,128)(2,1)S(1)} %get-tuple-element.34.refs_0_.refs_1_.refs_2_.refs_3_.refs_4_.refs_5_.refs_6_, ...), custom_call_target="tpu_custom_call" | custom-call | flops 4932501504 | bytes 9175040 | tf_op jit(solution)/shard_map/pallas_call | solution.py:236
  225.5 3.5 %collective-permute-start.12 = (bf16[896,384]{1,0:T(8,128)(2,1)S(1)}, bf16[896,384]{1,0:T(8,128)(2,1)S(1)}, u32[]{:S(2)}, u32[]{:S(2)}) collective-permute-start(bf16[896,384]{1,0:T(8,128)(2,1)S(1)} %get-tuple-element.24), channel_id=1, source_target_pairs={{16,0},{48,32},{64,80},{96,112},{17,1},{49,33},{65,81},{97,113},{1... | collective-permute-start | bytes 2064392 | tf_op jit(solution)/shard_map/ppermute | solution.py:307
  229.2 14.3 %shard_map.70 = (f32[896,512]{1,0:T(8,128)S(1)}, bf16[896,512]{1,0:T(8,128)(2,1)S(1)}) custom-call(bf16[896,896]{1,0:T(8,128)(2,1)S(1)} %get-tuple-element.34.refs_0_.refs_1_.refs_2_.refs_3_.refs_4_.refs_5_.refs_6_, bf16[896,896]{1,0:T(8,128)(2,1)S(1)} %get-tuple-element.34.refs_0_.refs_1_.refs_2_.refs_3_.refs_4_.refs_5_.refs_6_, ...), custom_call_target="tpu_custom_call" | custom-call | flops 6576668672 | bytes 10092544 | tf_op jit(solution)/shard_map/pallas_call | solution.py:236
  244.9 3.1 %collective-permute-start.18 = (bf16[896,384]{1,0:T(8,128)(2,1)S(1)}, bf16[896,384]{1,0:T(8,128)(2,1)S(1)}, u32[]{:S(2)}, u32[]{:S(2)}) collective-permute-start(bf16[896,384]{1,0:T(8,128)(2,1)S(1)} %add_convert_fusion.refs_16_), channel_id=1, source_target_pairs={{16,64},{48,96},{64,16},{96,48},{17,65},{49,97},{65,17},{97,49},{1... | collective-permute-start | bytes 2064392 | tf_op jit(solution)/shard_map/ppermute | solution.py:299
  248.0 4.0 %collective-permute-start.17 = (bf16[896,256]{1,0:T(8,128)(2,1)S(1)}, bf16[896,256]{1,0:T(8,128)(2,1)S(1)}, u32[]{:S(2)}, u32[]{:S(2)}) collective-permute-start(bf16[896,256]{1,0:T(8,128)(2,1)S(1)} %add_convert_fusion.2.refs_16_), channel_id=1, source_target_pairs={{16,64},{48,96},{64,16},{96,48},{17,65},{49,97},{65,17},{97,49},{1... | collective-permute-start | bytes 1376264 | tf_op jit(solution)/shard_map/ppermute | solution.py:299
  252.0 3.1 %collective-permute-start.16 = (bf16[896,256]{1,0:T(8,128)(2,1)S(1)}, bf16[896,256]{1,0:T(8,128)(2,1)S(1)}, u32[]{:S(2)}, u32[]{:S(2)}) collective-permute-start(bf16[896,256]{1,0:T(8,128)(2,1)S(1)} %add_convert_fusion.1.refs_15_), channel_id=1, source_target_pairs={{16,64},{48,96},{64,16},{96,48},{17,65},{49,97},{65,17},{97,49},{1... | collective-permute-start | bytes 1376264 | tf_op jit(solution)/shard_map/ppermute | solution.py:299
  255.6 8.0 %collective-permute-done.17 = bf16[896,256]{1,0:T(8,128)(2,1)S(1)} collective-permute-done((bf16[896,256]{1,0:T(8,128)(2,1)S(1)}, bf16[896,256]{1,0:T(8,128)(2,1)S(1)}, u32[]{:S(2)}, u32[]{:S(2)}) %collective-permute-start.17) | collective-permute-done | bytes 458784 | tf_op jit(solution)/shard_map/ppermute | solution.py:299
  263.6 4.9 %collective-permute-done.16 = bf16[896,256]{1,0:T(8,128)(2,1)S(1)} collective-permute-done((bf16[896,256]{1,0:T(8,128)(2,1)S(1)}, bf16[896,256]{1,0:T(8,128)(2,1)S(1)}, u32[]{:S(2)}, u32[]{:S(2)}) %collective-permute-start.16) | collective-permute-done | bytes 458784 | tf_op jit(solution)/shard_map/ppermute | solution.py:299
  268.5 1.6 fusion
  (81 shorter events, 17.6 us)
Async XLA Ops:
  0.0 156.6 %copy-start = (f32[4096]{0:T(1024)S(1)}, f32[4096]{0:T(1024)}, u32[]{:S(2)}) copy-start(f32[4096]{0:T(1024)} %param.10) | copy-start | bytes 49156
  0.0 12.6 %collective-permute-start.2 = (s32[7]{0:T(128)}, s32[7]{0:T(128)S(1)}, u32[]{:S(2)}, u32[]{:S(2)}) collective-permute-start(s32[7]{0:T(128)} %bitcast.73), channel_id=1, source_target_pairs={{0,32},{32,0},{64,96},{96,64},{1,33},{33,1},{65,97},{97,65},{2,34}... | collective-permute-start | bytes 92 | tf_op jit(solution)/shard_map/ppermute | solution.py:272
  5.6 6.9 %copy-start.8 = (s32[1,7]{1,0:T(1,128)S(1)}, s32[1,7]{1,0:T(1,128)}, u32[]{:S(2)}) copy-start(s32[1,7]{1,0:T(1,128)} %refs_15_.3) | copy-start | bytes 88
  5.6 37.9 %all-to-all-start = ((bf16[16,2,8,4096]{3,2,1,0:T(8,128)(2,1)}), bf16[16,2,8,4096]{3,2,1,0:T(8,128)(2,1)S(1)}, u32[]{:S(2)}, u32[]{:S(2)}) async-start(bf16[16,2,8,4096]{3,2,1,0:T(8,128)(2,1)} %bitcast.77), calls=%async_computation | async-start | bytes 4194304 | tf_op jit(solution)/shard_map/all_to_all | solution.py:269
  12.6 2.1 collective-permute-start.3
  14.8 5.2 %collective-permute-start.4 = (s32[4,7]{1,0:T(4,128)S(1)}, s32[4,7]{1,0:T(4,128)S(1)}, u32[]{:S(2)}, u32[]{:S(2)}) collective-permute-start(s32[4,7]{1,0:T(4,128)S(1)} %pad_add_fusion), channel_id=1, source_target_pairs={{1,0},{2,1},{3,2},{0,3},{5,4},{6,5},{7,6},{4,7},{9,8},{10,9},{11,1... | collective-permute-start | bytes 344 | tf_op jit(solution)/shard_map/ppermute | solution.py:45
  17.7 9.2 %collective-permute-start.5 = (s32[4,7]{1,0:T(4,128)S(1)}, s32[4,7]{1,0:T(4,128)S(1)}, u32[]{:S(2)}, u32[]{:S(2)}) collective-permute-start(s32[4,7]{1,0:T(4,128)S(1)} %pad_add_fusion), channel_id=1, source_target_pairs={{2,0},{3,1},{0,2},{1,3},{6,4},{7,5},{4,6},{5,7},{10,8},{11,9},{8,1... | collective-permute-start | bytes 344 | tf_op jit(solution)/shard_map/ppermute | solution.py:45
  18.2 10.6 %collective-permute-start.6 = (s32[4,7]{1,0:T(4,128)S(1)}, s32[4,7]{1,0:T(4,128)S(1)}, u32[]{:S(2)}, u32[]{:S(2)}) collective-permute-start(s32[4,7]{1,0:T(4,128)S(1)} %pad_add_fusion), channel_id=1, source_target_pairs={{3,0},{0,1},{1,2},{2,3},{7,4},{4,5},{5,6},{6,7},{11,8},{8,9},{9,10... | collective-permute-start | bytes 344 | tf_op jit(solution)/shard_map/ppermute | solution.py:45
  29.0 10.2 %collective-permute-start.7 = (s32[4,4,7]{2,1,0:T(4,128)S(1)}, s32[4,4,7]{2,1,0:T(4,128)S(1)}, u32[]{:S(2)}, u32[]{:S(2)}) collective-permute-start(s32[4,4,7]{2,1,0:T(4,128)S(1)} %get-tuple-element.32.after_ref), channel_id=1, source_target_pairs={{4,0},{8,4},{12,8},{0,12},{5,1},{9,5},{13,9},{1,13},{6,2},{10,6},{... | collective-permute-start | bytes 1352 | tf_op jit(solution)/shard_map/ppermute | solution.py:45
  38.3 4.0 %collective-permute-start.8 = (s32[4,4,7]{2,1,0:T(4,128)S(1)}, s32[4,4,7]{2,1,0:T(4,128)S(1)}, u32[]{:S(2)}, u32[]{:S(2)}) collective-permute-start(s32[4,4,7]{2,1,0:T(4,128)S(1)} %get-tuple-element.32.after_ref), channel_id=1, source_target_pairs={{8,0},{12,4},{0,8},{4,12},{9,1},{13,5},{1,9},{5,13},{10,2},{14,6},... | collective-permute-start | bytes 1352 | tf_op jit(solution)/shard_map/ppermute | solution.py:45
  39.0 3.7 %collective-permute-start.9 = (s32[4,4,7]{2,1,0:T(4,128)S(1)}, s32[4,4,7]{2,1,0:T(4,128)S(1)}, u32[]{:S(2)}, u32[]{:S(2)}) collective-permute-start(s32[4,4,7]{2,1,0:T(4,128)S(1)} %get-tuple-element.32.after_ref), channel_id=1, source_target_pairs={{12,0},{0,4},{4,8},{8,12},{13,1},{1,5},{5,9},{9,13},{14,2},{2,6},{... | collective-permute-start | bytes 1352 | tf_op jit(solution)/shard_map/ppermute | solution.py:45
  43.5 1.3 copy-start.10
  51.9 9.0 %copy-start.7 = (bf16[1,896,896]{2,1,0:T(8,128)(2,1)S(1)}, bf16[1,896,896]{2,1,0:T(8,128)(2,1)}, u32[]{:S(2)}) copy-start(bf16[1,896,896]{2,1,0:T(8,128)(2,1)} %param.6) | copy-start | bytes 4816900
  51.9 125.3 %all-to-all-start.1 = ((bf16[64,7,8,896]{3,2,1,0:T(8,128)(2,1)}), bf16[64,7,8,896]{3,2,1,0:T(8,128)(2,1)}, u32[]{:S(2)}, u32[]{:S(2)}) async-start(bf16[64,7,8,896]{3,2,1,0:T(8,128)(2,1)} %shard_map.64), calls=%async_computation.1 | async-start | bytes 12845056 | tf_op jit(solution)/shard_map/all_to_all | solution.py:287
  60.8 93.0 %collective-permute-start = (bf16[896,896]{1,0:T(8,128)(2,1)S(1)}, bf16[896,896]{1,0:T(8,128)(2,1)}, u32[]{:S(2)}, u32[]{:S(2)}) collective-permute-start(bf16[896,896]{1,0:T(8,128)(2,1)S(1)} %bitcast.70), channel_id=1, source_target_pairs={{16,64},{48,96},{64,16},{96,48},{17,65},{49,97},{65,17},{97,49},{1... | collective-permute-start | bytes 4816904 | tf_op jit(solution)/shard_map/ppermute | solution.py:262
  156.6 18.3 %collective-permute-start.1 = (bf16[896,896]{1,0:T(8,128)(2,1)}, bf16[896,896]{1,0:T(8,128)(2,1)}, u32[]{:S(2)}, u32[]{:S(2)}) collective-permute-start(bf16[896,896]{1,0:T(8,128)(2,1)} %broadcast_select_fusion.2), channel_id=1, source_target_pairs={{0,16},{16,0},{1,17},{17,1},{2,18},{18,2},{3,19},{19,3},{4,20},{20... | collective-permute-start | bytes 4816904 | tf_op jit(solution)/shard_map/ppermute | solution.py:39
  157.5 1.4 copy-start.9
  164.0 1.6 copy-start.2
  165.6 23.4 %collective-permute-start.10 = (bf16[896,896]{1,0:T(8,128)(2,1)}, bf16[896,896]{1,0:T(8,128)(2,1)}, u32[]{:S(2)}, u32[]{:S(2)}) collective-permute-start(bf16[896,896]{1,0:T(8,128)(2,1)} %get-tuple-element.18), channel_id=1, source_target_pairs={{16,80},{48,112},{64,0},{96,32},{17,81},{49,113},{65,1},{97,33},{1... | collective-permute-start | bytes 4816904 | tf_op jit(solution)/shard_map/ppermute | solution.py:284
  177.2 1.0 copy-start.6
  178.2 10.8 %copy-start.3 = (f32[896,896]{1,0:T(8,128)S(1)}, f32[896,896]{1,0:T(8,128)}, u32[]{:S(2)}) copy-start(f32[896,896]{1,0:T(8,128)} %copy-done.2) | copy-start | bytes 9633796
  187.7 12.3 %collective-permute-start.13 = (bf16[896,256]{1,0:T(8,128)(2,1)S(1)}, bf16[896,256]{1,0:T(8,128)(2,1)S(1)}, u32[]{:S(2)}, u32[]{:S(2)}) collective-permute-start(bf16[896,256]{1,0:T(8,128)(2,1)S(1)} %get-tuple-element.26), channel_id=1, source_target_pairs={{0,16},{32,48},{80,64},{112,96},{1,17},{33,49},{81,65},{113,97},{2... | collective-permute-start | bytes 1376264 | tf_op jit(solution)/shard_map/ppermute | solution.py:297
  189.1 1.8 copy-start.5
  198.4 1.7 copy-start.4
  198.4 14.9 %collective-permute-start.11 = (bf16[896,256]{1,0:T(8,128)(2,1)S(1)}, bf16[896,256]{1,0:T(8,128)(2,1)S(1)}, u32[]{:S(2)}, u32[]{:S(2)}) collective-permute-start(bf16[896,256]{1,0:T(8,128)(2,1)S(1)} %get-tuple-element.22), channel_id=1, source_target_pairs={{0,16},{32,48},{80,64},{112,96},{1,17},{33,49},{81,65},{113,97},{2... | collective-permute-start | bytes 1376264 | tf_op jit(solution)/shard_map/ppermute | solution.py:297
  212.0 17.0 %collective-permute-start.14 = (bf16[896,384]{1,0:T(8,128)(2,1)S(1)}, bf16[896,384]{1,0:T(8,128)(2,1)S(1)}, u32[]{:S(2)}, u32[]{:S(2)}) collective-permute-start(bf16[896,384]{1,0:T(8,128)(2,1)S(1)} %get-tuple-element.28), channel_id=1, source_target_pairs={{0,16},{32,48},{80,64},{112,96},{1,17},{33,49},{81,65},{113,97},{2... | collective-permute-start | bytes 2064392 | tf_op jit(solution)/shard_map/ppermute | solution.py:297
  225.5 29.6 %collective-permute-start.12 = (bf16[896,384]{1,0:T(8,128)(2,1)S(1)}, bf16[896,384]{1,0:T(8,128)(2,1)S(1)}, u32[]{:S(2)}, u32[]{:S(2)}) collective-permute-start(bf16[896,384]{1,0:T(8,128)(2,1)S(1)} %get-tuple-element.24), channel_id=1, source_target_pairs={{16,0},{48,32},{64,80},{96,112},{17,1},{49,33},{65,81},{97,113},{1... | collective-permute-start | bytes 2064392 | tf_op jit(solution)/shard_map/ppermute | solution.py:307
  243.5 11.7 %collective-permute-start.15 = (bf16[896,512]{1,0:T(8,128)(2,1)S(1)}, bf16[896,512]{1,0:T(8,128)(2,1)S(1)}, u32[]{:S(2)}, u32[]{:S(2)}) collective-permute-start(bf16[896,512]{1,0:T(8,128)(2,1)S(1)} %get-tuple-element.30), channel_id=1, source_target_pairs={{16,0},{48,32},{64,80},{96,112},{17,1},{49,33},{65,81},{97,113},{1... | collective-permute-start | bytes 2752520 | tf_op jit(solution)/shard_map/ppermute | solution.py:307
  244.9 23.6 %collective-permute-start.18 = (bf16[896,384]{1,0:T(8,128)(2,1)S(1)}, bf16[896,384]{1,0:T(8,128)(2,1)S(1)}, u32[]{:S(2)}, u32[]{:S(2)}) collective-permute-start(bf16[896,384]{1,0:T(8,128)(2,1)S(1)} %add_convert_fusion.refs_16_), channel_id=1, source_target_pairs={{16,64},{48,96},{64,16},{96,48},{17,65},{49,97},{65,17},{97,49},{1... | collective-permute-start | bytes 2064392 | tf_op jit(solution)/shard_map/ppermute | solution.py:299
  248.0 15.6 %collective-permute-start.17 = (bf16[896,256]{1,0:T(8,128)(2,1)S(1)}, bf16[896,256]{1,0:T(8,128)(2,1)S(1)}, u32[]{:S(2)}, u32[]{:S(2)}) collective-permute-start(bf16[896,256]{1,0:T(8,128)(2,1)S(1)} %add_convert_fusion.2.refs_16_), channel_id=1, source_target_pairs={{16,64},{48,96},{64,16},{96,48},{17,65},{49,97},{65,17},{97,49},{1... | collective-permute-start | bytes 1376264 | tf_op jit(solution)/shard_map/ppermute | solution.py:299
  252.0 16.5 %collective-permute-start.16 = (bf16[896,256]{1,0:T(8,128)(2,1)S(1)}, bf16[896,256]{1,0:T(8,128)(2,1)S(1)}, u32[]{:S(2)}, u32[]{:S(2)}) collective-permute-start(bf16[896,256]{1,0:T(8,128)(2,1)S(1)} %add_convert_fusion.1.refs_15_), channel_id=1, source_target_pairs={{16,64},{48,96},{64,16},{96,48},{17,65},{49,97},{65,17},{97,49},{1... | collective-permute-start | bytes 1376264 | tf_op jit(solution)/shard_map/ppermute | solution.py:299
  268.5 1.6 copy-start.1

commit v4 on v3

v4 whole, which is shorter than its diff:
```python
import functools

import jax
import jax.numpy as jnp
from jax import lax
from jax.experimental import pallas as pl
from jax.experimental.pallas import tpu as pltpu
from jax.sharding import Mesh
from jax.sharding import PartitionSpec as P

TILE = 128
NVT = 32
DT = 7
DV = DT * TILE
NZ, NC, NX, NY = 4, 2, 4, 4
OWNERS = NX * NY
SLICE = TILE // OWNERS
CHIPS = NZ * OWNERS
PIECES = ((0, 4), (4, 3))
MIB = 1024 * 1024


def partner_perm(to_other_core):
    pairs = []
    for z in range(NZ):
        core = 1 - z // 2
        target = 1 - core if to_other_core else core
        pairs.append((z * NC + core, (z ^ 2) * NC + target))
    return pairs


def home_perm(from_home):
    pairs = [(z * NC + z // 2, z * NC + 1 - z // 2) for z in range(NZ)]
    return pairs if from_home else [(b, a) for a, b in pairs]


def core_swap(value):
    return lax.ppermute(value, "core", [(0, 1), (1, 0)])


def spread_kernel(chol_ref, table_ref, out_ref, staged, in_sems, out_sems):
    arriving, leaving = [], []
    for m in range(OWNERS):
        for t in range(2):
            arriving.append(
                pltpu.make_async_copy(
                    chol_ref.at[t * OWNERS + m], staged.at[m, t, :, 0 : NVT * TILE], in_sems.at[m, t]
                )
            )
            leaving.append(
                pltpu.make_async_copy(staged.at[m, t], out_ref.at[m, t], out_sems.at[m, t])
            )
    for copy in arriving:
        copy.start()
    for m in range(OWNERS):
        for t in range(2):
            staged[m, t, :, NVT * TILE :] = table_ref[...]
            arriving[2 * m + t].wait()
            leaving[2 * m + t].start()
    for copy in leaving:
        copy.wait()


def spread(chol, table):
    return pl.pallas_call(
        spread_kernel,
        out_shape=jax.ShapeDtypeStruct((OWNERS, 2, SLICE, (NVT + 1) * TILE), jnp.bfloat16),
        in_specs=[pl.BlockSpec(memory_space=pl.ANY), pl.BlockSpec(memory_space=pltpu.VMEM)],
        out_specs=pl.BlockSpec(memory_space=pl.ANY),
        scratch_shapes=[
            pltpu.VMEM((OWNERS, 2, SLICE, (NVT + 1) * TILE), jnp.bfloat16),
            pltpu.SemaphoreType.DMA((OWNERS, 2)),
            pltpu.SemaphoreType.DMA((OWNERS, 2)),
        ],
        compiler_params=pltpu.CompilerParams(vmem_limit_bytes=56 * MIB),
    )(chol, table)


def pack_kernel(given_ref, out_ref, rows_ref, tables, tiles_ref, packed, row_sems, table_sem, sems):
    fetches = []
    for k in range(NVT // 4):
        part = pl.ds(k * 4, 4)
        fetches.append(pltpu.make_async_copy(given_ref.at[part], rows_ref.at[part], row_sems.at[k]))
    for fetch in fetches:
        fetch.start()
    for fetch in fetches:
        fetch.wait()
    for s in range(OWNERS):
        table = rows_ref[2 * s, :, NVT * TILE :].astype(jnp.float32).astype(jnp.int32)
        tables[s : s + 1, :] = table[0:1, :]
    move = pltpu.make_async_copy(tables, tiles_ref, table_sem)
    move.start()
    move.wait()

    def one(s, carry):
        for z in range(NZ):
            dest = z * OWNERS + s
            tiles = [tiles_ref[s, z * DT + t] for t in range(DT)]
            columns = [pl.multiple_of(tile * TILE, TILE) for tile in tiles]
            for i in range(DT):
                for j in range(DT):
                    packed[dest, i, :, j * TILE : (j + 1) * TILE] = rows_ref[
                        tiles[i], :, pl.ds(columns[j], TILE)
                    ]
            pltpu.make_async_copy(packed.at[dest], out_ref.at[dest], sems.at[dest]).start()
        return carry

    def finish(dest, carry):
        pltpu.make_async_copy(packed.at[dest], out_ref.at[dest], sems.at[dest]).wait()
        return carry

    lax.fori_loop(0, OWNERS, one, 0)
    lax.fori_loop(0, CHIPS, finish, 0)


def pack(rows):
    shape = (CHIPS, DT, SLICE, DV)
    return pl.pallas_call(
        pack_kernel,
        out_shape=jax.ShapeDtypeStruct(shape, jnp.bfloat16),
        in_specs=[pl.BlockSpec(memory_space=pl.ANY)],
        out_specs=pl.BlockSpec(memory_space=pl.ANY),
        scratch_shapes=[
            pltpu.VMEM(rows.shape, jnp.bfloat16),
            pltpu.VMEM((OWNERS, TILE), jnp.int32),
            pltpu.SMEM((OWNERS, TILE), jnp.int32),
            pltpu.VMEM(shape, jnp.bfloat16),
            pltpu.SemaphoreType.DMA((NVT // 4,)),
            pltpu.SemaphoreType.DMA,
            pltpu.SemaphoreType.DMA((CHIPS,)),
        ],
        compiler_params=pltpu.CompilerParams(vmem_limit_bytes=56 * MIB),
        cost_estimate=pl.CostEstimate(
            flops=0, bytes_accessed=2 * CHIPS * DT * SLICE * DV * 2, transcendentals=0
        ),
    )(rows)


def cycle_kernel(amps_ref, exch_all_ref, exch_ref, row_ref, col_ref, *refs):
    cycle = jnp.dot(amps_ref[...], exch_all_ref[...], preferred_element_type=jnp.float32)
    cycle = cycle.astype(jnp.bfloat16).astype(jnp.float32)
    denominator = col_ref[...] + row_ref[...]
    base = (
        exch_ref[...].astype(jnp.float32)
        + denominator * amps_ref[...].astype(jnp.float32)
        + cycle
    )
    turned = cycle.T.astype(jnp.bfloat16)
    step = pl.program_id(0)
    for k, (first, count) in enumerate(PIECES):
        refs[1 + k][...] = base[:, first * TILE : (first + count) * TILE]

        @pl.when(jnp.logical_and(step >= first, step < first + count))
        def _(k=k):
            refs[1 + len(PIECES) + k][...] = turned


def cycle_and_base(amps, exch, row, col, after):
    def turned_place(first, count):
        return lambda i: (0, jnp.clip(i - first, 0, count - 1))

    widths = [count * TILE for _, count in PIECES]
    return pl.pallas_call(
        cycle_kernel,
        out_shape=[jax.ShapeDtypeStruct((DV, width), jnp.float32) for width in widths]
        + [jax.ShapeDtypeStruct((DV, width), jnp.bfloat16) for width in widths],
        grid=(DT,),
        in_specs=[
            pl.BlockSpec((TILE, DV), lambda i: (i, 0)),
            pl.BlockSpec((DV, DV), lambda i: (0, 0)),
            pl.BlockSpec((TILE, DV), lambda i: (i, 0)),
            pl.BlockSpec((1, DV), lambda i: (0, 0)),
            pl.BlockSpec((TILE, 1), lambda i: (i, 0)),
            pl.BlockSpec(memory_space=pl.ANY),
        ],
        out_specs=[pl.BlockSpec((TILE, width), lambda i: (i, 0)) for width in widths]
        + [pl.BlockSpec((DV, TILE), turned_place(*piece)) for piece in PIECES],
        compiler_params=pltpu.CompilerParams(vmem_limit_bytes=32 * MIB),
        cost_estimate=pl.CostEstimate(
            flops=2 * DV**3, bytes_accessed=14 * DV * DV, transcendentals=0
        ),
    )(amps, exch, exch, row, col, after)


def choose_kernel(home_ref, *refs):
    sources, targets, sems = refs[:4], refs[4:6], refs[6]
    home = home_ref[0] > 0

    def copies(which):
        made = []
        for k in range(2):
            for i in range(DT):
                part = pl.ds(i * TILE, TILE)
                made.append(
                    pltpu.make_async_copy(
                        sources[2 * which + k].at[part], targets[k].at[part], sems.at[k, i]
                    )
                )
        return made

    for which in range(2):

        @pl.when(home if which == 0 else jnp.logical_not(home))
        def _(which=which):
            made = copies(which)
            for copy in made:
                copy.start()
            for copy in made:
                copy.wait()


def choose(home, at_home, elsewhere):
    vmem = pl.BlockSpec(memory_space=pltpu.VMEM)
    return pl.pallas_call(
        choose_kernel,
        out_shape=[pltpu.VMEM((DV, DV), jnp.bfloat16)] * 2,
        in_specs=[pl.BlockSpec(memory_space=pltpu.SMEM)] + [pl.BlockSpec(memory_space=pl.ANY)] * 4,
        out_specs=[vmem, vmem],
        scratch_shapes=[pltpu.SemaphoreType.DMA((2, DT))],
        compiler_params=pltpu.CompilerParams(vmem_limit_bytes=8 * MIB),
    )(home, *at_home, *elsewhere)


def ladder_kernel(first, count, raw, home, amps_ref, given_ref, added_ref, *refs):
    refs = list(refs)
    base_ref = refs.pop(0) if home else None
    home_ref = refs.pop(0) if home else None
    refs.pop(0)
    kept_ref, sent_ref = refs.pop(0), refs.pop(0)
    block_ref = refs.pop(0) if raw else given_ref
    half, total = refs.pop(0), refs.pop(0)
    if raw:
        landed, sems = refs.pop(0), refs.pop(0)
        copies = [
            [
                pltpu.make_async_copy(given_ref.at[q, :, i], landed.at[q, i], sems.at[q, i])
                for i in range(DT)
            ]
            for q in range(NZ)
        ]
        for q in range(NZ):
            for copy in copies[q]:
                copy.start()
    for q in range(NZ):
        if raw:
            for i in range(DT):
                copies[q][i].wait()
                tile = landed[q, i].astype(jnp.float32).reshape(TILE, DV)
                block_ref[q, i * TILE : (i + 1) * TILE, :] = tile.astype(jnp.bfloat16)
        for start in range(first, first + count, 2):
            stop = min(start + 2, first + count)
            half[:, (start - first) * TILE : (stop - first) * TILE] = lax.dot_general(
                amps_ref[...],
                block_ref[q, start * TILE : stop * TILE, :],
                (((1,), (1,)), ((), ())),
                preferred_element_type=jnp.float32,
            ).astype(jnp.bfloat16)
        for i in range(DT):
            place = slice(i * TILE, (i + 1) * TILE)
            part = jnp.dot(
                block_ref[q, place, :], half[...], preferred_element_type=jnp.float32
            )
            if q > 0:
                part = part + total[place, :]
            if q < NZ - 1:
                total[place, :] = part
            elif home:
                keep = (home_ref[0] > 0).astype(jnp.float32)
                sent_ref[place, :] = part.astype(jnp.bfloat16)
                added = base_ref[place, :] + added_ref[place, :].astype(jnp.float32)
                kept_ref[place, :] = added + keep * part
            else:
                kept_ref[place, :] = part
                sent_ref[place, :] = (part + added_ref[place, :].astype(jnp.float32)).astype(
                    jnp.bfloat16
                )


def in_vmem(value):
    return pltpu.with_memory_space_constraint(value, pltpu.VMEM)


def ladder_piece(amps, blocks, added, first, count, after, base=None, home=None):
    raw = blocks.ndim == 5
    width = count * TILE
    vmem = pl.BlockSpec(memory_space=pltpu.VMEM)
    anywhere = pl.BlockSpec(memory_space=pl.ANY)
    scratch = [pltpu.VMEM((DV, width), jnp.bfloat16), pltpu.VMEM((DV, width), jnp.float32)]
    out_shape = [
        pltpu.VMEM((DV, width), jnp.float32),
        pltpu.VMEM((DV, width), jnp.bfloat16),
    ]
    if raw:
        out_shape.append(pltpu.VMEM((NZ, DV, DV), jnp.bfloat16))
        scratch += [
            pltpu.VMEM((NZ, DT, OWNERS, SLICE, DV), jnp.bfloat16),
            pltpu.SemaphoreType.DMA((NZ, DT)),
        ]
    operands = [in_vmem(amps), blocks if raw else in_vmem(blocks), in_vmem(added)]
    specs = [vmem, anywhere if raw else vmem, vmem]
    if home is not None:
        operands += [in_vmem(base), home]
        specs += [vmem, pl.BlockSpec(memory_space=pltpu.SMEM)]
    return pl.pallas_call(
        functools.partial(ladder_kernel, first, count, raw, home is not None),
        out_shape=out_shape,
        in_specs=specs + [anywhere],
        out_specs=[vmem] * len(out_shape),
        scratch_shapes=scratch,
        compiler_params=pltpu.CompilerParams(vmem_limit_bytes=16 * MIB),
        cost_estimate=pl.CostEstimate(
            flops=4 * NZ * DV * DV * width,
            bytes_accessed=2 * NZ * DV * DV + 8 * DV * width,
            transcendentals=0,
        ),
    )(*operands, after)


def local(amplitudes, exchange_ints, chol, domain, virt_energy, pair_energy):
    z = lax.axis_index("z")
    core = lax.axis_index("core")
    home = core == z // 2
    amps, exch = amplitudes[0], exchange_ints[0]
    column_group = ("z", "core")

    zones = lax.ppermute(domain[0], "z", [(i, i ^ 1) for i in range(NZ)])
    column = jnp.stack([jnp.where(z % 2 == 0, domain[0], zones), jnp.where(z % 2 == 0, zones, domain[0])])
    swapped = core_swap(column)
    column = jnp.concatenate([jnp.where(core == 0, column, swapped), jnp.where(core == 0, swapped, column)])
    table = column.reshape(1, NZ * DT).astype(jnp.bfloat16)
    table = jnp.pad(table, ((0, SLICE - 1), (0, TILE - NZ * DT)))

    outgoing = spread(chol.reshape(2 * OWNERS, SLICE, NVT * TILE), table)
    rows = lax.all_to_all(outgoing, ("x", "y"), 0, 0, tiled=True)
    rows = rows.reshape(NVT, SLICE, (NVT + 1) * TILE)

    energies = jnp.take(virt_energy.reshape(NVT, TILE), domain[0], axis=0).reshape(DV)
    parts = cycle_and_base(
        amps, exch, energies[None, :], (energies - pair_energy[0])[:, None], outgoing
    )
    bases, turned = parts[: len(PIECES)], parts[len(PIECES) :]
    partner_turned = [lax.ppermute(piece, column_group, partner_perm(False)) for piece in turned]

    early, _ = lax.optimization_barrier((amps, outgoing))
    moved = lax.ppermute(early, column_group, partner_perm(True))
    home_amps, _ = lax.optimization_barrier((amps, turned[0]))
    home_amps = lax.ppermute(home_amps, column_group, home_perm(True))
    moved, _ = lax.optimization_barrier((moved, turned[0]))
    remote_amps = lax.ppermute(moved, column_group, home_perm(False))
    is_home = home.astype(jnp.int32)[None]
    home_amps, remote_amps = choose(is_home, (amps, remote_amps), (home_amps, moved))

    rows, home_amps, remote_amps, *partner_turned = lax.optimization_barrier(
        (rows, home_amps, remote_amps, *partner_turned)
    )

    arrived = lax.all_to_all(pack(rows), ("z", "x", "y"), 0, 0, tiled=True)
    blocks = arrived.reshape(NZ, OWNERS, DT, SLICE, DV)

    returned, waiting = [], None
    for k, (first, count) in enumerate(PIECES):
        kept, sent, *natural = ladder_piece(remote_amps, blocks, turned[k], first, count, domain)
        if natural:
            blocks = natural[0]
        received = lax.ppermute(sent, column_group, home_perm(True))
        if k < len(PIECES) - 1:
            finished = (kept + received.astype(jnp.float32)).astype(jnp.bfloat16)
            returned.append(lax.ppermute(finished, column_group, partner_perm(True)))

    results = []
    after = [sent, returned[0]]
    for k, (first, count) in enumerate(PIECES):
        held, sent = ladder_piece(
            home_amps, blocks, partner_turned[k], first, count, after[k], bases[k], is_home
        )
        if k == 0:
            kept, _ = lax.optimization_barrier((kept, sent))
            finished = (kept + received.astype(jnp.float32)).astype(jnp.bfloat16)
            returned.append(lax.ppermute(finished, column_group, partner_perm(True)))
        else:
            sent, *returned = lax.optimization_barrier((sent, *returned))
        results.append((held, lax.ppermute(sent, column_group, home_perm(False))))
    result = [
        held + came.astype(jnp.float32) + back.astype(jnp.float32)
        for (held, came), back in zip(results, returned)
    ]
    return jnp.concatenate(result, axis=1).astype(jnp.bfloat16)[None]


def solution(mesh):
    finer = Mesh(mesh.devices.reshape(NZ, NC, NX, NY), ("z", "core", "x", "y"))
    group, everywhere = ("z", "core"), ("z", "core", "x", "y")
    placed = (
        P(everywhere, None, None),
        P(everywhere, None, None),
        P(group, ("x", "y"), None),
        P(everywhere, None),
        P(),
        P(everywhere),
    )
    return jax.shard_map(
        local, mesh=finer, in_specs=placed, out_specs=P(everywhere, None, None), check_vma=False
    )
```

time: 271 us -> 212 us (0.78)
  waiting for transfers between devices: 109 us -> 12.9 us
  blocking collectives: 0 us -> 86.5 us
  starting transfers between devices: 68.4 us -> 39.1 us
  Pallas kernels: 67.3 us -> 60.4 us
  local copies, waits for them, and re-layouts: 14.4 us -> 7.59 us
  other arithmetic: 9.45 us -> 3.17 us
    ppermute x16 -> x11, waiting for transfers between devices: 109 us -> 11 us  [the longest x2 8.91 us: local(): lax.ppermute(piece, column_group, partner_perm(False))]
    all_to_all x0 -> x1, blocking collectives: none -> 86.5 us  [local(): arrived = lax.all_to_all(pack(rows), ('z', 'x', 'y'), 0, 0, tiled=True)]
    ppermute x16 -> x11, starting transfers between devices: 48.8 us -> 28 us  [the longest x2 7.59 us: local(): returned.append(lax.ppermute(finished, column_group, partner_perm(True)))]
    pallas_call x5 -> x4, Pallas kernels: 55.2 us -> 39.2 us  [ladder_piece(): pl.pallas_call(functools.partial(ladder_kernel, first, count, raw, home i...]
    pallas_call x1 -> x3, Pallas kernels: 5.02 us -> 14.4 us  [the longest x1 7.17 us: cycle_and_base(): pl.pallas_call(cycle_kernel, out_shape=[jax.ShapeDtypeStruct((DV, width),...]
    all_to_all x2 -> x1, starting transfers between devices: 15.8 us -> 6.94 us  [local(): rows = lax.all_to_all(outgoing, ('x', 'y'), 0, 0, tiled=True)]
    select_n x3 -> x0, other arithmetic: 5.04 us -> none  [the longest x1 2.83 us: local(): mine = jnp.where(home, amps, moved)]
    slice x2 -> x0, local copies, waits for them, and re-layouts: 4.21 us -> none  [local(): extra = turned[:, first * TILE:(first + count) * TILE]]
  transfers between devices with their start and end apart: 21 -> 14, of which waited for: 10 -> 5; matrix products, arithmetic and copies ran while one was open for 6% -> 1% of each run, Pallas kernels for 22% -> 18%
where the time goes in v4:
time: 212 us; the launch traced here: 211 us
  blocking collectives  86.5 us (41%)
  Pallas kernels  60.4 us (28%)
  starting transfers between devices  39.1 us (18%)
  waiting for transfers between devices  12.9 us (6%)
  local copies, waits for them, and re-layouts  7.59 us (4%)
  other arithmetic  3.17 us (1%)
    all_to_all x1, blocking collectives, local(): arrived = lax.all_to_all(pack(rows), ('z', 'x', 'y'), 0, 0, tiled=True)  86.5 us
    pallas_call x4, Pallas kernels, ladder_piece(): pl.pallas_call(functools.partial(ladder_kernel, first, count, raw, home i...  39.2 us
    ppermute x2, waiting for transfers between devices, local(): lax.ppermute(piece, column_group, partner_perm(False))  8.91 us
    ppermute x2, starting transfers between devices, local(): returned.append(lax.ppermute(finished, column_group, partner_perm(True)))  7.59 us
    pallas_call x1, Pallas kernels, cycle_and_base(): pl.pallas_call(cycle_kernel, out_shape=[jax.ShapeDtypeStruct((DV, width),...  7.17 us
    all_to_all x1, starting transfers between devices, local(): rows = lax.all_to_all(outgoing, ('x', 'y'), 0, 0, tiled=True)  6.94 us
    pallas_call x1, Pallas kernels, pack(): pl.pallas_call(pack_kernel, out_shape=jax.ShapeDtypeStruct(shape, jnp.bfl...  6.84 us
    unnamed x26, local copies, waits for them, and re-layouts  6.36 us
  transfers between devices with their start and end apart: 14, of which 5 were waited for; matrix products, arithmetic and copies ran while one was open for 1% of the time, Pallas kernels for 18%

profile of v4, /device:TPU:1, one launch (start us, length us, event | category | flops | bytes accessed | tf_op | source)
XLA Modules:
  0.0 210.7 jit_solution(9914435790082778883)
XLA Ops:
  0.0 2.5 %collective-permute-start = (s32[7]{0:T(128)}, s32[7]{0:T(128)S(1)}, u32[]{:S(2)}, u32[]{:S(2)}) collective-permute-start(s32[7]{0:T(128)} %bitcast.41), channel_id=1, source_target_pairs={{0,32},{32,0},{64,96},{96,64},{1,33},{33,1},{65,97},{97,65},{2,34}... | collective-permute-start | bytes 92 | tf_op jit(solution)/shard_map/ppermute | solution.py:326
  2.5 1.1 collective-permute-done
  4.2 1.6 collective-permute-start.1
  7.4 3.6 %shard_map.64.refs_0_ = bf16[16,2,8,4224]{3,2,1,0:T(8,128)(2,1)} custom-call(bf16[32,8,4096]{2,1,0:T(8,128)(2,1)} %bitcast.42, bf16[8,128]{1,0:T(8,128)(2,1)} %pad.4.table_ref), custom_call_target="tpu_custom_call" | custom-call | tf_op jit(solution)/shard_map/pallas_call | solution.py:65
  10.9 5.8 %collective-permute-start.2 = (bf16[896,896]{1,0:T(8,128)(2,1)}, bf16[896,896]{1,0:T(8,128)(2,1)}, u32[]{:S(2)}, u32[]{:S(2)}) collective-permute-start(bf16[896,896]{1,0:T(8,128)(2,1)} %bitcast.6.amps_ref.refs_0_), channel_id=1, source_target_pairs={{16,64},{48,96},{64,16},{96,48},{17,65},{49,97},{65,17},{97,49},{1... | collective-permute-start | bytes 4816904 | tf_op jit(solution)/shard_map/ppermute | solution.py:345
  18.0 6.9 %all-to-all-start = ((bf16[16,2,8,4224]{3,2,1,0:T(8,128)(2,1)}), bf16[16,2,8,4224]{3,2,1,0:T(8,128)(2,1)}, u32[]{:S(2)}, u32[]{:S(2)}) async-start(bf16[16,2,8,4224]{3,2,1,0:T(8,128)(2,1)} %shard_map.64.refs_0_), calls=%async_computation | async-start | bytes 4325376 | tf_op jit(solution)/shard_map/all_to_all | solution.py:334
  25.3 1.4 copy-done.2
  26.7 7.2 %shard_map.65 = (f32[896,512]{1,0:T(8,128)S(1)}, f32[896,384]{1,0:T(8,128)S(1)}, bf16[896,512]{1,0:T(8,128)(2,1)}, bf16[896,384]{1,0:T(8,128)(2,1)}) custom-call(bf16[896,896]{1,0:T(8,128)(2,1)} %bitcast.6.amps_ref.refs_0_, bf16[896,896]{1,0:T(8,128)(2,1)S(1)} %bitcast.38, bf16[896,896]{1,0:T(8,128)(2,1)S(1)} %bitcast.39, ...), custom_call_target="tpu_custom_call" | custom-call | flops 1438646272 | bytes 11239424 | tf_op jit(solution)/shard_map/pallas_call | solution.py:163
  33.9 1.3 copy-done.4
  35.1 1.1 copy-done.10
  36.3 1.3 collective-permute-start.4
  37.6 3.2 %collective-permute-start.3 = (bf16[896,896]{1,0:T(8,128)(2,1)}, bf16[896,896]{1,0:T(8,128)(2,1)S(1)}, u32[]{:S(2)}, u32[]{:S(2)}) collective-permute-start(bf16[896,896]{1,0:T(8,128)(2,1)} %collective-permute-done.2.refs_3_), channel_id=1, source_target_pairs={{16,0},{48,32},{64,80},{96,112},{17,1},{49,33},{65,81},{97,113},{1... | collective-permute-start | bytes 4816904 | tf_op jit(solution)/shard_map/ppermute | solution.py:349
  40.8 2.3 %collective-permute-start.5 = (bf16[896,512]{1,0:T(8,128)(2,1)}, bf16[896,512]{1,0:T(8,128)(2,1)}, u32[]{:S(2)}, u32[]{:S(2)}) collective-permute-start(bf16[896,512]{1,0:T(8,128)(2,1)} %get-tuple-element.33.added_ref), channel_id=1, source_target_pairs={{16,80},{48,112},{64,0},{96,32},{17,81},{49,113},{65,1},{97,33},{1... | collective-permute-start | bytes 2752520 | tf_op jit(solution)/shard_map/ppermute | solution.py:342
  43.1 2.2 %collective-permute-start.6 = (bf16[896,384]{1,0:T(8,128)(2,1)}, bf16[896,384]{1,0:T(8,128)(2,1)}, u32[]{:S(2)}, u32[]{:S(2)}) collective-permute-start(bf16[896,384]{1,0:T(8,128)(2,1)} %get-tuple-element.38.added_ref), channel_id=1, source_target_pairs={{16,80},{48,112},{64,0},{96,32},{17,81},{49,113},{65,1},{97,33},{1... | collective-permute-start | bytes 2064392 | tf_op jit(solution)/shard_map/ppermute | solution.py:342
  45.3 3.7 %shard_map.66 = (bf16[896,896]{1,0:T(8,128)(2,1)S(1)}, bf16[896,896]{1,0:T(8,128)(2,1)S(1)}) custom-call(s32[1]{0:T(128)} %bitcast.5.home_ref.refs_1_, bf16[896,896]{1,0:T(8,128)(2,1)} %bitcast.6.amps_ref.refs_0_, bf16[896,896]{1,0:T(8,128)(2,1)S(1)} %collective-permute-done.3.refs_1_, bf16[896,896]{1,0:T(8,128)(2,1)S(1)} %collective-permute-done.4.refs_2_, ...), custom_call_target="tpu_custom_call" | custom-call | tf_op jit(solution)/shard_map/pallas_call | solution.py:214
  48.9 1.1 copy-done.6
  50.1 1.2 copy-done.8
  51.2 8.9 %collective-permute-done.6.added_ref = bf16[896,384]{1,0:T(8,128)(2,1)} collective-permute-done((bf16[896,384]{1,0:T(8,128)(2,1)}, bf16[896,384]{1,0:T(8,128)(2,1)}, u32[]{:S(2)}, u32[]{:S(2)}) %collective-permute-start.6) | collective-permute-done | bytes 688160 | tf_op jit(solution)/shard_map/ppermute | solution.py:342
  60.1 6.8 %shard_map.67 = bf16[64,7,8,896]{3,2,1,0:T(8,128)(2,1)} custom-call(bf16[32,8,4224]{2,1,0:T(8,128)(2,1)} %bitcast.4.given_ref), custom_call_target="tpu_custom_call" | custom-call | bytes 12845056 | tf_op jit(solution)/shard_map/pallas_call | solution.py:118
  67.0 86.5 %all_to_all.10 = bf16[64,7,8,896]{3,2,1,0:T(8,128)(2,1)S(1)} all-to-all(bf16[64,7,8,896]{3,2,1,0:T(8,128)(2,1)} %shard_map.67), channel_id=1, replica_groups=mesh['z'=4,'core'=2,'x'=4,'y'=4] {'z','x','y'}, dimensions={0} | all-to-all | bytes 12845056 | tf_op jit(solution)/shard_map/all_to_all | solution.py:357
  153.5 11.1 %shard_map.68 = (f32[896,512]{1,0:T(8,128)S(1)}, bf16[896,512]{1,0:T(8,128)(2,1)S(1)}, bf16[4,896,896]{2,1,0:T(8,128)(2,1)S(1)}) custom-call(bf16[896,896]{1,0:T(8,128)(2,1)S(1)} %copy-done.9, bf16[4,16,7,8,896]{4,3,2,1,0:T(8,128)(2,1)S(1)} %bitcast.37, bf16[896,512]{1,0:T(8,128)(2,1)} %get-tuple-element.33.added_ref, s32[1,7]{1,0:T(1,128)S(1)} %copy-done.3), custom_call_target="tpu_custom_call" | custom-call | flops 6576668672 | bytes 10092544 | tf_op jit(solution)/shard_map/pallas_call | solution.py:304
  164.7 1.5 collective-permute-start.8
  166.2 9.3 %shard_map.69 = (f32[896,384]{1,0:T(8,128)S(1)}, bf16[896,384]{1,0:T(8,128)(2,1)S(1)}) custom-call(bf16[896,896]{1,0:T(8,128)(2,1)S(1)} %copy-done.9, bf16[4,896,896]{2,1,0:T(8,128)(2,1)S(1)} %get-tuple-element.42.given_ref, bf16[896,384]{1,0:T(8,128)(2,1)} %get-tuple-element.38.added_ref, s32[1,7]{1,0:T(1,128)S(1)} %copy-done.3), custom_call_target="tpu_custom_call" | custom-call | flops 4932501504 | bytes 9175040 | tf_op jit(solution)/shard_map/pallas_call | solution.py:304
  175.5 1.3 collective-permute-start.10
  177.1 5.5 %collective-permute-start.9 = (bf16[896,512]{1,0:T(8,128)(2,1)S(1)}, bf16[896,512]{1,0:T(8,128)(2,1)S(1)}, u32[]{:S(2)}, u32[]{:S(2)}) collective-permute-start(bf16[896,512]{1,0:T(8,128)(2,1)S(1)} %add_convert_fusion.1), channel_id=1, source_target_pairs={{16,64},{48,96},{64,16},{96,48},{17,65},{49,97},{65,17},{97,49},{1... | collective-permute-start | bytes 2752520 | tf_op jit(solution)/shard_map/ppermute | solution.py:368
  182.7 9.4 %shard_map.70 = (f32[896,512]{1,0:T(8,128)S(1)}, bf16[896,512]{1,0:T(8,128)(2,1)S(1)}) custom-call(bf16[896,896]{1,0:T(8,128)(2,1)S(1)} %copy-done.7, bf16[4,896,896]{2,1,0:T(8,128)(2,1)S(1)} %get-tuple-element.42.given_ref, bf16[896,512]{1,0:T(8,128)(2,1)} %collective-permute-done.5.added_ref, f32[896,512]{1,0:T(8,128)S(1)} %copy-done.5, ...), custom_call_target="tpu_custom_call" | custom-call | flops 6576668672 | bytes 10092544 | tf_op jit(solution)/shard_map/pallas_call | solution.py:304
  192.3 2.1 collective-permute-start.11
  194.4 1.6 collective-permute-start.7
  196.0 9.4 %shard_map.71 = (f32[896,384]{1,0:T(8,128)S(1)}, bf16[896,384]{1,0:T(8,128)(2,1)S(1)}) custom-call(bf16[896,896]{1,0:T(8,128)(2,1)S(1)} %copy-done.7, bf16[4,896,896]{2,1,0:T(8,128)(2,1)S(1)} %get-tuple-element.42.given_ref, bf16[896,384]{1,0:T(8,128)(2,1)} %collective-permute-done.6.added_ref, f32[896,384]{1,0:T(8,128)S(1)} %copy-done.11, ...), custom_call_target="tpu_custom_call" | custom-call | flops 4932501504 | bytes 9175040 | tf_op jit(solution)/shard_map/pallas_call | solution.py:304
  206.2 1.3 collective-permute-start.12
  207.9 1.3 collective-permute-done.12
  209.5 1.3 pad_maximum_fusion
  (47 shorter events, 5.1 us)
Async XLA Ops:
  0.0 17.4 %copy-start = (f32[4096]{0:T(1024)S(1)}, f32[4096]{0:T(1024)}, u32[]{:S(2)}) copy-start(f32[4096]{0:T(1024)} %param.10) | copy-start | bytes 49156
  0.0 3.5 %collective-permute-start = (s32[7]{0:T(128)}, s32[7]{0:T(128)S(1)}, u32[]{:S(2)}, u32[]{:S(2)}) collective-permute-start(s32[7]{0:T(128)} %bitcast.41), channel_id=1, source_target_pairs={{0,32},{32,0},{64,96},{96,64},{1,33},{33,1},{65,97},{97,65},{2,34}... | collective-permute-start | bytes 92 | tf_op jit(solution)/shard_map/ppermute | solution.py:326
  4.2 2.5 %collective-permute-start.1 = (s32[2,7]{1,0:T(2,128)S(1)}, s32[2,7]{1,0:T(2,128)S(1)}, u32[]{:S(2)}, u32[]{:S(2)}) collective-permute-start(s32[2,7]{1,0:T(2,128)S(1)} %pad_add_fusion), channel_id=1, source_target_pairs={{0,16},{16,0},{1,17},{17,1},{2,18},{18,2},{3,19},{19,3},{4,20},{20... | collective-permute-start | bytes 176 | tf_op jit(solution)/shard_map/ppermute | solution.py:38
  7.4 10.0 %copy-start.3 = (s32[1,7]{1,0:T(1,128)S(1)}, s32[1,7]{1,0:T(1,128)}, u32[]{:S(2)}) copy-start(s32[1,7]{1,0:T(1,128)} %refs_0_.3) | copy-start | bytes 88
  10.9 26.6 %collective-permute-start.2 = (bf16[896,896]{1,0:T(8,128)(2,1)}, bf16[896,896]{1,0:T(8,128)(2,1)}, u32[]{:S(2)}, u32[]{:S(2)}) collective-permute-start(bf16[896,896]{1,0:T(8,128)(2,1)} %bitcast.6.amps_ref.refs_0_), channel_id=1, source_target_pairs={{16,64},{48,96},{64,16},{96,48},{17,65},{49,97},{65,17},{97,49},{1... | collective-permute-start | bytes 4816904 | tf_op jit(solution)/shard_map/ppermute | solution.py:345
  18.0 7.3 %copy-start.1 = (bf16[16,2,8,4224]{3,2,1,0:T(8,128)(2,1)S(1)}, bf16[16,2,8,4224]{3,2,1,0:T(8,128)(2,1)}, u32[]{:S(2)}) copy-start(bf16[16,2,8,4224]{3,2,1,0:T(8,128)(2,1)} %shard_map.64.refs_0_) | copy-start | bytes 6488068
  18.0 42.1 %all-to-all-start = ((bf16[16,2,8,4224]{3,2,1,0:T(8,128)(2,1)}), bf16[16,2,8,4224]{3,2,1,0:T(8,128)(2,1)}, u32[]{:S(2)}, u32[]{:S(2)}) async-start(bf16[16,2,8,4224]{3,2,1,0:T(8,128)(2,1)} %shard_map.64.refs_0_), calls=%async_computation | async-start | bytes 4325376 | tf_op jit(solution)/shard_map/all_to_all | solution.py:334
  25.3 1.4 copy-start.2
  33.9 1.3 copy-start.4
  35.1 1.1 copy-start.10
  36.3 9.0 %collective-permute-start.4 = (bf16[896,896]{1,0:T(8,128)(2,1)}, bf16[896,896]{1,0:T(8,128)(2,1)S(1)}, u32[]{:S(2)}, u32[]{:S(2)}) collective-permute-start(bf16[896,896]{1,0:T(8,128)(2,1)} %bitcast.6.amps_ref.refs_0_), channel_id=1, source_target_pairs={{0,16},{32,48},{80,64},{112,96},{1,17},{33,49},{81,65},{113,97},{2... | collective-permute-start | bytes 4816904 | tf_op jit(solution)/shard_map/ppermute | solution.py:347
  37.6 7.7 %collective-permute-start.3 = (bf16[896,896]{1,0:T(8,128)(2,1)}, bf16[896,896]{1,0:T(8,128)(2,1)S(1)}, u32[]{:S(2)}, u32[]{:S(2)}) collective-permute-start(bf16[896,896]{1,0:T(8,128)(2,1)} %collective-permute-done.2.refs_3_), channel_id=1, source_target_pairs={{16,0},{48,32},{64,80},{96,112},{17,1},{49,33},{65,81},{97,113},{1... | collective-permute-start | bytes 4816904 | tf_op jit(solution)/shard_map/ppermute | solution.py:349
  40.8 19.3 %collective-permute-start.5 = (bf16[896,512]{1,0:T(8,128)(2,1)}, bf16[896,512]{1,0:T(8,128)(2,1)}, u32[]{:S(2)}, u32[]{:S(2)}) collective-permute-start(bf16[896,512]{1,0:T(8,128)(2,1)} %get-tuple-element.33.added_ref), channel_id=1, source_target_pairs={{16,80},{48,112},{64,0},{96,32},{17,81},{49,113},{65,1},{97,33},{1... | collective-permute-start | bytes 2752520 | tf_op jit(solution)/shard_map/ppermute | solution.py:342
  43.1 17.0 %collective-permute-start.6 = (bf16[896,384]{1,0:T(8,128)(2,1)}, bf16[896,384]{1,0:T(8,128)(2,1)}, u32[]{:S(2)}, u32[]{:S(2)}) collective-permute-start(bf16[896,384]{1,0:T(8,128)(2,1)} %get-tuple-element.38.added_ref), channel_id=1, source_target_pairs={{16,80},{48,112},{64,0},{96,32},{17,81},{49,113},{65,1},{97,33},{1... | collective-permute-start | bytes 2064392 | tf_op jit(solution)/shard_map/ppermute | solution.py:342
  48.9 1.1 copy-start.6
  50.1 1.2 copy-start.8
  67.0 86.5 %copy-start.9 = (bf16[896,896]{1,0:T(8,128)(2,1)S(1)}, bf16[896,896]{1,0:T(8,128)(2,1)}, u32[]{:S(2)}) copy-start(bf16[896,896]{1,0:T(8,128)(2,1)} %copy-done.8) | copy-start | bytes 4816900
  164.7 12.1 %collective-permute-start.8 = (bf16[896,512]{1,0:T(8,128)(2,1)S(1)}, bf16[896,512]{1,0:T(8,128)(2,1)S(1)}, u32[]{:S(2)}, u32[]{:S(2)}) collective-permute-start(bf16[896,512]{1,0:T(8,128)(2,1)S(1)} %get-tuple-element.51), channel_id=1, source_target_pairs={{0,16},{32,48},{80,64},{112,96},{1,17},{33,49},{81,65},{113,97},{2... | collective-permute-start | bytes 2752520 | tf_op jit(solution)/shard_map/ppermute | solution.py:365
  175.5 16.7 %collective-permute-start.10 = (bf16[896,384]{1,0:T(8,128)(2,1)S(1)}, bf16[896,384]{1,0:T(8,128)(2,1)S(1)}, u32[]{:S(2)}, u32[]{:S(2)}) collective-permute-start(bf16[896,384]{1,0:T(8,128)(2,1)S(1)} %get-tuple-element.45.refs_2_), channel_id=1, source_target_pairs={{0,16},{32,48},{80,64},{112,96},{1,17},{33,49},{81,65},{113,97},{2... | collective-permute-start | bytes 2064392 | tf_op jit(solution)/shard_map/ppermute | solution.py:365
  176.8 5.9 %copy-start.5 = (f32[896,512]{1,0:T(8,128)S(1)}, f32[896,512]{1,0:T(8,128)}, u32[]{:S(2)}) copy-start(f32[896,512]{1,0:T(8,128)} %copy-done.4) | copy-start | bytes 5505028
  176.8 5.9 %copy-start.7 = (bf16[896,896]{1,0:T(8,128)(2,1)S(1)}, bf16[896,896]{1,0:T(8,128)(2,1)}, u32[]{:S(2)}) copy-start(bf16[896,896]{1,0:T(8,128)(2,1)} %copy-done.6) | copy-start | bytes 4816900
  177.1 18.8 %collective-permute-start.9 = (bf16[896,512]{1,0:T(8,128)(2,1)S(1)}, bf16[896,512]{1,0:T(8,128)(2,1)S(1)}, u32[]{:S(2)}, u32[]{:S(2)}) collective-permute-start(bf16[896,512]{1,0:T(8,128)(2,1)S(1)} %add_convert_fusion.1), channel_id=1, source_target_pairs={{16,64},{48,96},{64,16},{96,48},{17,65},{49,97},{65,17},{97,49},{1... | collective-permute-start | bytes 2752520 | tf_op jit(solution)/shard_map/ppermute | solution.py:368
  192.1 3.9 %copy-start.11 = (f32[896,384]{1,0:T(8,128)S(1)}, f32[896,384]{1,0:T(8,128)}, u32[]{:S(2)}) copy-start(f32[896,384]{1,0:T(8,128)} %copy-done.10) | copy-start | bytes 4128772
  192.3 13.9 %collective-permute-start.11 = (bf16[896,384]{1,0:T(8,128)(2,1)S(1)}, bf16[896,384]{1,0:T(8,128)(2,1)S(1)}, u32[]{:S(2)}, u32[]{:S(2)}) collective-permute-start(bf16[896,384]{1,0:T(8,128)(2,1)S(1)} %add_convert_fusion.3), channel_id=1, source_target_pairs={{16,64},{48,96},{64,16},{96,48},{17,65},{49,97},{65,17},{97,49},{1... | collective-permute-start | bytes 2064392 | tf_op jit(solution)/shard_map/ppermute | solution.py:379
  194.4 13.2 %collective-permute-start.7 = (bf16[896,512]{1,0:T(8,128)(2,1)S(1)}, bf16[896,512]{1,0:T(8,128)(2,1)S(1)}, u32[]{:S(2)}, u32[]{:S(2)}) collective-permute-start(bf16[896,512]{1,0:T(8,128)(2,1)S(1)} %get-tuple-element.47), channel_id=1, source_target_pairs={{16,0},{48,32},{64,80},{96,112},{17,1},{49,33},{65,81},{97,113},{1... | collective-permute-start | bytes 2752520 | tf_op jit(solution)/shard_map/ppermute | solution.py:382
  206.2 3.0 %collective-permute-start.12 = (bf16[896,384]{1,0:T(8,128)(2,1)S(1)}, bf16[896,384]{1,0:T(8,128)(2,1)S(1)}, u32[]{:S(2)}, u32[]{:S(2)}) collective-permute-start(bf16[896,384]{1,0:T(8,128)(2,1)S(1)} %get-tuple-element.57), channel_id=1, source_target_pairs={{16,0},{48,32},{64,80},{96,112},{17,1},{49,33},{65,81},{97,113},{1... | collective-permute-start | bytes 2064392 | tf_op jit(solution)/shard_map/ppermute | solution.py:382

commit v5 on v4

v5 whole, which is shorter than its diff:
```python
import functools

import jax
import jax.numpy as jnp
from jax import lax
from jax.experimental import pallas as pl
from jax.experimental.pallas import tpu as pltpu
from jax.sharding import Mesh
from jax.sharding import PartitionSpec as P

TILE = 128
NVT = 32
DT = 7
DV = DT * TILE
NZ, NC, NX, NY = 4, 2, 4, 4
OWNERS = NX * NY
SLICE = TILE // OWNERS
CHIPS = NZ * OWNERS
AFTER = 3
CUT = 4
GROUP = 4
MIB = 1024 * 1024


def partner_perm(to_other_core):
    pairs = []
    for z in range(NZ):
        core = 1 - z // 2
        target = 1 - core if to_other_core else core
        pairs.append((z * NC + core, (z ^ 2) * NC + target))
    return pairs


def home_perm(from_home):
    pairs = [(z * NC + z // 2, z * NC + 1 - z // 2) for z in range(NZ)]
    return pairs if from_home else [(b, a) for a, b in pairs]


def core_swap(value):
    return lax.ppermute(value, "core", [(0, 1), (1, 0)])


def in_hbm(value):
    return pltpu.with_memory_space_constraint(value, pltpu.HBM)


def spread_kernel(chol_ref, out_ref, staged, in_sems, out_sems):
    arriving, leaving = [], []
    for m in range(OWNERS):
        for t in range(2):
            place = (m, t, slice(None), slice(0, NVT * TILE))
            arriving.append(
                pltpu.make_async_copy(
                    chol_ref.at[t * OWNERS + m], staged.at[m, t], in_sems.at[m, t]
                )
            )
            leaving.append(
                pltpu.make_async_copy(staged.at[m, t], out_ref.at[place], out_sems.at[m, t])
            )
    for copy in arriving:
        copy.start()
    for come, leave in zip(arriving, leaving):
        come.wait()
        leave.start()
    for copy in leaving:
        copy.wait()


def spread(chol):
    return pl.pallas_call(
        spread_kernel,
        out_shape=pltpu.HBM((OWNERS, 2, SLICE, (NVT + 1) * TILE), jnp.bfloat16),
        in_specs=[pl.BlockSpec(memory_space=pl.ANY)],
        out_specs=pl.BlockSpec(memory_space=pl.ANY),
        scratch_shapes=[
            pltpu.VMEM((OWNERS, 2, SLICE, NVT * TILE), jnp.bfloat16),
            pltpu.SemaphoreType.DMA((OWNERS, 2)),
            pltpu.SemaphoreType.DMA((OWNERS, 2)),
        ],
        compiler_params=pltpu.CompilerParams(vmem_limit_bytes=30 * MIB),
        cost_estimate=pl.CostEstimate(flops=0, bytes_accessed=4 * MIB, transcendentals=0),
    )(in_hbm(chol))


def table_kernel(table_ref, given_ref, out_ref, sems):
    del given_ref
    copies = []
    for m in range(OWNERS):
        for t in range(2):
            copies.append(
                pltpu.make_async_copy(
                    table_ref, out_ref.at[m, t, :, pl.ds(NVT * TILE, TILE)], sems.at[m, t]
                )
            )
    for copy in copies:
        copy.start()
    for copy in copies:
        copy.wait()


def with_table(spread_rows, table):
    anywhere = pl.BlockSpec(memory_space=pl.ANY)
    return pl.pallas_call(
        table_kernel,
        out_shape=pltpu.HBM(spread_rows.shape, jnp.bfloat16),
        in_specs=[pl.BlockSpec(memory_space=pltpu.VMEM), anywhere],
        out_specs=anywhere,
        scratch_shapes=[pltpu.SemaphoreType.DMA((OWNERS, 2))],
        input_output_aliases={1: 0},
        compiler_params=pltpu.CompilerParams(vmem_limit_bytes=8 * MIB),
    )(table, in_hbm(spread_rows))


def pack_kernel(given_ref, *refs):
    out_ref, rows_ref, given_tables, tables, tiles_ref, packed, row_sems, table_sems, sems = refs[AFTER:]
    beside = pltpu.make_async_copy(
        given_ref.at[:, :, pl.ds(NVT * TILE, TILE)], given_tables, table_sems.at[0]
    )
    beside.start()
    fetches = []
    for k in range(NVT // 4):
        part = pl.ds(k * 4, 4)
        fetches.append(
            pltpu.make_async_copy(
                given_ref.at[part, :, pl.ds(0, NVT * TILE)], rows_ref.at[part], row_sems.at[k]
            )
        )
    for fetch in fetches:
        fetch.start()
    beside.wait()
    for s in range(OWNERS):
        table = given_tables[2 * s].astype(jnp.float32).astype(jnp.int32)
        tables[s : s + 1, :] = table[0:1, :]
    move = pltpu.make_async_copy(tables, tiles_ref, table_sems.at[1])
    move.start()
    move.wait()
    for fetch in fetches:
        fetch.wait()

    def leave(group):
        dests = pl.ds(group * GROUP, GROUP)
        return pltpu.make_async_copy(packed.at[dests], out_ref.at[dests], sems.at[group])

    def one(group, carry):
        for k in range(GROUP):
            dest = group * GROUP + k
            z, s = dest // OWNERS, dest % OWNERS
            tiles = [tiles_ref[s, z * DT + t] for t in range(DT)]
            columns = [pl.multiple_of(tile * TILE, TILE) for tile in tiles]
            for i in range(DT):
                for j in range(DT):
                    packed[dest, i, :, j * TILE : (j + 1) * TILE] = rows_ref[
                        tiles[i], :, pl.ds(columns[j], TILE)
                    ]
        leave(group).start()
        return carry

    def gone(group, carry):
        leave(group).wait()
        return carry

    lax.fori_loop(0, CHIPS // GROUP, one, 0)
    lax.fori_loop(0, CHIPS // GROUP, gone, 0)


def pack(rows, *after):
    assert len(after) == AFTER
    shape = (CHIPS, DT, SLICE, DV)
    anywhere = pl.BlockSpec(memory_space=pl.ANY)
    return pl.pallas_call(
        pack_kernel,
        out_shape=pltpu.HBM(shape, jnp.bfloat16),
        in_specs=[anywhere] * (1 + AFTER),
        out_specs=anywhere,
        scratch_shapes=[
            pltpu.VMEM((NVT, SLICE, NVT * TILE), jnp.bfloat16),
            pltpu.VMEM((NVT, SLICE, TILE), jnp.bfloat16),
            pltpu.VMEM((OWNERS, TILE), jnp.int32),
            pltpu.SMEM((OWNERS, TILE), jnp.int32),
            pltpu.VMEM(shape, jnp.bfloat16),
            pltpu.SemaphoreType.DMA((NVT // 4,)),
            pltpu.SemaphoreType.DMA((2,)),
            pltpu.SemaphoreType.DMA((CHIPS // GROUP,)),
        ],
        compiler_params=pltpu.CompilerParams(vmem_limit_bytes=30 * MIB),
        cost_estimate=pl.CostEstimate(
            flops=0, bytes_accessed=4 * CHIPS * DT * SLICE * DV, transcendentals=0
        ),
    )(*map(in_hbm, (rows, *after)))


def cycle_kernel(
    amps_ref, exch_all_ref, exch_ref, row_ref, col_ref, after_ref, base_ref, turned_ref
):
    del after_ref
    cycle = jnp.dot(amps_ref[...], exch_all_ref[...], preferred_element_type=jnp.float32)
    cycle = cycle.astype(jnp.bfloat16).astype(jnp.float32)
    denominator = col_ref[...] + row_ref[...]
    base_ref[...] = (
        exch_ref[...].astype(jnp.float32)
        + denominator * amps_ref[...].astype(jnp.float32)
        + cycle
    )
    turned_ref[...] = cycle.T.astype(jnp.bfloat16)


def cycle_and_base(amps, exch, row, col, after):
    return pl.pallas_call(
        cycle_kernel,
        out_shape=(pltpu.HBM((DV, DV), jnp.float32), pltpu.HBM((DV, DV), jnp.bfloat16)),
        grid=(DT,),
        in_specs=[
            pl.BlockSpec((TILE, DV), lambda i: (i, 0)),
            pl.BlockSpec((DV, DV), lambda i: (0, 0)),
            pl.BlockSpec((TILE, DV), lambda i: (i, 0)),
            pl.BlockSpec((1, DV), lambda i: (0, 0)),
            pl.BlockSpec((TILE, 1), lambda i: (i, 0)),
            pl.BlockSpec(memory_space=pl.ANY),
        ],
        out_specs=(
            pl.BlockSpec((TILE, DV), lambda i: (i, 0)),
            pl.BlockSpec((DV, TILE), lambda i: (0, i)),
        ),
        compiler_params=pltpu.CompilerParams(vmem_limit_bytes=32 * MIB),
        cost_estimate=pl.CostEstimate(
            flops=2 * DV**3, bytes_accessed=14 * DV * DV, transcendentals=0
        ),
    )(amps, exch, exch, row, col, in_hbm(after))


def choose_kernel(home_ref, *refs):
    sources, targets, sems = (refs[:2], refs[2:4]), refs[4:6], refs[6]
    home = home_ref[0] > 0

    def copies(which):
        made = []
        for k in range(2):
            for i in range(DT):
                place = pl.ds(i * TILE, TILE)
                made.append(
                    pltpu.make_async_copy(
                        sources[which][k].at[place], targets[k].at[place], sems.at[k, i]
                    )
                )
        return made

    for which in range(2):

        @pl.when(home if which == 0 else jnp.logical_not(home))
        def _(which=which):
            made = copies(which)
            for copy in made:
                copy.start()
            for copy in made:
                copy.wait()


def choose(home, at_home, elsewhere):
    vmem = pl.BlockSpec(memory_space=pltpu.VMEM)
    return pl.pallas_call(
        choose_kernel,
        out_shape=[pltpu.VMEM((DV, DV), jnp.bfloat16)] * 2,
        in_specs=[pl.BlockSpec(memory_space=pltpu.SMEM)] + [pl.BlockSpec(memory_space=pl.ANY)] * 4,
        out_specs=[vmem, vmem],
        scratch_shapes=[pltpu.SemaphoreType.DMA((2, DT))],
        compiler_params=pltpu.CompilerParams(vmem_limit_bytes=8 * MIB),
        cost_estimate=pl.CostEstimate(flops=0, bytes_accessed=4 * DV * DV, transcendentals=0),
    )(home, *at_home, *elsewhere)


def ladder_kernel(raw, home, amps_ref, given_ref, added_ref, *refs):
    refs = list(refs)
    home_ref = refs.pop(0) if home else None
    refs.pop(0)
    kept_ref, sent_ref = refs.pop(0), refs.pop(0)
    rest_ref = refs.pop(0)
    block_ref = refs.pop(0) if raw else given_ref
    half, total = refs.pop(0), refs.pop(0)
    if raw:
        landed, sems = refs.pop(0), refs.pop(0)
        copies = [
            [
                pltpu.make_async_copy(given_ref.at[q, :, i], landed.at[q, i], sems.at[q, i])
                for i in range(DT)
            ]
            for q in range(NZ)
        ]
        for q in range(NZ):
            for copy in copies[q]:
                copy.start()
    for q in range(NZ):
        if raw:
            for i in range(DT):
                copies[q][i].wait()
                tile = landed[q, i].astype(jnp.float32).reshape(TILE, DV)
                block_ref[q, i * TILE : (i + 1) * TILE, :] = tile.astype(jnp.bfloat16)
        half[...] = lax.dot_general(
            amps_ref[...],
            block_ref[q],
            (((1,), (1,)), ((), ())),
            preferred_element_type=jnp.float32,
        ).astype(jnp.bfloat16)
        for i in range(DT):
            place = slice(i * TILE, (i + 1) * TILE)
            part = jnp.dot(
                block_ref[q, place, :], half[...], preferred_element_type=jnp.float32
            )
            if q > 0:
                part = part + total[place, :]
            if q < NZ - 1:
                total[place, :] = part
            else:
                if home:
                    keep = (home_ref[0] > 0).astype(jnp.float32)
                    kept_ref[place, :] = added_ref[place, :] + keep * part
                else:
                    kept_ref[place, :] = part
                    part = part + added_ref[place, :].astype(jnp.float32)
                if i < CUT:
                    sent_ref[place, :] = part.astype(jnp.bfloat16)
                else:
                    rest_ref[(i - CUT) * TILE : (i + 1 - CUT) * TILE, :] = part.astype(jnp.bfloat16)


def in_vmem(value):
    return pltpu.with_memory_space_constraint(value, pltpu.VMEM)


def ladder(amps, blocks, added, after, home=None):
    raw = blocks.ndim == 5
    vmem = pl.BlockSpec(memory_space=pltpu.VMEM)
    anywhere = pl.BlockSpec(memory_space=pl.ANY)
    scratch = [pltpu.VMEM((DV, DV), jnp.bfloat16), pltpu.VMEM((DV, DV), jnp.float32)]
    out_shape = [pltpu.VMEM((DV, DV), jnp.float32)]
    out_shape += [pltpu.VMEM((height, DV), jnp.bfloat16) for height in (CUT * TILE, DV - CUT * TILE)]
    if raw:
        out_shape.append(pltpu.VMEM((NZ, DV, DV), jnp.bfloat16))
        scratch += [
            pltpu.VMEM((NZ, DT, OWNERS, SLICE, DV), jnp.bfloat16),
            pltpu.SemaphoreType.DMA((NZ, DT)),
        ]
    operands = [in_vmem(amps), in_hbm(blocks) if raw else in_vmem(blocks), in_vmem(added)]
    specs = [vmem, anywhere if raw else vmem, vmem]
    if home is not None:
        operands.append(home)
        specs.append(pl.BlockSpec(memory_space=pltpu.SMEM))
    return pl.pallas_call(
        functools.partial(ladder_kernel, raw, home is not None),
        out_shape=out_shape,
        in_specs=specs + [anywhere],
        out_specs=[vmem] * len(out_shape),
        scratch_shapes=scratch,
        compiler_params=pltpu.CompilerParams(vmem_limit_bytes=16 * MIB),
        cost_estimate=pl.CostEstimate(
            flops=4 * NZ * DV**3, bytes_accessed=2 * NZ * DV * DV, transcendentals=0
        ),
    )(*operands, after)


def add_kernel(kept_ref, *refs):
    received, out_ref = refs[:2], refs[2]
    for i in range(DT):
        place = slice(i * TILE, (i + 1) * TILE)
        k, at = (0, i) if i < CUT else (1, i - CUT)
        came = received[k][at * TILE : (at + 1) * TILE, :].astype(jnp.float32)
        out_ref[place, :] = (kept_ref[place, :] + came).astype(jnp.bfloat16)


def add(kept, received):
    vmem = pl.BlockSpec(memory_space=pltpu.VMEM)
    return pl.pallas_call(
        add_kernel,
        out_shape=pltpu.VMEM((DV, DV), jnp.bfloat16),
        in_specs=[vmem] * 3,
        out_specs=vmem,
        compiler_params=pltpu.CompilerParams(vmem_limit_bytes=16 * MIB),
        cost_estimate=pl.CostEstimate(flops=DV * DV, bytes_accessed=DV * DV, transcendentals=0),
    )(*map(in_vmem, (kept, *received)))


def finish_kernel(kept_ref, partner_ref, returned_ref, *refs):
    received, out_ref = refs[:2], refs[2]
    for i in range(DT):
        place = slice(i * TILE, (i + 1) * TILE)
        k, at = (0, i) if i < CUT else (1, i - CUT)
        value = kept_ref[place, :] + received[k][at * TILE : (at + 1) * TILE, :].astype(jnp.float32)
        value = value + partner_ref[place, :].astype(jnp.float32)
        value = value + returned_ref[place, :].astype(jnp.float32)
        out_ref[place, :] = value.astype(jnp.bfloat16)


def finish(kept, partner_turned, returned, received):
    vmem = pl.BlockSpec(memory_space=pltpu.VMEM)
    return pl.pallas_call(
        finish_kernel,
        out_shape=jax.ShapeDtypeStruct((DV, DV), jnp.bfloat16),
        in_specs=[vmem] * 5,
        out_specs=vmem,
        compiler_params=pltpu.CompilerParams(vmem_limit_bytes=16 * MIB),
        cost_estimate=pl.CostEstimate(flops=DV * DV, bytes_accessed=DV * DV, transcendentals=0),
    )(*map(in_vmem, (kept, partner_turned, returned, *received)))


def local(amplitudes, exchange_ints, chol, domain, virt_energy, pair_energy):
    z = lax.axis_index("z")
    core = lax.axis_index("core")
    home = core == z // 2
    amps, exch = amplitudes[0], exchange_ints[0]
    column_group = ("z", "core")

    own = domain[0]
    flip_z = lambda pair: [(z * NC + c, (z ^ 1) * NC + (c ^ pair)) for z in range(NZ) for c in range(NC)]
    beside = lax.ppermute(own, column_group, flip_z(0))
    across = lax.ppermute(own, column_group, flip_z(1))
    swapped = core_swap(own)
    even, first_core = z % 2 == 0, core == 0
    mine = jnp.stack([jnp.where(even, own, beside), jnp.where(even, beside, own)])
    others = jnp.stack([jnp.where(even, swapped, across), jnp.where(even, across, swapped)])
    column = jnp.stack([jnp.where(first_core, mine, others), jnp.where(first_core, others, mine)])
    table = column.reshape(1, NZ * DT).astype(jnp.bfloat16)
    table = jnp.pad(table, ((0, SLICE - 1), (0, TILE - NZ * DT)))

    outgoing = with_table(spread(chol.reshape(2 * OWNERS, SLICE, NVT * TILE)), table)
    rows = lax.all_to_all(outgoing, ("x", "y"), 0, 0, tiled=True)
    rows = rows.reshape(NVT, SLICE, (NVT + 1) * TILE)

    early, _ = lax.optimization_barrier((amps, outgoing))
    moved = lax.ppermute(early, column_group, partner_perm(True))
    home_amps = lax.ppermute(early, column_group, home_perm(True))

    energies = jnp.take(virt_energy.reshape(NVT, TILE), own, axis=0).reshape(DV)
    base, turned = cycle_and_base(
        amps, exch, energies[None, :], (energies - pair_energy[0])[:, None], outgoing
    )

    moved, _ = lax.optimization_barrier((moved, turned))
    remote_amps = lax.ppermute(moved, column_group, home_perm(False))
    is_home = home.astype(jnp.int32)[None]
    home_amps, remote_amps = choose(is_home, (amps, remote_amps), (home_amps, moved))

    packed = pack(rows, home_amps, remote_amps, turned)
    arrived = lax.all_to_all(packed, ("z", "x", "y"), 0, 0, tiled=True)
    blocks = arrived.reshape(NZ, OWNERS, DT, SLICE, DV)

    turned_late, _ = lax.optimization_barrier((turned, arrived))
    partner_turned = lax.ppermute(turned_late, column_group, partner_perm(False))

    kept, *sent, blocks = ladder(remote_amps, blocks, turned, own)
    received = [lax.ppermute(part, column_group, home_perm(True)) for part in sent]
    kept, partner_turned = lax.optimization_barrier((kept, partner_turned))
    finished = add(kept, received)
    returned = lax.ppermute(finished, column_group, partner_perm(True))

    kept, *sent = ladder(home_amps, blocks, base, finished, is_home)
    received = [lax.ppermute(part, column_group, home_perm(False)) for part in sent]
    return finish(kept, partner_turned, returned, received)[None]


def solution(mesh):
    finer = Mesh(mesh.devices.reshape(NZ, NC, NX, NY), ("z", "core", "x", "y"))
    group, everywhere = ("z", "core"), ("z", "core", "x", "y")
    placed = (
        P(everywhere, None, None),
        P(everywhere, None, None),
        P(group, ("x", "y"), None),
        P(everywhere, None),
        P(),
        P(everywhere),
    )
    return jax.shard_map(
        local, mesh=finer, in_specs=placed, out_specs=P(everywhere, None, None), check_vma=False
    )
```

time: 212 us -> 196 us (0.925)
  Pallas kernels: 60.4 us -> 54.8 us
  starting transfers between devices: 39.1 us -> 34.6 us
  blocking collectives: 86.5 us -> 82.5 us
  other arithmetic: 3.17 us -> 0.13 us
    ppermute x10 -> x9, waiting for transfers between devices: 12.1 us -> 4.49 us  [the longest x2 2.76 us: local(): lax.ppermute(part, column_group, home_perm(True))]
    all_to_all x1, waiting for transfers between devices: 0.01 us -> 5.1 us  [local(): rows = lax.all_to_all(outgoing, ('x', 'y'), 0, 0, tiled=True)]
    all_to_all x1, blocking collectives: 86.5 us -> 82.5 us  [local(): arrived = lax.all_to_all(packed, ('z', 'x', 'y'), 0, 0, tiled=True)]
    pallas_call x7 -> x8, Pallas kernels: 56.8 us -> 52.7 us  [the longest x2 34.2 us: ladder(): pl.pallas_call(functools.partial(ladder_kernel, raw, home is not None), o...]
    ppermute x10 -> x9, starting transfers between devices: 21.5 us -> 17.6 us  [the longest x1 6.7 us: local(): returned = lax.ppermute(finished, column_group, partner_perm(True))]
    ppermute x1, waiting for transfers between devices: 0.01 us -> 3.14 us  [local(): remote_amps = lax.ppermute(moved, column_group, home_perm(False))]
    unnamed x26 -> x28, local copies, waits for them, and re-layouts: 6.36 us -> 7.37 us
  transfers between devices with their start and end apart: 14 -> 13, of which waited for: 5 -> 5; matrix products, arithmetic and copies ran while one was open for 1% -> 1% of each run, Pallas kernels for 18% -> 23%
where the time goes in v5:
time: 196 us
  blocking collectives  82.5 us (42%)
  Pallas kernels  54.8 us (28%)
  starting transfers between devices  34.6 us (18%)
  waiting for transfers between devices  14.6 us (7%)
  local copies, waits for them, and re-layouts  8.02 us (4%)
    all_to_all x1, blocking collectives, local(): arrived = lax.all_to_all(packed, ('z', 'x', 'y'), 0, 0, tiled=True)  82.5 us
    pallas_call x2, Pallas kernels, ladder(): pl.pallas_call(functools.partial(ladder_kernel, raw, home is not None), o...  34.2 us
    unnamed x28, local copies, waits for them, and re-layouts  7.37 us
    pallas_call x1, Pallas kernels, pack(): pl.pallas_call(pack_kernel, out_shape=pltpu.HBM(shape, jnp.bfloat16), in_...  7.23 us
    all_to_all x1, starting transfers between devices, local(): rows = lax.all_to_all(outgoing, ('x', 'y'), 0, 0, tiled=True)  6.94 us
    ppermute x1, starting transfers between devices, local(): returned = lax.ppermute(finished, column_group, partner_perm(True))  6.7 us
    ppermute x1, starting transfers between devices, local(): moved = lax.ppermute(early, column_group, partner_perm(True))  6.27 us
    pallas_call x1, Pallas kernels, cycle_and_base(): pl.pallas_call(cycle_kernel, out_shape=(pltpu.HBM((DV, DV), jnp.float32),...  5.38 us
  transfers between devices with their start and end apart: 13, of which 5 were waited for; matrix products, arithmetic and copies ran while one was open for 1% of the time, Pallas kernels for 23%

profile of v5, /device:TPU:1, one launch (start us, length us, event | category | flops | bytes accessed | tf_op | source)
XLA Modules:
  0.0 195.6 jit_solution(8896261059593357170)
XLA Ops:
  0.0 1.4 collective-permute-start.1
  1.4 1.7 collective-permute-start.2
  3.2 2.8 %shard_map.64.given_ref = bf16[16,2,8,4224]{3,2,1,0:T(8,128)(2,1)} custom-call(bf16[32,8,4096]{2,1,0:T(8,128)(2,1)} %bitcast.50), custom_call_target="tpu_custom_call" | custom-call | bytes 4194304 | tf_op jit(solution)/shard_map/pallas_call | solution.py:70
  6.2 1.0 shard_map.65.after_ref
  7.7 6.3 %collective-permute-start.3 = (bf16[896,896]{1,0:T(8,128)(2,1)S(1)}, bf16[896,896]{1,0:T(8,128)(2,1)}, u32[]{:S(2)}, u32[]{:S(2)}) collective-permute-start(bf16[896,896]{1,0:T(8,128)(2,1)S(1)} %bitcast.40), channel_id=1, source_target_pairs={{16,64},{48,96},{64,16},{96,48},{17,65},{49,97},{65,17},{97,49},{1... | collective-permute-start | bytes 4816904 | tf_op jit(solution)/shard_map/ppermute | solution.py:428
  15.2 6.9 %all-to-all-start = ((bf16[16,2,8,4224]{3,2,1,0:T(8,128)(2,1)}), bf16[16,2,8,4224]{3,2,1,0:T(8,128)(2,1)}, u32[]{:S(2)}, u32[]{:S(2)}) async-start(bf16[16,2,8,4224]{3,2,1,0:T(8,128)(2,1)} %shard_map.65.after_ref), calls=%async_computation | async-start | bytes 4325376 | tf_op jit(solution)/shard_map/all_to_all | solution.py:424
  22.3 1.0 copy.11
  23.2 1.3 collective-permute-start.5
  24.6 1.0 copy-done.3
  25.6 5.4 %shard_map.66 = (f32[896,896]{1,0:T(8,128)}, bf16[896,896]{1,0:T(8,128)(2,1)}) custom-call(bf16[896,896]{1,0:T(8,128)(2,1)S(1)} %bitcast.42, bf16[896,896]{1,0:T(8,128)(2,1)S(1)} %bitcast.38, bf16[896,896]{1,0:T(8,128)(2,1)S(1)} %bitcast.39, f32[1,896]{1,0:T(1,128)S(1)} %get-tuple-element.46.row_ref, f32[896,1]{1,0:T(8,128)S(1)} %bitcast.44, ...), custom_call_target="tpu_custom_call" | custom-call | flops 1438646272 | bytes 11239424 | tf_op jit(solution)/shard_map/pallas_call | solution.py:208
  30.9 1.8 collective-permute-done.3.refs_3_
  32.8 2.4 %collective-permute-start.4 = (bf16[896,896]{1,0:T(8,128)(2,1)}, bf16[896,896]{1,0:T(8,128)(2,1)S(1)}, u32[]{:S(2)}, u32[]{:S(2)}) collective-permute-start(bf16[896,896]{1,0:T(8,128)(2,1)} %collective-permute-done.3.refs_3_), channel_id=1, source_target_pairs={{16,0},{48,32},{64,80},{96,112},{17,1},{49,33},{65,81},{97,113},{1... | collective-permute-start | bytes 4816904 | tf_op jit(solution)/shard_map/ppermute | solution.py:437
  35.3 3.1 %collective-permute-done.4.refs_1_ = bf16[896,896]{1,0:T(8,128)(2,1)S(1)} collective-permute-done((bf16[896,896]{1,0:T(8,128)(2,1)}, bf16[896,896]{1,0:T(8,128)(2,1)S(1)}, u32[]{:S(2)}, u32[]{:S(2)}) %collective-permute-start.4) | collective-permute-done | bytes 1605664 | tf_op jit(solution)/shard_map/ppermute | solution.py:437
  38.4 1.2 copy-done.9
  39.6 1.4 copy-done.10
  41.0 2.1 %shard_map.67 = (bf16[896,896]{1,0:T(8,128)(2,1)S(1)}, bf16[896,896]{1,0:T(8,128)(2,1)S(1)}) custom-call(s32[1]{0:T(128)} %bitcast.home_ref.refs_0_, bf16[896,896]{1,0:T(8,128)(2,1)S(1)} %bitcast.43, bf16[896,896]{1,0:T(8,128)(2,1)S(1)} %copy-done.10, bf16[896,896]{1,0:T(8,128)(2,1)} %collective-permute-done.5.refs_2_, ...), custom_call_target="tpu_custom_call" | custom-call | bytes 3211264 | tf_op jit(solution)/shard_map/pallas_call | solution.py:260
  43.1 1.1 copy-done.5
  44.2 1.2 copy-done.7
  45.4 5.1 %all-to-all-done = bf16[16,2,8,4224]{3,2,1,0:T(8,128)(2,1)} async-done(((bf16[16,2,8,4224]{3,2,1,0:T(8,128)(2,1)}), bf16[16,2,8,4224]{3,2,1,0:T(8,128)(2,1)}, u32[]{:S(2)}, u32[]{:S(2)}) %all-to-all-start) | async-done | bytes 2162720 | tf_op jit(solution)/shard_map/all_to_all | solution.py:424
  50.5 7.2 %shard_map.68 = bf16[64,7,8,896]{3,2,1,0:T(8,128)(2,1)} custom-call(bf16[32,8,4224]{2,1,0:T(8,128)(2,1)} %bitcast.13.given_ref, bf16[896,896]{1,0:T(8,128)(2,1)} %copy-done.5, bf16[896,896]{1,0:T(8,128)(2,1)} %copy-done.7, bf16[896,896]{1,0:T(8,128)(2,1)} %get-tuple-element.29.refs_2_.added_ref), custom_call_target="tpu_custom_call" | custom-call | bytes 12845056 | tf_op jit(solution)/shard_map/pallas_call | solution.py:170
  57.7 82.5 %all_to_all.10 = bf16[64,7,8,896]{3,2,1,0:T(8,128)(2,1)} all-to-all(bf16[64,7,8,896]{3,2,1,0:T(8,128)(2,1)} %shard_map.68), channel_id=1, replica_groups=mesh['z'=4,'core'=2,'x'=4,'y'=4] {'z','x','y'}, dimensions={0} | all-to-all | bytes 12845056 | tf_op jit(solution)/shard_map/all_to_all | solution.py:442
  140.2 2.6 %collective-permute-start.6 = (bf16[896,896]{1,0:T(8,128)(2,1)S(1)}, bf16[896,896]{1,0:T(8,128)(2,1)S(1)}, u32[]{:S(2)}, u32[]{:S(2)}) collective-permute-start(bf16[896,896]{1,0:T(8,128)(2,1)S(1)} %copy-done.4), channel_id=1, source_target_pairs={{16,80},{48,112},{64,0},{96,32},{17,81},{49,113},{65,1},{97,33},{1... | collective-permute-start | bytes 4816904 | tf_op jit(solution)/shard_map/ppermute | solution.py:446
  142.8 18.4 %shard_map.69 = (f32[896,896]{1,0:T(8,128)S(1)}, bf16[512,896]{1,0:T(8,128)(2,1)S(1)}, bf16[384,896]{1,0:T(8,128)(2,1)S(1)}, bf16[4,896,896]{2,1,0:T(8,128)(2,1)S(1)}) custom-call(bf16[896,896]{1,0:T(8,128)(2,1)S(1)} %copy-done.8, bf16[4,16,7,8,896]{4,3,2,1,0:T(8,128)(2,1)} %bitcast.49, bf16[896,896]{1,0:T(8,128)(2,1)S(1)} %copy-done.4, s32[7]{0:T(128)S(1)} %bitcast.48), custom_call_target="tpu_custom_call" | custom-call | flops 11509170176 | bytes 6422528 | tf_op jit(solution)/shard_map/pallas_call | solution.py:347
  161.2 1.3 collective-permute-start.7
  162.5 1.3 collective-permute-start.8
  163.8 2.8 %collective-permute-done.8.refs_1_ = bf16[384,896]{1,0:T(8,128)(2,1)S(1)} collective-permute-done((bf16[384,896]{1,0:T(8,128)(2,1)S(1)}, bf16[384,896]{1,0:T(8,128)(2,1)S(1)}, u32[]{:S(2)}, u32[]{:S(2)}) %collective-permute-start.8) | collective-permute-done | bytes 688160 | tf_op jit(solution)/shard_map/ppermute | solution.py:449
  166.8 6.7 %collective-permute-start.9 = (bf16[896,896]{1,0:T(8,128)(2,1)S(1)}, bf16[896,896]{1,0:T(8,128)(2,1)S(1)}, u32[]{:S(2)}, u32[]{:S(2)}) collective-permute-start(bf16[896,896]{1,0:T(8,128)(2,1)S(1)} %shard_map.70.refs_1_), channel_id=1, source_target_pairs={{16,64},{48,96},{64,16},{96,48},{17,65},{49,97},{65,17},{97,49},{1... | collective-permute-start | bytes 4816904 | tf_op jit(solution)/shard_map/ppermute | solution.py:452
  173.5 15.8 %shard_map.71 = (f32[896,896]{1,0:T(8,128)S(1)}, bf16[512,896]{1,0:T(8,128)(2,1)S(1)}, bf16[384,896]{1,0:T(8,128)(2,1)S(1)}) custom-call(bf16[896,896]{1,0:T(8,128)(2,1)S(1)} %copy-done.6, bf16[4,896,896]{2,1,0:T(8,128)(2,1)S(1)} %get-tuple-element.26.given_ref, f32[896,896]{1,0:T(8,128)S(1)} %copy-done.12, s32[1]{0:T(128)} %bitcast.home_ref.refs_0_, ...), custom_call_target="tpu_custom_call" | custom-call | flops 11509170176 | bytes 6422528 | tf_op jit(solution)/shard_map/pallas_call | solution.py:347
  189.4 1.3 collective-permute-start.10
  190.7 1.3 collective-permute-start.11
  192.1 1.7 collective-permute-done.11.refs_1_
  193.8 1.8 shard_map.72
  (43 shorter events, 1.6 us)
Async XLA Ops:
  0.0 14.6 %copy-start = (f32[4096]{0:T(1024)S(1)}, f32[4096]{0:T(1024)}, u32[]{:S(2)}) copy-start(f32[4096]{0:T(1024)} %param.10) | copy-start | bytes 49156
  0.0 6.0 %collective-permute-start.1 = (s32[7]{0:T(128)}, s32[7]{0:T(128)S(1)}, u32[]{:S(2)}, u32[]{:S(2)}) collective-permute-start(s32[7]{0:T(128)} %bitcast.45), channel_id=1, source_target_pairs={{0,16},{16,0},{1,17},{17,1},{2,18},{18,2},{3,19},{19,3},{4,20},{20... | collective-permute-start | bytes 92 | tf_op jit(solution)/shard_map/ppermute | solution.py:40
  1.4 4.6 %collective-permute-start.2 = (s32[7]{0:T(128)}, s32[7]{0:T(128)S(1)}, u32[]{:S(2)}, u32[]{:S(2)}) collective-permute-start(s32[7]{0:T(128)} %bitcast.46), channel_id=1, source_target_pairs={{0,48},{16,32},{32,16},{48,0},{64,112},{80,96},{96,80},{112,64},{1... | collective-permute-start | bytes 92 | tf_op jit(solution)/shard_map/ppermute | solution.py:414
  3.1 2.9 %collective-permute-start = (s32[7]{0:T(128)}, s32[7]{0:T(128)S(1)}, u32[]{:S(2)}, u32[]{:S(2)}) collective-permute-start(s32[7]{0:T(128)} %bitcast.47), channel_id=1, source_target_pairs={{0,32},{16,48},{32,0},{48,16},{64,96},{80,112},{96,64},{112,80},{1... | collective-permute-start | bytes 92 | tf_op jit(solution)/shard_map/ppermute | solution.py:413
  3.2 2.8 %copy-start.11 = (s32[1,7]{1,0:T(1,128)S(1)}, s32[1,7]{1,0:T(1,128)}, u32[]{:S(2)}) copy-start(s32[1,7]{1,0:T(1,128)} %param.9) | copy-start | bytes 88
  6.2 1.5 copy-start.2
  7.7 25.1 %collective-permute-start.3 = (bf16[896,896]{1,0:T(8,128)(2,1)S(1)}, bf16[896,896]{1,0:T(8,128)(2,1)}, u32[]{:S(2)}, u32[]{:S(2)}) collective-permute-start(bf16[896,896]{1,0:T(8,128)(2,1)S(1)} %bitcast.40), channel_id=1, source_target_pairs={{16,64},{48,96},{64,16},{96,48},{17,65},{49,97},{65,17},{97,49},{1... | collective-permute-start | bytes 4816904 | tf_op jit(solution)/shard_map/ppermute | solution.py:428
  15.2 9.3 %copy-start.1 = (bf16[1,896,896]{2,1,0:T(8,128)(2,1)S(1)}, bf16[1,896,896]{2,1,0:T(8,128)(2,1)}, u32[]{:S(2)}) copy-start(bf16[1,896,896]{2,1,0:T(8,128)(2,1)} %param.7) | copy-start | bytes 4816900
  15.2 35.3 %all-to-all-start = ((bf16[16,2,8,4224]{3,2,1,0:T(8,128)(2,1)}), bf16[16,2,8,4224]{3,2,1,0:T(8,128)(2,1)}, u32[]{:S(2)}, u32[]{:S(2)}) async-start(bf16[16,2,8,4224]{3,2,1,0:T(8,128)(2,1)} %shard_map.65.after_ref), calls=%async_computation | async-start | bytes 4325376 | tf_op jit(solution)/shard_map/all_to_all | solution.py:424
  23.2 12.0 %collective-permute-start.5 = (bf16[896,896]{1,0:T(8,128)(2,1)S(1)}, bf16[896,896]{1,0:T(8,128)(2,1)}, u32[]{:S(2)}, u32[]{:S(2)}) collective-permute-start(bf16[896,896]{1,0:T(8,128)(2,1)S(1)} %bitcast.41), channel_id=1, source_target_pairs={{0,16},{32,48},{80,64},{112,96},{1,17},{33,49},{81,65},{113,97},{2... | collective-permute-start | bytes 4816904 | tf_op jit(solution)/shard_map/ppermute | solution.py:429
  24.5 1.0 copy-start.3
  32.8 5.6 %collective-permute-start.4 = (bf16[896,896]{1,0:T(8,128)(2,1)}, bf16[896,896]{1,0:T(8,128)(2,1)S(1)}, u32[]{:S(2)}, u32[]{:S(2)}) collective-permute-start(bf16[896,896]{1,0:T(8,128)(2,1)} %collective-permute-done.3.refs_3_), channel_id=1, source_target_pairs={{16,0},{48,32},{64,80},{96,112},{17,1},{49,33},{65,81},{97,113},{1... | collective-permute-start | bytes 4816904 | tf_op jit(solution)/shard_map/ppermute | solution.py:437
  38.4 1.2 copy-start.9
  39.6 1.4 copy-start.10
  43.1 1.2 copy-start.5
  44.2 1.2 copy-start.7
  57.7 82.5 %copy-start.4 = (bf16[896,896]{1,0:T(8,128)(2,1)S(1)}, bf16[896,896]{1,0:T(8,128)(2,1)}, u32[]{:S(2)}) copy-start(bf16[896,896]{1,0:T(8,128)(2,1)} %get-tuple-element.29.refs_2_.added_ref) | copy-start | bytes 4816900
  57.7 85.0 %copy-start.8 = (bf16[896,896]{1,0:T(8,128)(2,1)S(1)}, bf16[896,896]{1,0:T(8,128)(2,1)}, u32[]{:S(2)}) copy-start(bf16[896,896]{1,0:T(8,128)(2,1)} %copy-done.7) | copy-start | bytes 4816900
  140.2 23.6 %collective-permute-start.6 = (bf16[896,896]{1,0:T(8,128)(2,1)S(1)}, bf16[896,896]{1,0:T(8,128)(2,1)S(1)}, u32[]{:S(2)}, u32[]{:S(2)}) collective-permute-start(bf16[896,896]{1,0:T(8,128)(2,1)S(1)} %copy-done.4), channel_id=1, source_target_pairs={{16,80},{48,112},{64,0},{96,32},{17,81},{49,113},{65,1},{97,33},{1... | collective-permute-start | bytes 4816904 | tf_op jit(solution)/shard_map/ppermute | solution.py:446
  161.2 5.4 %collective-permute-start.7 = (bf16[512,896]{1,0:T(8,128)(2,1)S(1)}, bf16[512,896]{1,0:T(8,128)(2,1)S(1)}, u32[]{:S(2)}, u32[]{:S(2)}) collective-permute-start(bf16[512,896]{1,0:T(8,128)(2,1)S(1)} %get-tuple-element.31), channel_id=1, source_target_pairs={{0,16},{32,48},{80,64},{112,96},{1,17},{33,49},{81,65},{113,97},{2... | collective-permute-start | bytes 2752520 | tf_op jit(solution)/shard_map/ppermute | solution.py:449
  162.5 4.1 %collective-permute-start.8 = (bf16[384,896]{1,0:T(8,128)(2,1)S(1)}, bf16[384,896]{1,0:T(8,128)(2,1)S(1)}, u32[]{:S(2)}, u32[]{:S(2)}) collective-permute-start(bf16[384,896]{1,0:T(8,128)(2,1)S(1)} %get-tuple-element.32), channel_id=1, source_target_pairs={{0,16},{32,48},{80,64},{112,96},{1,17},{33,49},{81,65},{113,97},{2... | collective-permute-start | bytes 2064392 | tf_op jit(solution)/shard_map/ppermute | solution.py:449
  163.8 9.8 %copy-start.6 = (bf16[896,896]{1,0:T(8,128)(2,1)S(1)}, bf16[896,896]{1,0:T(8,128)(2,1)}, u32[]{:S(2)}) copy-start(bf16[896,896]{1,0:T(8,128)(2,1)} %copy-done.5) | copy-start | bytes 4816900
  163.8 9.8 %copy-start.12 = (f32[896,896]{1,0:T(8,128)S(1)}, f32[896,896]{1,0:T(8,128)}, u32[]{:S(2)}) copy-start(f32[896,896]{1,0:T(8,128)} %get-tuple-element.27.added_ref) | copy-start | bytes 9633796
  166.8 27.0 %collective-permute-start.9 = (bf16[896,896]{1,0:T(8,128)(2,1)S(1)}, bf16[896,896]{1,0:T(8,128)(2,1)S(1)}, u32[]{:S(2)}, u32[]{:S(2)}) collective-permute-start(bf16[896,896]{1,0:T(8,128)(2,1)S(1)} %shard_map.70.refs_1_), channel_id=1, source_target_pairs={{16,64},{48,96},{64,16},{96,48},{17,65},{49,97},{65,17},{97,49},{1... | collective-permute-start | bytes 4816904 | tf_op jit(solution)/shard_map/ppermute | solution.py:452
  189.4 4.4 %collective-permute-start.10 = (bf16[512,896]{1,0:T(8,128)(2,1)S(1)}, bf16[512,896]{1,0:T(8,128)(2,1)S(1)}, u32[]{:S(2)}, u32[]{:S(2)}) collective-permute-start(bf16[512,896]{1,0:T(8,128)(2,1)S(1)} %get-tuple-element.35), channel_id=1, source_target_pairs={{16,0},{48,32},{64,80},{96,112},{17,1},{49,33},{65,81},{97,113},{1... | collective-permute-start | bytes 2752520 | tf_op jit(solution)/shard_map/ppermute | solution.py:455
  190.7 3.1 %collective-permute-start.11 = (bf16[384,896]{1,0:T(8,128)(2,1)S(1)}, bf16[384,896]{1,0:T(8,128)(2,1)S(1)}, u32[]{:S(2)}, u32[]{:S(2)}) collective-permute-start(bf16[384,896]{1,0:T(8,128)(2,1)S(1)} %get-tuple-element.36), channel_id=1, source_target_pairs={{16,0},{48,32},{64,80},{96,112},{17,1},{49,33},{65,81},{97,113},{1... | collective-permute-start | bytes 2064392 | tf_op jit(solution)/shard_map/ppermute | solution.py:455

commit v6 on v5

--- a/solution.py
+++ b/solution.py
@@ -18,6 +18,7 @@
 CHIPS = NZ * OWNERS
 AFTER = 3
 CUT = 4
+BEGIN = 1
 GROUP = 4
 MIB = 1024 * 1024
 
@@ -268,114 +269,147 @@
     )(home, *at_home, *elsewhere)
 
 
-def ladder_kernel(raw, home, amps_ref, given_ref, added_ref, *refs):
-    refs = list(refs)
-    home_ref = refs.pop(0) if home else None
-    refs.pop(0)
-    kept_ref, sent_ref = refs.pop(0), refs.pop(0)
-    rest_ref = refs.pop(0)
-    block_ref = refs.pop(0) if raw else given_ref
-    half, total = refs.pop(0), refs.pop(0)
-    if raw:
-        landed, sems = refs.pop(0), refs.pop(0)
-        copies = [
-            [
-                pltpu.make_async_copy(given_ref.at[q, :, i], landed.at[q, i], sems.at[q, i])
-                for i in range(DT)
-            ]
-            for q in range(NZ)
-        ]
-        for q in range(NZ):
-            for copy in copies[q]:
-                copy.start()
-    for q in range(NZ):
-        if raw:
-            for i in range(DT):
-                copies[q][i].wait()
-                tile = landed[q, i].astype(jnp.float32).reshape(TILE, DV)
-                block_ref[q, i * TILE : (i + 1) * TILE, :] = tile.astype(jnp.bfloat16)
+def ladder_products(vectors, amps_ref, block_ref, half, total, so_far, ready, give):
+    ready(vectors[0])
+    for q in vectors:
         half[...] = lax.dot_general(
             amps_ref[...],
             block_ref[q],
             (((1,), (1,)), ((), ())),
             preferred_element_type=jnp.float32,
         ).astype(jnp.bfloat16)
+        if q < vectors[-1]:
+            ready(q + 1)
         for i in range(DT):
             place = slice(i * TILE, (i + 1) * TILE)
             part = jnp.dot(
                 block_ref[q, place, :], half[...], preferred_element_type=jnp.float32
             )
-            if q > 0:
+            if q > vectors[0]:
                 part = part + total[place, :]
-            if q < NZ - 1:
+            elif so_far is not None:
+                part = part + so_far[place, :]
+            if q < vectors[-1]:
                 total[place, :] = part
             else:
-                if home:
-                    keep = (home_ref[0] > 0).astype(jnp.float32)
-                    kept_ref[place, :] = added_ref[place, :] + keep * part
-                else:
-                    kept_ref[place, :] = part
-                    part = part + added_ref[place, :].astype(jnp.float32)
-                if i < CUT:
-                    sent_ref[place, :] = part.astype(jnp.bfloat16)
-                else:
-                    rest_ref[(i - CUT) * TILE : (i + 1 - CUT) * TILE, :] = part.astype(jnp.bfloat16)
+                give(i, place, part)
+
+
+def put(part, i, first_ref, second_ref):
+    target, at = (first_ref, i) if i < CUT else (second_ref, i - CUT)
+    target[at * TILE : (at + 1) * TILE, :] = part.astype(jnp.bfloat16)
+
+
+def remote_kernel(amps_ref, given_ref, added_ref, *refs):
+    kept_ref, sent_ref, block_ref, half, total, landed, sems = refs
+    copies = [
+        [
+            pltpu.make_async_copy(given_ref.at[q, :, i], landed.at[q, i], sems.at[q, i])
+            for i in range(DT)
+        ]
+        for q in range(NZ)
+    ]
+    for q in range(NZ):
+        for copy in copies[q]:
+            copy.start()
+
+    def ready(q):
+        for copy in copies[q]:
+            copy.wait()
+        for i in range(DT):
+            tile = landed[q, i].astype(jnp.float32).reshape(TILE, DV)
+            block_ref[q, i * TILE : (i + 1) * TILE, :] = tile.astype(jnp.bfloat16)
+
+    def give(i, place, part):
+        kept_ref[place, :] = part
+        sent_ref[place, :] = (part + added_ref[place, :].astype(jnp.float32)).astype(jnp.bfloat16)
+
+    ladder_products(range(NZ), amps_ref, block_ref, half, total, None, ready, give)
+
+
+def begin_kernel(amps_ref, block_ref, total_ref, half):
+    def give(i, place, part):
+        total_ref[place, :] = part
+
+    ladder_products(range(BEGIN), amps_ref, block_ref, half, total_ref, None, lambda q: None, give)
+
+
+def home_kernel(home_ref, amps_ref, block_ref, so_far_ref, added_ref, after_ref, *refs):
+    del after_ref
+    kept_ref, first_ref, second_ref, half, total = refs
+    keep = (home_ref[0] > 0).astype(jnp.float32)
+
+    def give(i, place, part):
+        kept_ref[place, :] = added_ref[place, :] + keep * part
+        put(part, i, first_ref, second_ref)
+
+    ladder_products(
+        range(BEGIN, NZ), amps_ref, block_ref, half, total, so_far_ref, lambda q: None, give
+    )
 
 
 def in_vmem(value):
     return pltpu.with_memory_space_constraint(value, pltpu.VMEM)
 
 
-def ladder(amps, blocks, added, after, home=None):
-    raw = blocks.ndim == 5
-    vmem = pl.BlockSpec(memory_space=pltpu.VMEM)
-    anywhere = pl.BlockSpec(memory_space=pl.ANY)
-    scratch = [pltpu.VMEM((DV, DV), jnp.bfloat16), pltpu.VMEM((DV, DV), jnp.float32)]
-    out_shape = [pltpu.VMEM((DV, DV), jnp.float32)]
-    out_shape += [pltpu.VMEM((height, DV), jnp.bfloat16) for height in (CUT * TILE, DV - CUT * TILE)]
-    if raw:
-        out_shape.append(pltpu.VMEM((NZ, DV, DV), jnp.bfloat16))
-        scratch += [
+def ladder_cost(vectors):
+    return pl.CostEstimate(
+        flops=4 * vectors * DV**3, bytes_accessed=2 * vectors * DV * DV, transcendentals=0
+    )
+
+
+def remote_ladder(amps, arrived, turned):
+    vmem, anywhere = pl.BlockSpec(memory_space=pltpu.VMEM), pl.BlockSpec(memory_space=pl.ANY)
+    out_shape = [
+        pltpu.VMEM((DV, DV), jnp.float32),
+        pltpu.VMEM((DV, DV), jnp.bfloat16),
+        pltpu.VMEM((NZ, DV, DV), jnp.bfloat16),
+    ]
+    return pl.pallas_call(
+        remote_kernel,
+        out_shape=out_shape,
+        in_specs=[vmem, anywhere, vmem],
+        out_specs=[vmem] * len(out_shape),
+        scratch_shapes=[
+            pltpu.VMEM((DV, DV), jnp.bfloat16),
+            pltpu.VMEM((DV, DV), jnp.float32),
             pltpu.VMEM((NZ, DT, OWNERS, SLICE, DV), jnp.bfloat16),
             pltpu.SemaphoreType.DMA((NZ, DT)),
-        ]
-    operands = [in_vmem(amps), in_hbm(blocks) if raw else in_vmem(blocks), in_vmem(added)]
-    specs = [vmem, anywhere if raw else vmem, vmem]
-    if home is not None:
-        operands.append(home)
-        specs.append(pl.BlockSpec(memory_space=pltpu.SMEM))
-    return pl.pallas_call(
-        functools.partial(ladder_kernel, raw, home is not None),
+        ],
+        compiler_params=pltpu.CompilerParams(vmem_limit_bytes=16 * MIB),
+        cost_estimate=ladder_cost(NZ),
+    )(in_vmem(amps), in_hbm(arrived), in_vmem(turned))
+
+
+def begin_ladder(amps, blocks):
+    vmem = pl.BlockSpec(memory_space=pltpu.VMEM)
+    return pl.pallas_call(
+        begin_kernel,
+        out_shape=pltpu.VMEM((DV, DV), jnp.float32),
+        in_specs=[vmem] * 2,
+        out_specs=vmem,
+        scratch_shapes=[pltpu.VMEM((DV, DV), jnp.bfloat16)],
+        compiler_params=pltpu.CompilerParams(vmem_limit_bytes=16 * MIB),
+        cost_estimate=ladder_cost(BEGIN),
+    )(in_vmem(amps), in_vmem(blocks))
+
+
+def home_ladder(home, amps, blocks, so_far, base, after):
+    vmem, anywhere = pl.BlockSpec(memory_space=pltpu.VMEM), pl.BlockSpec(memory_space=pl.ANY)
+    out_shape = [
+        pltpu.VMEM((DV, DV), jnp.float32),
+        pltpu.VMEM((CUT * TILE, DV), jnp.bfloat16),
+        pltpu.VMEM((DV - CUT * TILE, DV), jnp.bfloat16),
+    ]
+    return pl.pallas_call(
+        home_kernel,
         out_shape=out_shape,
-        in_specs=specs + [anywhere],
+        in_specs=[pl.BlockSpec(memory_space=pltpu.SMEM)] + [vmem] * 4 + [anywhere],
         out_specs=[vmem] * len(out_shape),
-        scratch_shapes=scratch,
+        scratch_shapes=[pltpu.VMEM((DV, DV), jnp.bfloat16), pltpu.VMEM((DV, DV), jnp.float32)],
         compiler_params=pltpu.CompilerParams(vmem_limit_bytes=16 * MIB),
-        cost_estimate=pl.CostEstimate(
-            flops=4 * NZ * DV**3, bytes_accessed=2 * NZ * DV * DV, transcendentals=0
-        ),
-    )(*operands, after)
-
-
-def add_kernel(kept_ref, *refs):
-    received, out_ref = refs[:2], refs[2]
-    for i in range(DT):
-        place = slice(i * TILE, (i + 1) * TILE)
-        k, at = (0, i) if i < CUT else (1, i - CUT)
-        came = received[k][at * TILE : (at + 1) * TILE, :].astype(jnp.float32)
-        out_ref[place, :] = (kept_ref[place, :] + came).astype(jnp.bfloat16)
-
-
-def add(kept, received):
-    vmem = pl.BlockSpec(memory_space=pltpu.VMEM)
-    return pl.pallas_call(
-        add_kernel,
-        out_shape=pltpu.VMEM((DV, DV), jnp.bfloat16),
-        in_specs=[vmem] * 3,
-        out_specs=vmem,
-        compiler_params=pltpu.CompilerParams(vmem_limit_bytes=16 * MIB),
-        cost_estimate=pl.CostEstimate(flops=DV * DV, bytes_accessed=DV * DV, transcendentals=0),
-    )(*map(in_vmem, (kept, *received)))
+        cost_estimate=ladder_cost(NZ - BEGIN),
+    )(home, *map(in_vmem, (amps, blocks, so_far, base)), after)
 
 
 def finish_kernel(kept_ref, partner_ref, returned_ref, *refs):
@@ -440,18 +474,20 @@
 
     packed = pack(rows, home_amps, remote_amps, turned)
     arrived = lax.all_to_all(packed, ("z", "x", "y"), 0, 0, tiled=True)
-    blocks = arrived.reshape(NZ, OWNERS, DT, SLICE, DV)
+    arrived = arrived.reshape(NZ, OWNERS, DT, SLICE, DV)
 
     turned_late, _ = lax.optimization_barrier((turned, arrived))
     partner_turned = lax.ppermute(turned_late, column_group, partner_perm(False))
 
-    kept, *sent, blocks = ladder(remote_amps, blocks, turned, own)
-    received = [lax.ppermute(part, column_group, home_perm(True)) for part in sent]
-    kept, partner_turned = lax.optimization_barrier((kept, partner_turned))
-    finished = add(kept, received)
+    kept, sent, blocks = remote_ladder(remote_amps, arrived, turned)
+    received = lax.ppermute(sent, column_group, home_perm(True))
+    home_amps, partner_turned = lax.optimization_barrier((home_amps, partner_turned))
+    begun = begin_ladder(home_amps, blocks)
+    kept, begun = lax.optimization_barrier((kept, begun))
+    finished = (kept + received.astype(jnp.float32)).astype(jnp.bfloat16)
     returned = lax.ppermute(finished, column_group, partner_perm(True))
 
-    kept, *sent = ladder(home_amps, blocks, base, finished, is_home)
+    kept, *sent = home_ladder(is_home, home_amps, blocks, begun, base, finished)
     received = [lax.ppermute(part, column_group, home_perm(False)) for part in sent]
     return finish(kept, partner_turned, returned, received)[None]
 

time: 196 us -> 194 us (0.990)
    ppermute x2 -> x1, waiting for transfers between devices: 2.76 us -> 0.32 us  [local(): received = lax.ppermute(sent, column_group, home_perm(True))]
    ppermute x1, starting transfers between devices: 0.06 us -> 2.47 us  [local(): beside = lax.ppermute(own, column_group, flip_z(0))]
    ppermute x1, waiting for transfers between devices: 0.01 us -> 2.38 us  [local(): returned = lax.ppermute(finished, column_group, partner_perm(True))]
  transfers between devices with their start and end apart: 13 -> 12, of which waited for: 5 -> 7; matrix products, arithmetic and copies ran while one was open for 1% -> 1% of each run, Pallas kernels for 23% -> 23%
where the time goes in v6:
time: 194 us; the launch traced here: 193 us
  blocking collectives  82.2 us (42%)
  Pallas kernels  54.1 us (28%)
  starting transfers between devices  33.1 us (17%)
  waiting for transfers between devices  14.5 us (7%)
  local copies, waits for them, and re-layouts  8 us (4%)
    all_to_all x1, blocking collectives, local(): arrived = lax.all_to_all(packed, ('z', 'x', 'y'), 0, 0, tiled=True)  82.2 us
    pallas_call x1, Pallas kernels, remote_ladder(): pl.pallas_call(remote_kernel, out_shape=out_shape, in_specs=[vmem, anywhe...  18.2 us
    pallas_call x1, Pallas kernels, home_ladder(): pl.pallas_call(home_kernel, out_shape=out_shape, in_specs=[pl.BlockSpec(m...  11.6 us
    unnamed x28, local copies, waits for them, and re-layouts  7.35 us
    pallas_call x1, Pallas kernels, pack(): pl.pallas_call(pack_kernel, out_shape=pltpu.HBM(shape, jnp.bfloat16), in_...  7.22 us
    ppermute x1, starting transfers between devices, local(): returned = lax.ppermute(finished, column_group, partner_perm(True))  7.03 us
    all_to_all x1, starting transfers between devices, local(): rows = lax.all_to_all(outgoing, ('x', 'y'), 0, 0, tiled=True)  6.94 us
    ppermute x1, starting transfers between devices, local(): moved = lax.ppermute(early, column_group, partner_perm(True))  5.42 us
  transfers between devices with their start and end apart: 12, of which 7 were waited for; matrix products, arithmetic and copies ran while one was open for 1% of the time, Pallas kernels for 23%

profile of v6, /device:TPU:1, one launch (start us, length us, event | category | flops | bytes accessed | tf_op | source)
XLA Modules:
  0.0 193.4 jit_solution(183563720912162951)
XLA Ops:
  0.0 2.5 %collective-permute-start = (s32[7]{0:T(128)}, s32[7]{0:T(128)S(1)}, u32[]{:S(2)}, u32[]{:S(2)}) collective-permute-start(s32[7]{0:T(128)} %bitcast.47), channel_id=1, source_target_pairs={{0,32},{16,48},{32,0},{48,16},{64,96},{80,112},{96,64},{112,80},{1... | collective-permute-start | bytes 92 | tf_op jit(solution)/shard_map/ppermute | solution.py:447
  2.5 1.0 collective-permute-start.1
  3.4 2.8 %shard_map.64.given_ref = bf16[16,2,8,4224]{3,2,1,0:T(8,128)(2,1)} custom-call(bf16[32,8,4096]{2,1,0:T(8,128)(2,1)} %bitcast.46), custom_call_target="tpu_custom_call" | custom-call | bytes 4194304 | tf_op jit(solution)/shard_map/pallas_call | solution.py:71
  6.7 1.0 shard_map.65.after_ref
  8.1 5.4 %collective-permute-start.3 = (bf16[896,896]{1,0:T(8,128)(2,1)S(1)}, bf16[896,896]{1,0:T(8,128)(2,1)}, u32[]{:S(2)}, u32[]{:S(2)}) collective-permute-start(bf16[896,896]{1,0:T(8,128)(2,1)S(1)} %bitcast.40), channel_id=1, source_target_pairs={{16,64},{48,96},{64,16},{96,48},{17,65},{49,97},{65,17},{97,49},{1... | collective-permute-start | bytes 4816904 | tf_op jit(solution)/shard_map/ppermute | solution.py:462
  14.8 6.9 %all-to-all-start = ((bf16[16,2,8,4224]{3,2,1,0:T(8,128)(2,1)}), bf16[16,2,8,4224]{3,2,1,0:T(8,128)(2,1)}, u32[]{:S(2)}, u32[]{:S(2)}) async-start(bf16[16,2,8,4224]{3,2,1,0:T(8,128)(2,1)} %shard_map.65.after_ref), calls=%async_computation | async-start | bytes 4325376 | tf_op jit(solution)/shard_map/all_to_all | solution.py:458
  21.8 1.0 copy.11
  22.8 1.3 collective-permute-start.5
  24.1 1.0 copy-done.5
  25.2 5.3 %shard_map.66 = (f32[896,896]{1,0:T(8,128)}, bf16[896,896]{1,0:T(8,128)(2,1)}) custom-call(bf16[896,896]{1,0:T(8,128)(2,1)S(1)} %bitcast.42, bf16[896,896]{1,0:T(8,128)(2,1)S(1)} %bitcast.38, bf16[896,896]{1,0:T(8,128)(2,1)S(1)} %bitcast.39, f32[1,896]{1,0:T(1,128)S(1)} %get-tuple-element.48.row_ref, f32[896,1]{1,0:T(8,128)S(1)} %bitcast.44, ...), custom_call_target="tpu_custom_call" | custom-call | flops 1438646272 | bytes 11239424 | tf_op jit(solution)/shard_map/pallas_call | solution.py:209
  30.5 1.9 collective-permute-done.3.refs_3_
  32.4 2.4 %collective-permute-start.4 = (bf16[896,896]{1,0:T(8,128)(2,1)}, bf16[896,896]{1,0:T(8,128)(2,1)S(1)}, u32[]{:S(2)}, u32[]{:S(2)}) collective-permute-start(bf16[896,896]{1,0:T(8,128)(2,1)} %collective-permute-done.3.refs_3_), channel_id=1, source_target_pairs={{16,0},{48,32},{64,80},{96,112},{17,1},{49,33},{65,81},{97,113},{1... | collective-permute-start | bytes 4816904 | tf_op jit(solution)/shard_map/ppermute | solution.py:471
  34.8 3.1 %collective-permute-done.4.refs_1_ = bf16[896,896]{1,0:T(8,128)(2,1)S(1)} collective-permute-done((bf16[896,896]{1,0:T(8,128)(2,1)}, bf16[896,896]{1,0:T(8,128)(2,1)S(1)}, u32[]{:S(2)}, u32[]{:S(2)}) %collective-permute-start.4) | collective-permute-done | bytes 1605664 | tf_op jit(solution)/shard_map/ppermute | solution.py:471
  37.9 1.2 copy-done.9
  39.1 1.4 copy-done.10
  40.5 2.1 %shard_map.67 = (bf16[896,896]{1,0:T(8,128)(2,1)S(1)}, bf16[896,896]{1,0:T(8,128)(2,1)S(1)}) custom-call(s32[1]{0:T(128)} %bitcast.home_ref, bf16[896,896]{1,0:T(8,128)(2,1)S(1)} %bitcast.43, bf16[896,896]{1,0:T(8,128)(2,1)S(1)} %copy-done.10, bf16[896,896]{1,0:T(8,128)(2,1)} %collective-permute-done.5.refs_2_, bf16[896,896]{1,0:T(8,128)(2,1)} %collective-permute-done.3.refs_3_), custom_call_target="tpu_custom_call" | custom-call | bytes 3211264 | tf_op jit(solution)/shard_map/pallas_call | solution.py:261
  42.6 1.1 copy-done.3
  43.8 1.1 copy-done.7
  44.9 4.9 %all-to-all-done = bf16[16,2,8,4224]{3,2,1,0:T(8,128)(2,1)} async-done(((bf16[16,2,8,4224]{3,2,1,0:T(8,128)(2,1)}), bf16[16,2,8,4224]{3,2,1,0:T(8,128)(2,1)}, u32[]{:S(2)}, u32[]{:S(2)}) %all-to-all-start) | async-done | bytes 2162720 | tf_op jit(solution)/shard_map/all_to_all | solution.py:458
  49.8 7.2 %shard_map.68 = bf16[64,7,8,896]{3,2,1,0:T(8,128)(2,1)} custom-call(bf16[32,8,4224]{2,1,0:T(8,128)(2,1)} %bitcast.13.given_ref, bf16[896,896]{1,0:T(8,128)(2,1)} %copy-done.3, bf16[896,896]{1,0:T(8,128)(2,1)} %copy-done.7, bf16[896,896]{1,0:T(8,128)(2,1)} %get-tuple-element.27.refs_2_.added_ref), custom_call_target="tpu_custom_call" | custom-call | bytes 12845056 | tf_op jit(solution)/shard_map/pallas_call | solution.py:171
  57.0 82.2 %all_to_all.10 = bf16[64,7,8,896]{3,2,1,0:T(8,128)(2,1)} all-to-all(bf16[64,7,8,896]{3,2,1,0:T(8,128)(2,1)} %shard_map.68), channel_id=1, replica_groups=mesh['z'=4,'core'=2,'x'=4,'y'=4] {'z','x','y'}, dimensions={0} | all-to-all | bytes 12845056 | tf_op jit(solution)/shard_map/all_to_all | solution.py:476
  139.3 2.7 %collective-permute-start.6 = (bf16[896,896]{1,0:T(8,128)(2,1)S(1)}, bf16[896,896]{1,0:T(8,128)(2,1)S(1)}, u32[]{:S(2)}, u32[]{:S(2)}) collective-permute-start(bf16[896,896]{1,0:T(8,128)(2,1)S(1)} %copy-done.6), channel_id=1, source_target_pairs={{16,80},{48,112},{64,0},{96,32},{17,81},{49,113},{65,1},{97,33},{1... | collective-permute-start | bytes 4816904 | tf_op jit(solution)/shard_map/ppermute | solution.py:480
  142.0 18.2 %shard_map.69 = (f32[896,896]{1,0:T(8,128)S(1)}, bf16[896,896]{1,0:T(8,128)(2,1)S(1)}, bf16[4,896,896]{2,1,0:T(8,128)(2,1)S(1)}) custom-call(bf16[896,896]{1,0:T(8,128)(2,1)S(1)} %copy-done.8, bf16[4,16,7,8,896]{4,3,2,1,0:T(8,128)(2,1)} %bitcast.45, bf16[896,896]{1,0:T(8,128)(2,1)S(1)} %copy-done.6), custom_call_target="tpu_custom_call" | custom-call | flops 11509170176 | bytes 6422528 | tf_op jit(solution)/shard_map/pallas_call | solution.py:368
  160.1 1.3 collective-permute-start.7
  161.5 4.0 %shard_map.70.so_far_ref = f32[896,896]{1,0:T(8,128)S(1)} custom-call(bf16[896,896]{1,0:T(8,128)(2,1)S(1)} %copy-done.4, bf16[4,896,896]{2,1,0:T(8,128)(2,1)S(1)} %get-tuple-element.29.block_ref), custom_call_target="tpu_custom_call" | custom-call | flops 2877292544 | bytes 1605632 | tf_op jit(solution)/shard_map/pallas_call | solution.py:386
  166.0 7.0 %collective-permute-start.8 = (bf16[896,896]{1,0:T(8,128)(2,1)S(1)}, bf16[896,896]{1,0:T(8,128)(2,1)S(1)}, u32[]{:S(2)}, u32[]{:S(2)}) collective-permute-start(bf16[896,896]{1,0:T(8,128)(2,1)S(1)} %add_convert_fusion.after_ref), channel_id=1, source_target_pairs={{16,64},{48,96},{64,16},{96,48},{17,65},{49,97},{65,17},{97,49},{1... | collective-permute-start | bytes 4816904 | tf_op jit(solution)/shard_map/ppermute | solution.py:488
  173.1 11.6 %shard_map.71 = (f32[896,896]{1,0:T(8,128)S(1)}, bf16[512,896]{1,0:T(8,128)(2,1)S(1)}, bf16[384,896]{1,0:T(8,128)(2,1)S(1)}) custom-call(s32[1]{0:T(128)} %bitcast.home_ref, bf16[896,896]{1,0:T(8,128)(2,1)S(1)} %copy-done.4, bf16[4,896,896]{2,1,0:T(8,128)(2,1)S(1)} %get-tuple-element.29.block_ref, f32[896,896]{1,0:T(8,128)S(1)} %shard_map.70.so_far_ref, ...), custom_call_target="tpu_custom_call" | custom-call | flops 8631877632 | bytes 4816896 | tf_op jit(solution)/shard_map/pallas_call | solution.py:404
  184.7 1.3 collective-permute-start.9
  186.1 1.3 collective-permute-start.10
  187.4 1.7 collective-permute-done.10.refs_1_
  189.1 2.4 %collective-permute-done.8.returned_ref = bf16[896,896]{1,0:T(8,128)(2,1)S(1)} collective-permute-done((bf16[896,896]{1,0:T(8,128)(2,1)S(1)}, bf16[896,896]{1,0:T(8,128)(2,1)S(1)}, u32[]{:S(2)}, u32[]{:S(2)}) %collective-permute-start.8) | collective-permute-done | bytes 1605664 | tf_op jit(solution)/shard_map/ppermute | solution.py:488
  191.5 1.8 shard_map.72
  (42 shorter events, 2.1 us)
Async XLA Ops:
  0.0 14.2 %copy-start = (f32[4096]{0:T(1024)S(1)}, f32[4096]{0:T(1024)}, u32[]{:S(2)}) copy-start(f32[4096]{0:T(1024)} %param.10) | copy-start | bytes 49156
  0.0 6.3 %collective-permute-start = (s32[7]{0:T(128)}, s32[7]{0:T(128)S(1)}, u32[]{:S(2)}, u32[]{:S(2)}) collective-permute-start(s32[7]{0:T(128)} %bitcast.47), channel_id=1, source_target_pairs={{0,32},{16,48},{32,0},{48,16},{64,96},{80,112},{96,64},{112,80},{1... | collective-permute-start | bytes 92 | tf_op jit(solution)/shard_map/ppermute | solution.py:447
  2.5 3.8 %collective-permute-start.1 = (s32[7]{0:T(128)}, s32[7]{0:T(128)S(1)}, u32[]{:S(2)}, u32[]{:S(2)}) collective-permute-start(s32[7]{0:T(128)} %bitcast.48), channel_id=1, source_target_pairs={{0,16},{16,0},{1,17},{17,1},{2,18},{18,2},{3,19},{19,3},{4,20},{20... | collective-permute-start | bytes 92 | tf_op jit(solution)/shard_map/ppermute | solution.py:41
  3.4 3.1 %collective-permute-start.2 = (s32[7]{0:T(128)}, s32[7]{0:T(128)S(1)}, u32[]{:S(2)}, u32[]{:S(2)}) collective-permute-start(s32[7]{0:T(128)} %bitcast.49), channel_id=1, source_target_pairs={{0,48},{16,32},{32,16},{48,0},{64,112},{80,96},{96,80},{112,64},{1... | collective-permute-start | bytes 92 | tf_op jit(solution)/shard_map/ppermute | solution.py:448
  3.4 2.9 %copy-start.12 = (s32[1,7]{1,0:T(1,128)S(1)}, s32[1,7]{1,0:T(1,128)}, u32[]{:S(2)}) copy-start(s32[1,7]{1,0:T(1,128)} %param.9) | copy-start | bytes 88
  6.7 1.5 copy-start.2
  8.1 24.3 %collective-permute-start.3 = (bf16[896,896]{1,0:T(8,128)(2,1)S(1)}, bf16[896,896]{1,0:T(8,128)(2,1)}, u32[]{:S(2)}, u32[]{:S(2)}) collective-permute-start(bf16[896,896]{1,0:T(8,128)(2,1)S(1)} %bitcast.40), channel_id=1, source_target_pairs={{16,64},{48,96},{64,16},{96,48},{17,65},{49,97},{65,17},{97,49},{1... | collective-permute-start | bytes 4816904 | tf_op jit(solution)/shard_map/ppermute | solution.py:462
  14.8 9.3 %copy-start.1 = (bf16[1,896,896]{2,1,0:T(8,128)(2,1)S(1)}, bf16[1,896,896]{2,1,0:T(8,128)(2,1)}, u32[]{:S(2)}) copy-start(bf16[1,896,896]{2,1,0:T(8,128)(2,1)} %param.7) | copy-start | bytes 4816900
  14.8 35.0 %all-to-all-start = ((bf16[16,2,8,4224]{3,2,1,0:T(8,128)(2,1)}), bf16[16,2,8,4224]{3,2,1,0:T(8,128)(2,1)}, u32[]{:S(2)}, u32[]{:S(2)}) async-start(bf16[16,2,8,4224]{3,2,1,0:T(8,128)(2,1)} %shard_map.65.after_ref), calls=%async_computation | async-start | bytes 4325376 | tf_op jit(solution)/shard_map/all_to_all | solution.py:458
  22.8 11.9 %collective-permute-start.5 = (bf16[896,896]{1,0:T(8,128)(2,1)S(1)}, bf16[896,896]{1,0:T(8,128)(2,1)}, u32[]{:S(2)}, u32[]{:S(2)}) collective-permute-start(bf16[896,896]{1,0:T(8,128)(2,1)S(1)} %bitcast.41), channel_id=1, source_target_pairs={{0,16},{32,48},{80,64},{112,96},{1,17},{33,49},{81,65},{113,97},{2... | collective-permute-start | bytes 4816904 | tf_op jit(solution)/shard_map/ppermute | solution.py:463
  24.1 1.0 copy-start.5
  32.4 5.6 %collective-permute-start.4 = (bf16[896,896]{1,0:T(8,128)(2,1)}, bf16[896,896]{1,0:T(8,128)(2,1)S(1)}, u32[]{:S(2)}, u32[]{:S(2)}) collective-permute-start(bf16[896,896]{1,0:T(8,128)(2,1)} %collective-permute-done.3.refs_3_), channel_id=1, source_target_pairs={{16,0},{48,32},{64,80},{96,112},{17,1},{49,33},{65,81},{97,113},{1... | collective-permute-start | bytes 4816904 | tf_op jit(solution)/shard_map/ppermute | solution.py:471
  37.9 1.2 copy-start.9
  39.1 1.4 copy-start.10
  42.6 1.2 copy-start.3
  43.8 1.1 copy-start.7
  57.0 82.3 %copy-start.6 = (bf16[896,896]{1,0:T(8,128)(2,1)S(1)}, bf16[896,896]{1,0:T(8,128)(2,1)}, u32[]{:S(2)}) copy-start(bf16[896,896]{1,0:T(8,128)(2,1)} %get-tuple-element.27.refs_2_.added_ref) | copy-start | bytes 4816900
  57.0 84.9 %copy-start.8 = (bf16[896,896]{1,0:T(8,128)(2,1)S(1)}, bf16[896,896]{1,0:T(8,128)(2,1)}, u32[]{:S(2)}) copy-start(bf16[896,896]{1,0:T(8,128)(2,1)} %copy-done.7) | copy-start | bytes 4816900
  139.3 22.2 %copy-start.4 = (bf16[896,896]{1,0:T(8,128)(2,1)S(1)}, bf16[896,896]{1,0:T(8,128)(2,1)}, u32[]{:S(2)}) copy-start(bf16[896,896]{1,0:T(8,128)(2,1)} %copy-done.3) | copy-start | bytes 4816900
  139.3 22.2 %collective-permute-start.6 = (bf16[896,896]{1,0:T(8,128)(2,1)S(1)}, bf16[896,896]{1,0:T(8,128)(2,1)S(1)}, u32[]{:S(2)}, u32[]{:S(2)}) collective-permute-start(bf16[896,896]{1,0:T(8,128)(2,1)S(1)} %copy-done.6), channel_id=1, source_target_pairs={{16,80},{48,112},{64,0},{96,32},{17,81},{49,113},{65,1},{97,33},{1... | collective-permute-start | bytes 4816904 | tf_op jit(solution)/shard_map/ppermute | solution.py:480
  160.1 5.6 %collective-permute-start.7 = (bf16[896,896]{1,0:T(8,128)(2,1)S(1)}, bf16[896,896]{1,0:T(8,128)(2,1)S(1)}, u32[]{:S(2)}, u32[]{:S(2)}) collective-permute-start(bf16[896,896]{1,0:T(8,128)(2,1)S(1)} %get-tuple-element.34), channel_id=1, source_target_pairs={{0,16},{32,48},{80,64},{112,96},{1,17},{33,49},{81,65},{113,97},{2... | collective-permute-start | bytes 4816904 | tf_op jit(solution)/shard_map/ppermute | solution.py:483
  165.4 7.7 %copy-start.11 = (f32[896,896]{1,0:T(8,128)S(1)}, f32[896,896]{1,0:T(8,128)}, u32[]{:S(2)}) copy-start(f32[896,896]{1,0:T(8,128)} %get-tuple-element.32.added_ref) | copy-start | bytes 9633796
  166.0 25.5 %collective-permute-start.8 = (bf16[896,896]{1,0:T(8,128)(2,1)S(1)}, bf16[896,896]{1,0:T(8,128)(2,1)S(1)}, u32[]{:S(2)}, u32[]{:S(2)}) collective-permute-start(bf16[896,896]{1,0:T(8,128)(2,1)S(1)} %add_convert_fusion.after_ref), channel_id=1, source_target_pairs={{16,64},{48,96},{64,16},{96,48},{17,65},{49,97},{65,17},{97,49},{1... | collective-permute-start | bytes 4816904 | tf_op jit(solution)/shard_map/ppermute | solution.py:488
  184.7 4.4 %collective-permute-start.9 = (bf16[512,896]{1,0:T(8,128)(2,1)S(1)}, bf16[512,896]{1,0:T(8,128)(2,1)S(1)}, u32[]{:S(2)}, u32[]{:S(2)}) collective-permute-start(bf16[512,896]{1,0:T(8,128)(2,1)S(1)} %get-tuple-element.37), channel_id=1, source_target_pairs={{16,0},{48,32},{64,80},{96,112},{17,1},{49,33},{65,81},{97,113},{1... | collective-permute-start | bytes 2752520 | tf_op jit(solution)/shard_map/ppermute | solution.py:491
  186.1 3.1 %collective-permute-start.10 = (bf16[384,896]{1,0:T(8,128)(2,1)S(1)}, bf16[384,896]{1,0:T(8,128)(2,1)S(1)}, u32[]{:S(2)}, u32[]{:S(2)}) collective-permute-start(bf16[384,896]{1,0:T(8,128)(2,1)S(1)} %get-tuple-element.38), channel_id=1, source_target_pairs={{16,0},{48,32},{64,80},{96,112},{17,1},{49,33},{65,81},{97,113},{1... | collective-permute-start | bytes 2064392 | tf_op jit(solution)/shard_map/ppermute | solution.py:491

commit v7 on v6

--- a/solution.py
+++ b/solution.py
@@ -280,8 +280,8 @@
         ).astype(jnp.bfloat16)
         if q < vectors[-1]:
             ready(q + 1)
-        for i in range(DT):
-            place = slice(i * TILE, (i + 1) * TILE)
+        for i, (start, stop) in enumerate(((0, CUT), (CUT, DT))):
+            place = slice(start * TILE, stop * TILE)
             part = jnp.dot(
                 block_ref[q, place, :], half[...], preferred_element_type=jnp.float32
             )
@@ -296,8 +296,8 @@
 
 
 def put(part, i, first_ref, second_ref):
-    target, at = (first_ref, i) if i < CUT else (second_ref, i - CUT)
-    target[at * TILE : (at + 1) * TILE, :] = part.astype(jnp.bfloat16)
+    target = first_ref if i == 0 else second_ref
+    target[...] = part.astype(jnp.bfloat16)
 
 
 def remote_kernel(amps_ref, given_ref, added_ref, *refs):
@@ -376,7 +376,7 @@
             pltpu.VMEM((NZ, DT, OWNERS, SLICE, DV), jnp.bfloat16),
             pltpu.SemaphoreType.DMA((NZ, DT)),
         ],
-        compiler_params=pltpu.CompilerParams(vmem_limit_bytes=16 * MIB),
+        compiler_params=pltpu.CompilerParams(vmem_limit_bytes=20 * MIB),
         cost_estimate=ladder_cost(NZ),
     )(in_vmem(amps), in_hbm(arrived), in_vmem(turned))
 
@@ -389,7 +389,7 @@
         in_specs=[vmem] * 2,
         out_specs=vmem,
         scratch_shapes=[pltpu.VMEM((DV, DV), jnp.bfloat16)],
-        compiler_params=pltpu.CompilerParams(vmem_limit_bytes=16 * MIB),
+        compiler_params=pltpu.CompilerParams(vmem_limit_bytes=20 * MIB),
         cost_estimate=ladder_cost(BEGIN),
     )(in_vmem(amps), in_vmem(blocks))
 
@@ -407,7 +407,7 @@
         in_specs=[pl.BlockSpec(memory_space=pltpu.SMEM)] + [vmem] * 4 + [anywhere],
         out_specs=[vmem] * len(out_shape),
         scratch_shapes=[pltpu.VMEM((DV, DV), jnp.bfloat16), pltpu.VMEM((DV, DV), jnp.float32)],
-        compiler_params=pltpu.CompilerParams(vmem_limit_bytes=16 * MIB),
+        compiler_params=pltpu.CompilerParams(vmem_limit_bytes=20 * MIB),
         cost_estimate=ladder_cost(NZ - BEGIN),
     )(home, *map(in_vmem, (amps, blocks, so_far, base)), after)
 
@@ -430,7 +430,7 @@
         out_shape=jax.ShapeDtypeStruct((DV, DV), jnp.bfloat16),
         in_specs=[vmem] * 5,
         out_specs=vmem,
-        compiler_params=pltpu.CompilerParams(vmem_limit_bytes=16 * MIB),
+        compiler_params=pltpu.CompilerParams(vmem_limit_bytes=20 * MIB),
         cost_estimate=pl.CostEstimate(flops=DV * DV, bytes_accessed=DV * DV, transcendentals=0),
     )(*map(in_vmem, (kept, partner_turned, returned, *received)))
 

time: 194 us -> 193 us (level)
  transfers between devices with their start and end apart: 12 -> 12, of which waited for: 7 -> 7; matrix products, arithmetic and copies ran while one was open for 1% -> 1% of each run, Pallas kernels for 23% -> 22%
where the time goes in v7:
time: 193 us
  blocking collectives  82.2 us (43%)
  Pallas kernels  53.1 us (28%)
  starting transfers between devices  33.4 us (17%)
  waiting for transfers between devices  14.8 us (8%)
  local copies, waits for them, and re-layouts  8 us (4%)
    all_to_all x1, blocking collectives, local(): arrived = lax.all_to_all(packed, ('z', 'x', 'y'), 0, 0, tiled=True)  82.2 us
    pallas_call x1, Pallas kernels, remote_ladder(): pl.pallas_call(remote_kernel, out_shape=out_shape, in_specs=[vmem, anywhe...  17.6 us
    pallas_call x1, Pallas kernels, home_ladder(): pl.pallas_call(home_kernel, out_shape=out_shape, in_specs=[pl.BlockSpec(m...  11.3 us
    unnamed x28, local copies, waits for them, and re-layouts  7.35 us
    pallas_call x1, Pallas kernels, pack(): pl.pallas_call(pack_kernel, out_shape=pltpu.HBM(shape, jnp.bfloat16), in_...  7.22 us
    ppermute x1, starting transfers between devices, local(): returned = lax.ppermute(finished, column_group, partner_perm(True))  7.12 us
    all_to_all x1, starting transfers between devices, local(): rows = lax.all_to_all(outgoing, ('x', 'y'), 0, 0, tiled=True)  6.94 us
    ppermute x1, starting transfers between devices, local(): moved = lax.ppermute(early, column_group, partner_perm(True))  5.42 us
  transfers between devices with their start and end apart: 12, of which 7 were waited for; matrix products, arithmetic and copies ran while one was open for 1% of the time, Pallas kernels for 22%

profile of v7, /device:TPU:1, one launch (start us, length us, event | category | flops | bytes accessed | tf_op | source)
XLA Modules:
  0.0 192.9 jit_solution(12295782483808356251)
XLA Ops:
  0.0 2.5 %collective-permute-start = (s32[7]{0:T(128)}, s32[7]{0:T(128)S(1)}, u32[]{:S(2)}, u32[]{:S(2)}) collective-permute-start(s32[7]{0:T(128)} %bitcast.47), channel_id=1, source_target_pairs={{0,32},{16,48},{32,0},{48,16},{64,96},{80,112},{96,64},{112,80},{1... | collective-permute-start | bytes 92 | tf_op jit(solution)/shard_map/ppermute | solution.py:447
  2.5 1.0 collective-permute-start.1
  3.4 2.8 %shard_map.64.given_ref = bf16[16,2,8,4224]{3,2,1,0:T(8,128)(2,1)} custom-call(bf16[32,8,4096]{2,1,0:T(8,128)(2,1)} %bitcast.46), custom_call_target="tpu_custom_call" | custom-call | bytes 4194304 | tf_op jit(solution)/shard_map/pallas_call | solution.py:71
  6.7 1.0 shard_map.65.after_ref
  8.1 5.4 %collective-permute-start.3 = (bf16[896,896]{1,0:T(8,128)(2,1)S(1)}, bf16[896,896]{1,0:T(8,128)(2,1)}, u32[]{:S(2)}, u32[]{:S(2)}) collective-permute-start(bf16[896,896]{1,0:T(8,128)(2,1)S(1)} %bitcast.40), channel_id=1, source_target_pairs={{16,64},{48,96},{64,16},{96,48},{17,65},{49,97},{65,17},{97,49},{1... | collective-permute-start | bytes 4816904 | tf_op jit(solution)/shard_map/ppermute | solution.py:462
  14.8 6.9 %all-to-all-start = ((bf16[16,2,8,4224]{3,2,1,0:T(8,128)(2,1)}), bf16[16,2,8,4224]{3,2,1,0:T(8,128)(2,1)}, u32[]{:S(2)}, u32[]{:S(2)}) async-start(bf16[16,2,8,4224]{3,2,1,0:T(8,128)(2,1)} %shard_map.65.after_ref), calls=%async_computation | async-start | bytes 4325376 | tf_op jit(solution)/shard_map/all_to_all | solution.py:458
  21.8 1.0 copy.11
  22.8 1.3 collective-permute-start.5
  24.1 1.0 copy-done.5
  25.2 5.3 %shard_map.66 = (f32[896,896]{1,0:T(8,128)}, bf16[896,896]{1,0:T(8,128)(2,1)}) custom-call(bf16[896,896]{1,0:T(8,128)(2,1)S(1)} %bitcast.42, bf16[896,896]{1,0:T(8,128)(2,1)S(1)} %bitcast.38, bf16[896,896]{1,0:T(8,128)(2,1)S(1)} %bitcast.39, f32[1,896]{1,0:T(1,128)S(1)} %get-tuple-element.48.row_ref, f32[896,1]{1,0:T(8,128)S(1)} %bitcast.44, ...), custom_call_target="tpu_custom_call" | custom-call | flops 1438646272 | bytes 11239424 | tf_op jit(solution)/shard_map/pallas_call | solution.py:209
  30.5 1.9 collective-permute-done.3.refs_3_
  32.4 2.4 %collective-permute-start.4 = (bf16[896,896]{1,0:T(8,128)(2,1)}, bf16[896,896]{1,0:T(8,128)(2,1)S(1)}, u32[]{:S(2)}, u32[]{:S(2)}) collective-permute-start(bf16[896,896]{1,0:T(8,128)(2,1)} %collective-permute-done.3.refs_3_), channel_id=1, source_target_pairs={{16,0},{48,32},{64,80},{96,112},{17,1},{49,33},{65,81},{97,113},{1... | collective-permute-start | bytes 4816904 | tf_op jit(solution)/shard_map/ppermute | solution.py:471
  34.8 3.1 %collective-permute-done.4.refs_1_ = bf16[896,896]{1,0:T(8,128)(2,1)S(1)} collective-permute-done((bf16[896,896]{1,0:T(8,128)(2,1)}, bf16[896,896]{1,0:T(8,128)(2,1)S(1)}, u32[]{:S(2)}, u32[]{:S(2)}) %collective-permute-start.4) | collective-permute-done | bytes 1605664 | tf_op jit(solution)/shard_map/ppermute | solution.py:471
  37.9 1.2 copy-done.9
  39.1 1.4 copy-done.10
  40.5 2.1 %shard_map.67 = (bf16[896,896]{1,0:T(8,128)(2,1)S(1)}, bf16[896,896]{1,0:T(8,128)(2,1)S(1)}) custom-call(s32[1]{0:T(128)} %bitcast.home_ref, bf16[896,896]{1,0:T(8,128)(2,1)S(1)} %bitcast.43, bf16[896,896]{1,0:T(8,128)(2,1)S(1)} %copy-done.10, bf16[896,896]{1,0:T(8,128)(2,1)} %collective-permute-done.5.refs_2_, bf16[896,896]{1,0:T(8,128)(2,1)} %collective-permute-done.3.refs_3_), custom_call_target="tpu_custom_call" | custom-call | bytes 3211264 | tf_op jit(solution)/shard_map/pallas_call | solution.py:261
  42.6 1.1 copy-done.3
  43.8 1.1 copy-done.7
  44.9 4.9 %all-to-all-done = bf16[16,2,8,4224]{3,2,1,0:T(8,128)(2,1)} async-done(((bf16[16,2,8,4224]{3,2,1,0:T(8,128)(2,1)}), bf16[16,2,8,4224]{3,2,1,0:T(8,128)(2,1)}, u32[]{:S(2)}, u32[]{:S(2)}) %all-to-all-start) | async-done | bytes 2162720 | tf_op jit(solution)/shard_map/all_to_all | solution.py:458
  49.8 7.2 %shard_map.68 = bf16[64,7,8,896]{3,2,1,0:T(8,128)(2,1)} custom-call(bf16[32,8,4224]{2,1,0:T(8,128)(2,1)} %bitcast.13.given_ref, bf16[896,896]{1,0:T(8,128)(2,1)} %copy-done.3, bf16[896,896]{1,0:T(8,128)(2,1)} %copy-done.7, bf16[896,896]{1,0:T(8,128)(2,1)} %get-tuple-element.27.refs_2_.added_ref), custom_call_target="tpu_custom_call" | custom-call | bytes 12845056 | tf_op jit(solution)/shard_map/pallas_call | solution.py:171
  57.0 82.2 %all_to_all.10 = bf16[64,7,8,896]{3,2,1,0:T(8,128)(2,1)} all-to-all(bf16[64,7,8,896]{3,2,1,0:T(8,128)(2,1)} %shard_map.68), channel_id=1, replica_groups=mesh['z'=4,'core'=2,'x'=4,'y'=4] {'z','x','y'}, dimensions={0} | all-to-all | bytes 12845056 | tf_op jit(solution)/shard_map/all_to_all | solution.py:476
  139.3 2.7 %collective-permute-start.6 = (bf16[896,896]{1,0:T(8,128)(2,1)S(1)}, bf16[896,896]{1,0:T(8,128)(2,1)S(1)}, u32[]{:S(2)}, u32[]{:S(2)}) collective-permute-start(bf16[896,896]{1,0:T(8,128)(2,1)S(1)} %copy-done.6), channel_id=1, source_target_pairs={{16,80},{48,112},{64,0},{96,32},{17,81},{49,113},{65,1},{97,33},{1... | collective-permute-start | bytes 4816904 | tf_op jit(solution)/shard_map/ppermute | solution.py:480
  142.0 17.6 %shard_map.69 = (f32[896,896]{1,0:T(8,128)S(1)}, bf16[896,896]{1,0:T(8,128)(2,1)S(1)}, bf16[4,896,896]{2,1,0:T(8,128)(2,1)S(1)}) custom-call(bf16[896,896]{1,0:T(8,128)(2,1)S(1)} %copy-done.8, bf16[4,16,7,8,896]{4,3,2,1,0:T(8,128)(2,1)} %bitcast.45, bf16[896,896]{1,0:T(8,128)(2,1)S(1)} %copy-done.6), custom_call_target="tpu_custom_call" | custom-call | flops 11509170176 | bytes 6422528 | tf_op jit(solution)/shard_map/pallas_call | solution.py:368
  159.6 1.5 collective-permute-start.7
  161.1 3.9 %shard_map.70.so_far_ref = f32[896,896]{1,0:T(8,128)S(1)} custom-call(bf16[896,896]{1,0:T(8,128)(2,1)S(1)} %copy-done.4, bf16[4,896,896]{2,1,0:T(8,128)(2,1)S(1)} %get-tuple-element.29.block_ref), custom_call_target="tpu_custom_call" | custom-call | flops 2877292544 | bytes 1605632 | tf_op jit(solution)/shard_map/pallas_call | solution.py:386
  165.5 7.1 %collective-permute-start.8 = (bf16[896,896]{1,0:T(8,128)(2,1)S(1)}, bf16[896,896]{1,0:T(8,128)(2,1)S(1)}, u32[]{:S(2)}, u32[]{:S(2)}) collective-permute-start(bf16[896,896]{1,0:T(8,128)(2,1)S(1)} %add_convert_fusion.after_ref), channel_id=1, source_target_pairs={{16,64},{48,96},{64,16},{96,48},{17,65},{49,97},{65,17},{97,49},{1... | collective-permute-start | bytes 4816904 | tf_op jit(solution)/shard_map/ppermute | solution.py:488
  172.6 11.3 %shard_map.71 = (f32[896,896]{1,0:T(8,128)S(1)}, bf16[512,896]{1,0:T(8,128)(2,1)S(1)}, bf16[384,896]{1,0:T(8,128)(2,1)S(1)}) custom-call(s32[1]{0:T(128)} %bitcast.home_ref, bf16[896,896]{1,0:T(8,128)(2,1)S(1)} %copy-done.4, bf16[4,896,896]{2,1,0:T(8,128)(2,1)S(1)} %get-tuple-element.29.block_ref, f32[896,896]{1,0:T(8,128)S(1)} %shard_map.70.so_far_ref, ...), custom_call_target="tpu_custom_call" | custom-call | flops 8631877632 | bytes 4816896 | tf_op jit(solution)/shard_map/pallas_call | solution.py:404
  183.9 1.3 collective-permute-start.9
  185.3 1.3 collective-permute-start.10
  186.6 1.7 collective-permute-done.10.refs_1_
  188.3 2.7 %collective-permute-done.8.returned_ref = bf16[896,896]{1,0:T(8,128)(2,1)S(1)} collective-permute-done((bf16[896,896]{1,0:T(8,128)(2,1)S(1)}, bf16[896,896]{1,0:T(8,128)(2,1)S(1)}, u32[]{:S(2)}, u32[]{:S(2)}) %collective-permute-start.8) | collective-permute-done | bytes 1605664 | tf_op jit(solution)/shard_map/ppermute | solution.py:488
  191.0 1.8 shard_map.72
  (42 shorter events, 2.0 us)
Async XLA Ops:
  0.0 14.2 %copy-start = (f32[4096]{0:T(1024)S(1)}, f32[4096]{0:T(1024)}, u32[]{:S(2)}) copy-start(f32[4096]{0:T(1024)} %param.10) | copy-start | bytes 49156
  0.0 6.3 %collective-permute-start = (s32[7]{0:T(128)}, s32[7]{0:T(128)S(1)}, u32[]{:S(2)}, u32[]{:S(2)}) collective-permute-start(s32[7]{0:T(128)} %bitcast.47), channel_id=1, source_target_pairs={{0,32},{16,48},{32,0},{48,16},{64,96},{80,112},{96,64},{112,80},{1... | collective-permute-start | bytes 92 | tf_op jit(solution)/shard_map/ppermute | solution.py:447
  2.5 3.8 %collective-permute-start.1 = (s32[7]{0:T(128)}, s32[7]{0:T(128)S(1)}, u32[]{:S(2)}, u32[]{:S(2)}) collective-permute-start(s32[7]{0:T(128)} %bitcast.48), channel_id=1, source_target_pairs={{0,16},{16,0},{1,17},{17,1},{2,18},{18,2},{3,19},{19,3},{4,20},{20... | collective-permute-start | bytes 92 | tf_op jit(solution)/shard_map/ppermute | solution.py:41
  3.4 3.1 %collective-permute-start.2 = (s32[7]{0:T(128)}, s32[7]{0:T(128)S(1)}, u32[]{:S(2)}, u32[]{:S(2)}) collective-permute-start(s32[7]{0:T(128)} %bitcast.49), channel_id=1, source_target_pairs={{0,48},{16,32},{32,16},{48,0},{64,112},{80,96},{96,80},{112,64},{1... | collective-permute-start | bytes 92 | tf_op jit(solution)/shard_map/ppermute | solution.py:448
  3.4 2.9 %copy-start.12 = (s32[1,7]{1,0:T(1,128)S(1)}, s32[1,7]{1,0:T(1,128)}, u32[]{:S(2)}) copy-start(s32[1,7]{1,0:T(1,128)} %param.9) | copy-start | bytes 88
  6.7 1.5 copy-start.2
  8.1 24.3 %collective-permute-start.3 = (bf16[896,896]{1,0:T(8,128)(2,1)S(1)}, bf16[896,896]{1,0:T(8,128)(2,1)}, u32[]{:S(2)}, u32[]{:S(2)}) collective-permute-start(bf16[896,896]{1,0:T(8,128)(2,1)S(1)} %bitcast.40), channel_id=1, source_target_pairs={{16,64},{48,96},{64,16},{96,48},{17,65},{49,97},{65,17},{97,49},{1... | collective-permute-start | bytes 4816904 | tf_op jit(solution)/shard_map/ppermute | solution.py:462
  14.8 9.3 %copy-start.1 = (bf16[1,896,896]{2,1,0:T(8,128)(2,1)S(1)}, bf16[1,896,896]{2,1,0:T(8,128)(2,1)}, u32[]{:S(2)}) copy-start(bf16[1,896,896]{2,1,0:T(8,128)(2,1)} %param.7) | copy-start | bytes 4816900
  14.8 35.0 %all-to-all-start = ((bf16[16,2,8,4224]{3,2,1,0:T(8,128)(2,1)}), bf16[16,2,8,4224]{3,2,1,0:T(8,128)(2,1)}, u32[]{:S(2)}, u32[]{:S(2)}) async-start(bf16[16,2,8,4224]{3,2,1,0:T(8,128)(2,1)} %shard_map.65.after_ref), calls=%async_computation | async-start | bytes 4325376 | tf_op jit(solution)/shard_map/all_to_all | solution.py:458
  22.8 11.9 %collective-permute-start.5 = (bf16[896,896]{1,0:T(8,128)(2,1)S(1)}, bf16[896,896]{1,0:T(8,128)(2,1)}, u32[]{:S(2)}, u32[]{:S(2)}) collective-permute-start(bf16[896,896]{1,0:T(8,128)(2,1)S(1)} %bitcast.41), channel_id=1, source_target_pairs={{0,16},{32,48},{80,64},{112,96},{1,17},{33,49},{81,65},{113,97},{2... | collective-permute-start | bytes 4816904 | tf_op jit(solution)/shard_map/ppermute | solution.py:463
  24.1 1.0 copy-start.5
  32.4 5.6 %collective-permute-start.4 = (bf16[896,896]{1,0:T(8,128)(2,1)}, bf16[896,896]{1,0:T(8,128)(2,1)S(1)}, u32[]{:S(2)}, u32[]{:S(2)}) collective-permute-start(bf16[896,896]{1,0:T(8,128)(2,1)} %collective-permute-done.3.refs_3_), channel_id=1, source_target_pairs={{16,0},{48,32},{64,80},{96,112},{17,1},{49,33},{65,81},{97,113},{1... | collective-permute-start | bytes 4816904 | tf_op jit(solution)/shard_map/ppermute | solution.py:471
  37.9 1.2 copy-start.9
  39.1 1.4 copy-start.10
  42.6 1.2 copy-start.3
  43.8 1.1 copy-start.7
  57.0 82.3 %copy-start.6 = (bf16[896,896]{1,0:T(8,128)(2,1)S(1)}, bf16[896,896]{1,0:T(8,128)(2,1)}, u32[]{:S(2)}) copy-start(bf16[896,896]{1,0:T(8,128)(2,1)} %get-tuple-element.27.refs_2_.added_ref) | copy-start | bytes 4816900
  57.0 84.9 %copy-start.8 = (bf16[896,896]{1,0:T(8,128)(2,1)S(1)}, bf16[896,896]{1,0:T(8,128)(2,1)}, u32[]{:S(2)}) copy-start(bf16[896,896]{1,0:T(8,128)(2,1)} %copy-done.7) | copy-start | bytes 4816900
  139.3 21.8 %copy-start.4 = (bf16[896,896]{1,0:T(8,128)(2,1)S(1)}, bf16[896,896]{1,0:T(8,128)(2,1)}, u32[]{:S(2)}) copy-start(bf16[896,896]{1,0:T(8,128)(2,1)} %copy-done.3) | copy-start | bytes 4816900
  139.3 21.8 %collective-permute-start.6 = (bf16[896,896]{1,0:T(8,128)(2,1)S(1)}, bf16[896,896]{1,0:T(8,128)(2,1)S(1)}, u32[]{:S(2)}, u32[]{:S(2)}) collective-permute-start(bf16[896,896]{1,0:T(8,128)(2,1)S(1)} %copy-done.6), channel_id=1, source_target_pairs={{16,80},{48,112},{64,0},{96,32},{17,81},{49,113},{65,1},{97,33},{1... | collective-permute-start | bytes 4816904 | tf_op jit(solution)/shard_map/ppermute | solution.py:480
  159.6 5.6 %collective-permute-start.7 = (bf16[896,896]{1,0:T(8,128)(2,1)S(1)}, bf16[896,896]{1,0:T(8,128)(2,1)S(1)}, u32[]{:S(2)}, u32[]{:S(2)}) collective-permute-start(bf16[896,896]{1,0:T(8,128)(2,1)S(1)} %get-tuple-element.34), channel_id=1, source_target_pairs={{0,16},{32,48},{80,64},{112,96},{1,17},{33,49},{81,65},{113,97},{2... | collective-permute-start | bytes 4816904 | tf_op jit(solution)/shard_map/ppermute | solution.py:483
  165.0 7.6 %copy-start.11 = (f32[896,896]{1,0:T(8,128)S(1)}, f32[896,896]{1,0:T(8,128)}, u32[]{:S(2)}) copy-start(f32[896,896]{1,0:T(8,128)} %get-tuple-element.32.added_ref) | copy-start | bytes 9633796
  165.5 25.6 %collective-permute-start.8 = (bf16[896,896]{1,0:T(8,128)(2,1)S(1)}, bf16[896,896]{1,0:T(8,128)(2,1)S(1)}, u32[]{:S(2)}, u32[]{:S(2)}) collective-permute-start(bf16[896,896]{1,0:T(8,128)(2,1)S(1)} %add_convert_fusion.after_ref), channel_id=1, source_target_pairs={{16,64},{48,96},{64,16},{96,48},{17,65},{49,97},{65,17},{97,49},{1... | collective-permute-start | bytes 4816904 | tf_op jit(solution)/shard_map/ppermute | solution.py:488
  183.9 4.4 %collective-permute-start.9 = (bf16[512,896]{1,0:T(8,128)(2,1)S(1)}, bf16[512,896]{1,0:T(8,128)(2,1)S(1)}, u32[]{:S(2)}, u32[]{:S(2)}) collective-permute-start(bf16[512,896]{1,0:T(8,128)(2,1)S(1)} %get-tuple-element.37), channel_id=1, source_target_pairs={{16,0},{48,32},{64,80},{96,112},{17,1},{49,33},{65,81},{97,113},{1... | collective-permute-start | bytes 2752520 | tf_op jit(solution)/shard_map/ppermute | solution.py:491
  185.3 3.1 %collective-permute-start.10 = (bf16[384,896]{1,0:T(8,128)(2,1)S(1)}, bf16[384,896]{1,0:T(8,128)(2,1)S(1)}, u32[]{:S(2)}, u32[]{:S(2)}) collective-permute-start(bf16[384,896]{1,0:T(8,128)(2,1)S(1)} %get-tuple-element.38), channel_id=1, source_target_pairs={{16,0},{48,32},{64,80},{96,112},{17,1},{49,33},{65,81},{97,113},{1... | collective-permute-start | bytes 2064392 | tf_op jit(solution)/shard_map/ppermute | solution.py:491

commit v8 on v7

--- a/solution.py
+++ b/solution.py
@@ -191,12 +191,15 @@
 
 
 def cycle_kernel(
-    amps_ref, exch_all_ref, exch_ref, row_ref, col_ref, after_ref, base_ref, turned_ref
+    domain_ref, pair_ref, amps_ref, exch_all_ref, exch_ref, energy_ref, after_ref, base_ref, turned_ref
 ):
     del after_ref
     cycle = jnp.dot(amps_ref[...], exch_all_ref[...], preferred_element_type=jnp.float32)
     cycle = cycle.astype(jnp.bfloat16).astype(jnp.float32)
-    denominator = col_ref[...] + row_ref[...]
+    energies = [energy_ref[pl.ds(domain_ref[t], 1), :] for t in range(DT)]
+    here = energy_ref[pl.ds(domain_ref[pl.program_id(0)], 1), :]
+    column = jnp.broadcast_to(here, (TILE, TILE)).T[:, 0:1] - pair_ref[0]
+    denominator = column + jnp.concatenate(energies, axis=1)
     base_ref[...] = (
         exch_ref[...].astype(jnp.float32)
         + denominator * amps_ref[...].astype(jnp.float32)
@@ -205,17 +208,18 @@
     turned_ref[...] = cycle.T.astype(jnp.bfloat16)
 
 
-def cycle_and_base(amps, exch, row, col, after):
+def cycle_and_base(domain, pair_energy, amps, exch, energies, after):
     return pl.pallas_call(
         cycle_kernel,
         out_shape=(pltpu.HBM((DV, DV), jnp.float32), pltpu.HBM((DV, DV), jnp.bfloat16)),
         grid=(DT,),
         in_specs=[
+            pl.BlockSpec(memory_space=pltpu.SMEM),
+            pl.BlockSpec(memory_space=pltpu.SMEM),
             pl.BlockSpec((TILE, DV), lambda i: (i, 0)),
             pl.BlockSpec((DV, DV), lambda i: (0, 0)),
             pl.BlockSpec((TILE, DV), lambda i: (i, 0)),
-            pl.BlockSpec((1, DV), lambda i: (0, 0)),
-            pl.BlockSpec((TILE, 1), lambda i: (i, 0)),
+            pl.BlockSpec((NVT, TILE), lambda i: (0, 0)),
             pl.BlockSpec(memory_space=pl.ANY),
         ],
         out_specs=(
@@ -226,7 +230,7 @@
         cost_estimate=pl.CostEstimate(
             flops=2 * DV**3, bytes_accessed=14 * DV * DV, transcendentals=0
         ),
-    )(amps, exch, exch, row, col, in_hbm(after))
+    )(domain, pair_energy, amps, exch, exch, energies, in_hbm(after))
 
 
 def choose_kernel(home_ref, *refs):
@@ -462,9 +466,8 @@
     moved = lax.ppermute(early, column_group, partner_perm(True))
     home_amps = lax.ppermute(early, column_group, home_perm(True))
 
-    energies = jnp.take(virt_energy.reshape(NVT, TILE), own, axis=0).reshape(DV)
     base, turned = cycle_and_base(
-        amps, exch, energies[None, :], (energies - pair_energy[0])[:, None], outgoing
+        own, pair_energy, amps, exch, virt_energy.reshape(NVT, TILE), outgoing
     )
 
     moved, _ = lax.optimization_barrier((moved, turned))

time: 193 us -> 192 us (level)
  local copies, waits for them, and re-layouts: 8 us -> 2.88 us
  waiting for transfers between devices: 14.8 us -> 19.4 us
    unnamed x28 -> x20, local copies, waits for them, and re-layouts: 7.35 us -> 2.78 us
    all_to_all x1, waiting for transfers between devices: 4.87 us -> 7.31 us  [local(): rows = lax.all_to_all(outgoing, ('x', 'y'), 0, 0, tiled=True)]
  transfers between devices with their start and end apart: 12 -> 12, of which waited for: 7 -> 7; matrix products, arithmetic and copies ran while one was open for 1% -> 0% of each run, Pallas kernels for 22% -> 23%
where the time goes in v8:
time: 192 us; the launch traced here: 191 us
  blocking collectives  81.5 us (42%)
  Pallas kernels  53.7 us (28%)
  starting transfers between devices  32.5 us (17%)
  waiting for transfers between devices  19.4 us (10%)
  local copies, waits for them, and re-layouts  2.88 us (2%)
    all_to_all x1, blocking collectives, local(): arrived = lax.all_to_all(packed, ('z', 'x', 'y'), 0, 0, tiled=True)  81.5 us
    pallas_call x1, Pallas kernels, remote_ladder(): pl.pallas_call(remote_kernel, out_shape=out_shape, in_specs=[vmem, anywhe...  17.6 us
    pallas_call x1, Pallas kernels, home_ladder(): pl.pallas_call(home_kernel, out_shape=out_shape, in_specs=[pl.BlockSpec(m...  11.3 us
    all_to_all x1, waiting for transfers between devices, local(): rows = lax.all_to_all(outgoing, ('x', 'y'), 0, 0, tiled=True)  7.31 us
    pallas_call x1, Pallas kernels, pack(): pl.pallas_call(pack_kernel, out_shape=pltpu.HBM(shape, jnp.bfloat16), in_...  7.21 us
    ppermute x1, starting transfers between devices, local(): returned = lax.ppermute(finished, column_group, partner_perm(True))  7.11 us
    all_to_all x1, starting transfers between devices, local(): rows = lax.all_to_all(outgoing, ('x', 'y'), 0, 0, tiled=True)  6.81 us
    pallas_call x1, Pallas kernels, cycle_and_base(): pl.pallas_call(cycle_kernel, out_shape=(pltpu.HBM((DV, DV), jnp.float32),...  5.96 us
  transfers between devices with their start and end apart: 12, of which 7 were waited for; matrix products, arithmetic and copies ran while one was open for 0% of the time, Pallas kernels for 23%

profile of v8, /device:TPU:1, one launch (start us, length us, event | category | flops | bytes accessed | tf_op | source)
XLA Modules:
  0.0 191.2 jit_solution(14945350709488891503)
XLA Ops:
  0.0 2.5 %collective-permute-start = (s32[7]{0:T(128)}, s32[7]{0:T(128)S(1)}, u32[]{:S(2)}, u32[]{:S(2)}) collective-permute-start(s32[7]{0:T(128)} %bitcast.26), channel_id=1, source_target_pairs={{0,32},{16,48},{32,0},{48,16},{64,96},{80,112},{96,64},{112,80},{1... | collective-permute-start | bytes 92 | tf_op jit(solution)/shard_map/ppermute | solution.py:451
  2.5 1.0 collective-permute-start.1
  3.4 2.9 %shard_map.64.given_ref = bf16[16,2,8,4224]{3,2,1,0:T(8,128)(2,1)} custom-call(bf16[32,8,4096]{2,1,0:T(8,128)(2,1)} %bitcast.31), custom_call_target="tpu_custom_call" | custom-call | bytes 4194304 | tf_op jit(solution)/shard_map/pallas_call | solution.py:71
  6.3 0.2 collective-permute-done.2
  6.7 1.0 shard_map.65.after_ref
  7.6 0.5 copy-done.1
  8.1 5.6 %collective-permute-start.3 = (bf16[896,896]{1,0:T(8,128)(2,1)S(1)}, bf16[896,896]{1,0:T(8,128)(2,1)}, u32[]{:S(2)}, u32[]{:S(2)}) collective-permute-start(bf16[896,896]{1,0:T(8,128)(2,1)S(1)} %bitcast.21), channel_id=1, source_target_pairs={{16,64},{48,96},{64,16},{96,48},{17,65},{49,97},{65,17},{97,49},{1... | collective-permute-start | bytes 4816904 | tf_op jit(solution)/shard_map/ppermute | solution.py:466
  13.7 6.8 %all-to-all-start = ((bf16[16,2,8,4224]{3,2,1,0:T(8,128)(2,1)}), bf16[16,2,8,4224]{3,2,1,0:T(8,128)(2,1)}, u32[]{:S(2)}, u32[]{:S(2)}) async-start(bf16[16,2,8,4224]{3,2,1,0:T(8,128)(2,1)} %shard_map.65.after_ref), calls=%async_computation | async-start | bytes 4325376 | tf_op jit(solution)/shard_map/all_to_all | solution.py:462
  21.2 1.3 collective-permute-start.5
  22.5 6.0 %shard_map.66 = (f32[896,896]{1,0:T(8,128)}, bf16[896,896]{1,0:T(8,128)(2,1)}) custom-call(s32[7]{0:T(128)S(1)} %bitcast.29, f32[1]{0:T(128)S(6)} %copy.9.pair_ref, bf16[896,896]{1,0:T(8,128)(2,1)S(1)} %bitcast.23, bf16[896,896]{1,0:T(8,128)(2,1)S(1)} %bitcast.19, bf16[896,896]{1,0:T(8,128)(2,1)S(1)} %bitcast.20, f32[32,128]{1,0:T(8,128)S(1)} %bitcast.25, ...), custom_call_target="tpu_custom_call" | custom-call | flops 1438646272 | bytes 11239424 | tf_op jit(solution)/shard_map/pallas_call | solution.py:212
  28.4 3.8 %collective-permute-done.3.refs_3_ = bf16[896,896]{1,0:T(8,128)(2,1)} collective-permute-done((bf16[896,896]{1,0:T(8,128)(2,1)S(1)}, bf16[896,896]{1,0:T(8,128)(2,1)}, u32[]{:S(2)}, u32[]{:S(2)}) %collective-permute-start.3) | collective-permute-done | bytes 1605664 | tf_op jit(solution)/shard_map/ppermute | solution.py:466
  32.2 1.4 collective-permute-start.4
  33.7 3.1 %collective-permute-done.4.refs_1_ = bf16[896,896]{1,0:T(8,128)(2,1)S(1)} collective-permute-done((bf16[896,896]{1,0:T(8,128)(2,1)}, bf16[896,896]{1,0:T(8,128)(2,1)S(1)}, u32[]{:S(2)}, u32[]{:S(2)}) %collective-permute-start.4) | collective-permute-done | bytes 1605664 | tf_op jit(solution)/shard_map/ppermute | solution.py:474
  36.8 2.1 %shard_map.67 = (bf16[896,896]{1,0:T(8,128)(2,1)S(1)}, bf16[896,896]{1,0:T(8,128)(2,1)S(1)}) custom-call(s32[1]{0:T(128)} %bitcast.home_ref, bf16[896,896]{1,0:T(8,128)(2,1)S(1)} %bitcast.24, bf16[896,896]{1,0:T(8,128)(2,1)S(1)} %collective-permute-done.4.refs_1_, bf16[896,896]{1,0:T(8,128)(2,1)} %collective-permute-done.5.refs_2_, ...), custom_call_target="tpu_custom_call" | custom-call | bytes 3211264 | tf_op jit(solution)/shard_map/pallas_call | solution.py:265
  38.9 1.1 copy-done.2
  40.1 1.1 copy-done.5
  41.2 7.3 %all-to-all-done = bf16[16,2,8,4224]{3,2,1,0:T(8,128)(2,1)} async-done(((bf16[16,2,8,4224]{3,2,1,0:T(8,128)(2,1)}), bf16[16,2,8,4224]{3,2,1,0:T(8,128)(2,1)}, u32[]{:S(2)}, u32[]{:S(2)}) %all-to-all-start) | async-done | bytes 2162720 | tf_op jit(solution)/shard_map/all_to_all | solution.py:462
  48.5 7.2 %shard_map.68 = bf16[64,7,8,896]{3,2,1,0:T(8,128)(2,1)} custom-call(bf16[32,8,4224]{2,1,0:T(8,128)(2,1)} %bitcast.10.given_ref, bf16[896,896]{1,0:T(8,128)(2,1)} %copy-done.2, bf16[896,896]{1,0:T(8,128)(2,1)} %copy-done.5, bf16[896,896]{1,0:T(8,128)(2,1)} %get-tuple-element.27.refs_2_.added_ref), custom_call_target="tpu_custom_call" | custom-call | bytes 12845056 | tf_op jit(solution)/shard_map/pallas_call | solution.py:171
  55.8 81.5 %all_to_all.10 = bf16[64,7,8,896]{3,2,1,0:T(8,128)(2,1)} all-to-all(bf16[64,7,8,896]{3,2,1,0:T(8,128)(2,1)} %shard_map.68), channel_id=1, replica_groups=mesh['z'=4,'core'=2,'x'=4,'y'=4] {'z','x','y'}, dimensions={0} | all-to-all | bytes 12845056 | tf_op jit(solution)/shard_map/all_to_all | solution.py:479
  137.2 2.7 %collective-permute-start.6 = (bf16[896,896]{1,0:T(8,128)(2,1)S(1)}, bf16[896,896]{1,0:T(8,128)(2,1)S(1)}, u32[]{:S(2)}, u32[]{:S(2)}) collective-permute-start(bf16[896,896]{1,0:T(8,128)(2,1)S(1)} %copy-done.4), channel_id=1, source_target_pairs={{16,80},{48,112},{64,0},{96,32},{17,81},{49,113},{65,1},{97,33},{1... | collective-permute-start | bytes 4816904 | tf_op jit(solution)/shard_map/ppermute | solution.py:483
  140.0 17.6 %shard_map.69 = (f32[896,896]{1,0:T(8,128)S(1)}, bf16[896,896]{1,0:T(8,128)(2,1)S(1)}, bf16[4,896,896]{2,1,0:T(8,128)(2,1)S(1)}) custom-call(bf16[896,896]{1,0:T(8,128)(2,1)S(1)} %copy-done.6, bf16[4,16,7,8,896]{4,3,2,1,0:T(8,128)(2,1)} %bitcast.30, bf16[896,896]{1,0:T(8,128)(2,1)S(1)} %copy-done.4), custom_call_target="tpu_custom_call" | custom-call | flops 11509170176 | bytes 6422528 | tf_op jit(solution)/shard_map/pallas_call | solution.py:372
  157.6 1.5 collective-permute-start.7
  159.1 3.9 %shard_map.70.so_far_ref = f32[896,896]{1,0:T(8,128)S(1)} custom-call(bf16[896,896]{1,0:T(8,128)(2,1)S(1)} %copy-done.3, bf16[4,896,896]{2,1,0:T(8,128)(2,1)S(1)} %get-tuple-element.29.block_ref), custom_call_target="tpu_custom_call" | custom-call | flops 2877292544 | bytes 1605632 | tf_op jit(solution)/shard_map/pallas_call | solution.py:390
  163.0 0.5 collective-permute-done.7
  163.5 0.3 add_convert_fusion.after_ref
  163.8 7.1 %collective-permute-start.8 = (bf16[896,896]{1,0:T(8,128)(2,1)S(1)}, bf16[896,896]{1,0:T(8,128)(2,1)S(1)}, u32[]{:S(2)}, u32[]{:S(2)}) collective-permute-start(bf16[896,896]{1,0:T(8,128)(2,1)S(1)} %add_convert_fusion.after_ref), channel_id=1, source_target_pairs={{16,64},{48,96},{64,16},{96,48},{17,65},{49,97},{65,17},{97,49},{1... | collective-permute-start | bytes 4816904 | tf_op jit(solution)/shard_map/ppermute | solution.py:491
  171.0 11.3 %shard_map.71 = (f32[896,896]{1,0:T(8,128)S(1)}, bf16[512,896]{1,0:T(8,128)(2,1)S(1)}, bf16[384,896]{1,0:T(8,128)(2,1)S(1)}) custom-call(s32[1]{0:T(128)} %bitcast.home_ref, bf16[896,896]{1,0:T(8,128)(2,1)S(1)} %copy-done.3, bf16[4,896,896]{2,1,0:T(8,128)(2,1)S(1)} %get-tuple-element.29.block_ref, f32[896,896]{1,0:T(8,128)S(1)} %shard_map.70.so_far_ref, ...), custom_call_target="tpu_custom_call" | custom-call | flops 8631877632 | bytes 4816896 | tf_op jit(solution)/shard_map/pallas_call | solution.py:408
  182.3 1.3 collective-permute-start.9
  183.6 1.3 collective-permute-start.10
  185.0 1.7 collective-permute-done.10.refs_1_
  186.7 2.7 %collective-permute-done.8.returned_ref = bf16[896,896]{1,0:T(8,128)(2,1)S(1)} collective-permute-done((bf16[896,896]{1,0:T(8,128)(2,1)S(1)}, bf16[896,896]{1,0:T(8,128)(2,1)S(1)}, u32[]{:S(2)}, u32[]{:S(2)}) %collective-permute-start.8) | collective-permute-done | bytes 1605664 | tf_op jit(solution)/shard_map/ppermute | solution.py:491
  189.4 1.8 shard_map.72
  (29 shorter events, 0.2 us)
Async XLA Ops:
  0.0 6.3 %collective-permute-start = (s32[7]{0:T(128)}, s32[7]{0:T(128)S(1)}, u32[]{:S(2)}, u32[]{:S(2)}) collective-permute-start(s32[7]{0:T(128)} %bitcast.26), channel_id=1, source_target_pairs={{0,32},{16,48},{32,0},{48,16},{64,96},{80,112},{96,64},{112,80},{1... | collective-permute-start | bytes 92 | tf_op jit(solution)/shard_map/ppermute | solution.py:451
  2.5 3.9 %collective-permute-start.1 = (s32[7]{0:T(128)}, s32[7]{0:T(128)S(1)}, u32[]{:S(2)}, u32[]{:S(2)}) collective-permute-start(s32[7]{0:T(128)} %bitcast.27), channel_id=1, source_target_pairs={{0,16},{16,0},{1,17},{17,1},{2,18},{18,2},{3,19},{19,3},{4,20},{20... | collective-permute-start | bytes 92 | tf_op jit(solution)/shard_map/ppermute | solution.py:41
  3.4 3.1 %collective-permute-start.2 = (s32[7]{0:T(128)}, s32[7]{0:T(128)S(1)}, u32[]{:S(2)}, u32[]{:S(2)}) collective-permute-start(s32[7]{0:T(128)} %bitcast.28), channel_id=1, source_target_pairs={{0,48},{16,32},{32,16},{48,0},{64,112},{80,96},{96,80},{112,64},{1... | collective-permute-start | bytes 92 | tf_op jit(solution)/shard_map/ppermute | solution.py:452
  3.4 2.9 %copy-start.8 = (s32[1,7]{1,0:T(1,128)S(1)}, s32[1,7]{1,0:T(1,128)}, u32[]{:S(2)}) copy-start(s32[1,7]{1,0:T(1,128)} %param.9) | copy-start | bytes 88
  6.7 1.5 copy-start.1
  8.1 14.3 %copy-start = (bf16[1,896,896]{2,1,0:T(8,128)(2,1)S(1)}, bf16[1,896,896]{2,1,0:T(8,128)(2,1)}, u32[]{:S(2)}) copy-start(bf16[1,896,896]{2,1,0:T(8,128)(2,1)} %param.7) | copy-start | bytes 4816900
  8.1 14.4 %copy-start.7 = (f32[4096]{0:T(1024)S(1)}, f32[4096]{0:T(1024)}, u32[]{:S(2)}) copy-start(f32[4096]{0:T(1024)} %param.10) | copy-start | bytes 49156
  8.1 24.1 %collective-permute-start.3 = (bf16[896,896]{1,0:T(8,128)(2,1)S(1)}, bf16[896,896]{1,0:T(8,128)(2,1)}, u32[]{:S(2)}, u32[]{:S(2)}) collective-permute-start(bf16[896,896]{1,0:T(8,128)(2,1)S(1)} %bitcast.21), channel_id=1, source_target_pairs={{16,64},{48,96},{64,16},{96,48},{17,65},{49,97},{65,17},{97,49},{1... | collective-permute-start | bytes 4816904 | tf_op jit(solution)/shard_map/ppermute | solution.py:466
  13.7 34.8 %all-to-all-start = ((bf16[16,2,8,4224]{3,2,1,0:T(8,128)(2,1)}), bf16[16,2,8,4224]{3,2,1,0:T(8,128)(2,1)}, u32[]{:S(2)}, u32[]{:S(2)}) async-start(bf16[16,2,8,4224]{3,2,1,0:T(8,128)(2,1)} %shard_map.65.after_ref), calls=%async_computation | async-start | bytes 4325376 | tf_op jit(solution)/shard_map/all_to_all | solution.py:462
  21.2 12.5 %collective-permute-start.5 = (bf16[896,896]{1,0:T(8,128)(2,1)S(1)}, bf16[896,896]{1,0:T(8,128)(2,1)}, u32[]{:S(2)}, u32[]{:S(2)}) collective-permute-start(bf16[896,896]{1,0:T(8,128)(2,1)S(1)} %bitcast.22), channel_id=1, source_target_pairs={{0,16},{32,48},{80,64},{112,96},{1,17},{33,49},{81,65},{113,97},{2... | collective-permute-start | bytes 4816904 | tf_op jit(solution)/shard_map/ppermute | solution.py:467
  32.2 4.6 %collective-permute-start.4 = (bf16[896,896]{1,0:T(8,128)(2,1)}, bf16[896,896]{1,0:T(8,128)(2,1)S(1)}, u32[]{:S(2)}, u32[]{:S(2)}) collective-permute-start(bf16[896,896]{1,0:T(8,128)(2,1)} %collective-permute-done.3.refs_3_), channel_id=1, source_target_pairs={{16,0},{48,32},{64,80},{96,112},{17,1},{49,33},{65,81},{97,113},{1... | collective-permute-start | bytes 4816904 | tf_op jit(solution)/shard_map/ppermute | solution.py:474
  38.9 1.2 copy-start.2
  40.1 1.1 copy-start.5
  55.7 81.5 %copy-start.4 = (bf16[896,896]{1,0:T(8,128)(2,1)S(1)}, bf16[896,896]{1,0:T(8,128)(2,1)}, u32[]{:S(2)}) copy-start(bf16[896,896]{1,0:T(8,128)(2,1)} %get-tuple-element.27.refs_2_.added_ref) | copy-start | bytes 4816900
  55.7 84.2 %copy-start.6 = (bf16[896,896]{1,0:T(8,128)(2,1)S(1)}, bf16[896,896]{1,0:T(8,128)(2,1)}, u32[]{:S(2)}) copy-start(bf16[896,896]{1,0:T(8,128)(2,1)} %copy-done.5) | copy-start | bytes 4816900
  137.2 21.9 %copy-start.3 = (bf16[896,896]{1,0:T(8,128)(2,1)S(1)}, bf16[896,896]{1,0:T(8,128)(2,1)}, u32[]{:S(2)}) copy-start(bf16[896,896]{1,0:T(8,128)(2,1)} %copy-done.2) | copy-start | bytes 4816900
  137.2 21.9 %collective-permute-start.6 = (bf16[896,896]{1,0:T(8,128)(2,1)S(1)}, bf16[896,896]{1,0:T(8,128)(2,1)S(1)}, u32[]{:S(2)}, u32[]{:S(2)}) collective-permute-start(bf16[896,896]{1,0:T(8,128)(2,1)S(1)} %copy-done.4), channel_id=1, source_target_pairs={{16,80},{48,112},{64,0},{96,32},{17,81},{49,113},{65,1},{97,33},{1... | collective-permute-start | bytes 4816904 | tf_op jit(solution)/shard_map/ppermute | solution.py:483
  157.6 6.0 %collective-permute-start.7 = (bf16[896,896]{1,0:T(8,128)(2,1)S(1)}, bf16[896,896]{1,0:T(8,128)(2,1)S(1)}, u32[]{:S(2)}, u32[]{:S(2)}) collective-permute-start(bf16[896,896]{1,0:T(8,128)(2,1)S(1)} %get-tuple-element.34), channel_id=1, source_target_pairs={{0,16},{32,48},{80,64},{112,96},{1,17},{33,49},{81,65},{113,97},{2... | collective-permute-start | bytes 4816904 | tf_op jit(solution)/shard_map/ppermute | solution.py:486
  163.0 8.0 %copy-start.9 = (f32[896,896]{1,0:T(8,128)S(1)}, f32[896,896]{1,0:T(8,128)}, u32[]{:S(2)}) copy-start(f32[896,896]{1,0:T(8,128)} %get-tuple-element.32.added_ref) | copy-start | bytes 9633796
  163.8 25.6 %collective-permute-start.8 = (bf16[896,896]{1,0:T(8,128)(2,1)S(1)}, bf16[896,896]{1,0:T(8,128)(2,1)S(1)}, u32[]{:S(2)}, u32[]{:S(2)}) collective-permute-start(bf16[896,896]{1,0:T(8,128)(2,1)S(1)} %add_convert_fusion.after_ref), channel_id=1, source_target_pairs={{16,64},{48,96},{64,16},{96,48},{17,65},{49,97},{65,17},{97,49},{1... | collective-permute-start | bytes 4816904 | tf_op jit(solution)/shard_map/ppermute | solution.py:491
  182.3 4.4 %collective-permute-start.9 = (bf16[512,896]{1,0:T(8,128)(2,1)S(1)}, bf16[512,896]{1,0:T(8,128)(2,1)S(1)}, u32[]{:S(2)}, u32[]{:S(2)}) collective-permute-start(bf16[512,896]{1,0:T(8,128)(2,1)S(1)} %get-tuple-element.37), channel_id=1, source_target_pairs={{16,0},{48,32},{64,80},{96,112},{17,1},{49,33},{65,81},{97,113},{1... | collective-permute-start | bytes 2752520 | tf_op jit(solution)/shard_map/ppermute | solution.py:494
  183.6 3.1 %collective-permute-start.10 = (bf16[384,896]{1,0:T(8,128)(2,1)S(1)}, bf16[384,896]{1,0:T(8,128)(2,1)S(1)}, u32[]{:S(2)}, u32[]{:S(2)}) collective-permute-start(bf16[384,896]{1,0:T(8,128)(2,1)S(1)} %get-tuple-element.38), channel_id=1, source_target_pairs={{16,0},{48,32},{64,80},{96,112},{17,1},{49,33},{65,81},{97,113},{1... | collective-permute-start | bytes 2064392 | tf_op jit(solution)/shard_map/ppermute | solution.py:494
